TPU v7x, 512 devices: a whole 4x4x16 slice. The times are simulated.
512 devices in a mesh: row: 16 (over z_lo, x), col: 8 (over z_hi, core), vis: 4 (over y).
Axes of the slice: x: 4, y: 4, z: 16 (z_hi: 4, z_lo: 4; z = z_hi * 4 + z_lo), core: 2. Of those that a mesh axis runs over, the one named last changes fastest.
Arguments:
- tile_rows: bfloat16 [2048, 12800], P('vis', 'row'), may hold values from -6 to 6
- tile_slot: int32 [4], replicated, may hold values from 0 to 7, as said below
- proj_weight: bfloat16 [12800, 8192], P('row', ('col', 'vis')), may hold values from -0.0546875 to 0.0546875
- gate_weight: bfloat16 [8192, 14784], P('col', ('row', 'vis')), may hold values from -0.0625 to 0.0625
- up_weight: bfloat16 [8192, 14784], P('col', ('row', 'vis')), may hold values from -0.0625 to 0.0625
- cotangent: bfloat16 [1024, 14784], P('vis', 'row'), may hold values from -0.19921875 to 0.19921875
Outputs:
- proj_grad: bfloat16 [12800, 8192], P('row', ('col', 'vis'))
Inputs may be any that keep to these rules, and one draw needn't show every extreme that they name: `tile_slot`: the entries are distinct slots of the 8 slots; in every draw all 2 slots of some vision group are used.
All inputs are finite; a program needn't handle non-finite values.
Results may differ from a plain program's by a relative error of at most 0.01.
Values may be sent and summed in bfloat16 or wider, within the bound.
No kernel may reach another device: no remote copies, remote signals or barrier semaphores. Data moves between devices by JAX's collectives and lax.ppermute only.
A program may use at most 64 MiB of HBM per device.

v0:
```python
import jax
import jax.numpy as jnp
from jax import lax
from jax.sharding import PartitionSpec as P

TILE = 256


def gelu_exact(value):
    return 0.5 * value * (1.0 + lax.erf(value * 0.7071067811865476))


def gelu_slope(value):
    normal_cdf = 0.5 * (1.0 + lax.erf(value * 0.7071067811865476))
    return normal_cdf + value * jnp.exp(-0.5 * value * value) * 0.3989422804014327


def shards(tile_rows, tile_slot, proj_weight, gate_weight, up_weight, cotangent):
    vis_count = lax.axis_size("vis")
    arrived = lax.all_gather(tile_rows, "vis", axis=0, tiled=True)
    features = arrived.shape[1]
    per_group = tile_slot.shape[0] // vis_count
    own_slots = lax.dynamic_slice_in_dim(tile_slot, lax.axis_index("vis") * per_group, per_group, 0)
    tokens = arrived.reshape(-1, TILE, features)[own_slots].reshape(per_group * TILE, features)
    partial_value = jnp.dot(
        tokens,
        lax.all_gather(proj_weight, "vis", axis=1, tiled=True),
        preferred_element_type=jnp.float32,
    )
    preact = lax.psum(partial_value, "row")
    hidden = gelu_exact(preact).astype(jnp.bfloat16)
    gate_block, up_block = (
        lax.all_gather(gate_weight, "vis", axis=1, tiled=True),
        lax.all_gather(up_weight, "vis", axis=1, tiled=True),
    )
    gate_part = jnp.dot(hidden, gate_block, preferred_element_type=jnp.float32)
    up_part = jnp.dot(hidden, up_block, preferred_element_type=jnp.float32)
    gate_sum, up_sum = lax.psum((gate_part, up_part), "col")
    sigmoid_gate = jax.nn.sigmoid(gate_sum)
    d_gate = (cotangent * up_sum * sigmoid_gate * (1.0 + gate_sum * (1.0 - sigmoid_gate))).astype(
        jnp.bfloat16
    )
    d_up = (cotangent * gate_sum * sigmoid_gate).astype(jnp.bfloat16)
    contract = (((1,), (1,)), ((), ()))
    dact_part = lax.dot_general(d_gate, gate_block, contract, preferred_element_type=jnp.float32)
    dact_part = dact_part + lax.dot_general(
        d_up, up_block, contract, preferred_element_type=jnp.float32
    )
    dact = lax.psum(dact_part, "row")
    dpre = (dact * gelu_slope(preact)).astype(jnp.bfloat16)
    token_contract = (((0,), (0,)), ((), ()))
    grad_term = lax.dot_general(tokens, dpre, token_contract, preferred_element_type=jnp.float32)
    grad_block = lax.psum_scatter(grad_term, "vis", scatter_dimension=1, tiled=True)
    return grad_block.astype(jnp.bfloat16)


def solution(mesh):
    in_specs = (
        P("vis", "row"),
        P(),
        P("row", ("col", "vis")),
        P("col", ("row", "vis")),
        P("col", ("row", "vis")),
        P("vis", "row"),
    )
    out_specs = P("row", ("col", "vis"))
    return jax.shard_map(shards, mesh=mesh, in_specs=in_specs, out_specs=out_specs, check_vma=False)
```

profile of v0, /device:TPU:1, one launch (start us, length us, event | category | flops | bytes accessed | tf_op | source)
XLA Modules:
  0.0 728.3 jit_solution(52501847398977807)
XLA Ops:
  6.5 0.7 all-gather.7.cloned.1.call-update
  7.3 0.0 all-gather.9.cloned.1.call-start
  7.3 0.7 all-gather.9.cloned.1.call-update
  8.0 0.0 all-gather.13.cloned.1.call-start
  8.1 0.7 all-gather.13.cloned.1.call-update
  8.7 0.0 all-gather.11.cloned.1.call-start
  8.8 0.5 all-gather.11.cloned.1.call-update
  9.3 0.0 all-reduce.5.cloned.1.call-start
  9.4 0.6 dynamic_slice.3
  11.9 51.2 %all-gather.7.cloned.1.call-done = bf16[2048,800]{0,1:T(8,128)(2,1)} async-done(((bf16[512,800]{0,1:T(8,128)(2,1)}), bf16[2048,800]{0,1:T(8,128)(2,1)}) %all-gather.7.cloned.1.call-update) | async-done | bytes 3276816 | tf_op jit(solution)/shard_map/all_gather | solution.py:20
  63.1 3.1 copy.8
  66.2 0.8 constant_dynamic-slice_fusion
  67.0 36.0 %all-gather.9.cloned.1.call-done = bf16[800,1024]{1,0:T(8,128)(2,1)} async-done(((bf16[800,256]{1,0:T(8,128)(2,1)}), bf16[800,1024]{1,0:T(8,128)(2,1)}) %all-gather.9.cloned.1.call-update) | async-done | bytes 1638416 | tf_op jit(solution)/shard_map/all_gather | solution.py:27
  103.1 3.2 fusion.21
  106.3 0.0 all-reduce.9.cloned.1.call-start
  106.3 37.7 %all-gather.13.cloned.1.call-done = bf16[4,231,1024]{2,1,0:T(8,128)(2,1)} async-done(((bf16[1,231,1024]{2,1,0:T(8,128)(2,1)}), bf16[4,231,1024]{2,1,0:T(8,128)(2,1)}) %all-gather.13.cloned.1.call-update) | async-done | bytes 1892368 | tf_op jit(solution)/shard_map/all_gather | solution.py:33
  144.0 2.0 reshape.33
  146.1 36.9 %all-gather.11.cloned.1.call-done = bf16[4,231,1024]{2,1,0:T(8,128)(2,1)} async-done(((bf16[1,231,1024]{2,1,0:T(8,128)(2,1)}), bf16[4,231,1024]{2,1,0:T(8,128)(2,1)}) %all-gather.11.cloned.1.call-update) | async-done | bytes 1892368 | tf_op jit(solution)/shard_map/all_gather | solution.py:34
  183.0 3.3 reshape.31
  186.3 162.6 %all-reduce.5.cloned.1.call-done = f32[256,1024]{1,0:T(8,128)} async-done(((f32[256,1024]{1,0:T(8,128)}), f32[256,1024]{1,0:T(8,128)}) %all-reduce.5.cloned.1.call-update) | async-done | bytes 1048592 | tf_op jit(solution)/shard_map/psum | solution.py:30
  348.9 1.4 multiply_convert_fusion
  350.3 1.6 fusion.31
  352.0 1.7 fusion.30
  353.6 0.0 all-reduce.7.cloned.1.call-start
  353.7 140.1 %all-reduce.9.cloned.1.call-done = (f32[256,924]{0,1:T(8,128)}, f32[256,924]{0,1:T(8,128)}) async-done(((f32[256,924]{0,1:T(8,128)}, f32[256,924]{0,1:T(8,128)}), (f32[256,924]{0,1:T(8,128)}, f32[256,924]{0,1:T(8,128)})) %all-reduce.9.cloned.1.call-update) | async-done | bytes 1892368 | tf_op jit(solution)/shard_map/psum | solution.py:38
  493.8 2.5 fusion.18
  496.3 1.8 convolution_add_fusion
  498.1 0.0 reduce-scatter.2.cloned.1.call-start
  498.2 161.7 %all-reduce.7.cloned.1.call-done = f32[256,1024]{1,0:T(8,128)} async-done(((f32[256,1024]{1,0:T(8,128)}), f32[256,1024]{1,0:T(8,128)}) %all-reduce.7.cloned.1.call-update) | async-done | bytes 1048592 | tf_op jit(solution)/shard_map/psum | solution.py:49
  659.9 3.7 fusion.11
  663.7 55.9 %reduce-scatter.2.cloned.1.call-done = f32[800,256]{1,0:T(8,128)} async-done(((f32[800,1024]{1,0:T(8,128)}), f32[800,256]{1,0:T(8,128)}) %reduce-scatter.2.cloned.1.call-update) | async-done | bytes 819216 | tf_op jit(solution)/shard_map/reduce_scatter | solution.py:53
  719.5 1.9 convert_element_type.24
  (17 shorter events, 0.1 us)
Async XLA Ops:
  6.5 2.8 copy-start.5
  6.5 56.6 %all-gather.7.cloned.1.call-start = ((), (), s32[]{:S(2)}) async-start(), calls=%async_computation.1 | async-start | bytes 4096000 | tf_op jit(solution)/shard_map/all_gather | solution.py:20
  7.3 95.8 %all-gather.9.cloned.1.call-start = ((), (), s32[]{:S(2)}) async-start(), calls=%async_computation.2 | async-start | bytes 2048000 | tf_op jit(solution)/shard_map/all_gather | solution.py:27
  8.0 136.0 %all-gather.13.cloned.1.call-start = ((), (), s32[]{:S(2)}) async-start(), calls=%async_computation.7 | async-start | bytes 2375680 | tf_op jit(solution)/shard_map/all_gather | solution.py:33
  8.7 174.2 %all-gather.11.cloned.1.call-start = ((), (), s32[]{:S(2)}) async-start(), calls=%async_computation.6 | async-start | bytes 2375680 | tf_op jit(solution)/shard_map/all_gather | solution.py:34
  9.3 339.6 %all-reduce.5.cloned.1.call-start = ((), (), s32[]{:S(2)}) async-start(), calls=%async_computation.3 | async-start | bytes 2097152 | tf_op jit(solution)/shard_map/psum | solution.py:30
  106.3 387.5 %all-reduce.9.cloned.1.call-start = ((), (), s32[]{:S(2)}) async-start(), calls=%async_computation.8 | async-start | bytes 3801088 | tf_op jit(solution)/shard_map/psum | solution.py:38
  350.3 1.6 copy-start
  352.0 141.8 %copy-start.4 = (bf16[256,924]{0,1:T(8,128)(2,1)S(1)}, bf16[256,924]{0,1:T(8,128)(2,1)}, u32[]{:S(2)}) copy-start(bf16[256,924]{0,1:T(8,128)(2,1)} %param.11) | copy-start | bytes 1419268
  353.6 306.3 %all-reduce.7.cloned.1.call-start = ((), (), s32[]{:S(2)}) async-start(), calls=%async_computation.4 | async-start | bytes 2097152 | tf_op jit(solution)/shard_map/psum | solution.py:49
  493.8 2.5 copy-start.1
  493.8 2.5 copy-start.3
  496.3 163.6 %copy-start.2 = (f32[256,1024]{1,0:T(8,128)S(1)}, f32[256,1024]{1,0:T(8,128)}, u32[]{:S(2)}) copy-start(f32[256,1024]{1,0:T(8,128)} %all-reduce.5.cloned.1.call-done) | copy-start | bytes 3145732
  498.1 221.4 %reduce-scatter.2.cloned.1.call-start = ((), (), s32[]{:S(2)}) async-start(), calls=%async_computation.5 | async-start | bytes 4096000 | tf_op jit(solution)/shard_map/reduce_scatter | solution.py:53
Sparse Core Ops, SparseCore 0:
  9.5 53.5 all-gather.6
  65.2 37.8 all-gather.8
  105.2 38.8 all-gather.12
  146.0 36.9 all-gather.10
  185.7 163.0 all-reduce.4
  353.8 139.9 all-reduce.8
  498.3 161.6 all-reduce.6
  663.8 55.6 reduce-scatter.1
where the time goes:
time: 729 us; the launch traced here: 728 us
  waiting for transfers between devices  685 us (94%)
  between operations  15.5 us (2%)
  matrix products  14.5 us (2%)
  local copies, waits for them, and re-layouts  9.85 us (1%)
    psum x1, waiting for transfers between devices, shards(): preact = lax.psum(partial_value, 'row')  163 us
    psum x1, waiting for transfers between devices, shards(): dact = lax.psum(dact_part, 'row')  162 us
    psum x1, waiting for transfers between devices, shards(): gate_sum, up_sum = lax.psum((gate_part, up_part), 'col')  140 us
    reduce_scatter x1, waiting for transfers between devices, shards(): lax.psum_scatter(grad_term, 'vis', scatter_dimension=1, tiled=True)  55.9 us
    all_gather x1, waiting for transfers between devices, shards(): arrived = lax.all_gather(tile_rows, 'vis', axis=0, tiled=True)  51.2 us
    all_gather x1, waiting for transfers between devices, shards(): lax.all_gather(gate_weight, 'vis', axis=1, tiled=True)  37.7 us
    all_gather x1, waiting for transfers between devices, shards(): lax.all_gather(up_weight, 'vis', axis=1, tiled=True)  36.9 us
    all_gather x1, waiting for transfers between devices, shards(): lax.all_gather(proj_weight, 'vis', axis=1, tiled=True)  36 us
  transfers between devices with their start and end apart: 8, of which 8 were waited for; matrix products, arithmetic and copies ran while one was open for 2% of the time, Pallas kernels for 0%

commit v1 on v0

v1 whole, which is shorter than its diff:
```python
import jax
import jax.numpy as jnp
from jax import lax
from jax.sharding import PartitionSpec as P

TILE = 256
F32 = jnp.float32
BF16 = jnp.bfloat16


def gelu_exact(value):
    return 0.5 * value * (1.0 + lax.erf(value * 0.7071067811865476))


def gelu_slope(value):
    normal_cdf = 0.5 * (1.0 + lax.erf(value * 0.7071067811865476))
    return normal_cdf + value * jnp.exp(-0.5 * value * value) * 0.3989422804014327


def dot(a, b, contract):
    return lax.dot_general(a, b, (contract, ((), ())), preferred_element_type=F32)


def shards(tile_rows, tile_slot, proj_weight, gate_weight, up_weight, cotangent):
    n_vis, n_row, n_col = lax.axis_size("vis"), lax.axis_size("row"), lax.axis_size("col")
    n_quarter = n_col // 2
    vis, col = lax.axis_index("vis"), lax.axis_index("col")
    core, quarter = col % 2, col // 2
    features = tile_rows.shape[1]
    half = features // 2
    core_pairs = [(2 * i + k, 2 * i + 1 - k) for i in range(n_quarter) for k in range(2)]
    quarter_groups = [[2 * i + k for i in range(n_quarter)] for k in range(2)]
    n_tiles = tile_slot.shape[0]
    slots = tile_rows.shape[0] // TILE

    gate_t, up_t = gate_weight.T, up_weight.T
    gate_block = lax.all_gather(gate_t, "vis", axis=0)
    up_block = lax.all_gather(up_t, "vis", axis=0)

    rows_t = tile_rows.T
    own_half = lax.dynamic_slice_in_dim(rows_t, core * half, half, 0)
    arrived = lax.all_to_all(jnp.broadcast_to(own_half[None], (n_vis,) + own_half.shape), "vis", 0, 0)
    picked = []
    for t in range(n_tiles):
        slot = tile_slot[t]
        picked.append(
            lax.dynamic_slice(arrived, (slot // slots, 0, (slot % slots) * TILE), (1, half, TILE))[0]
        )
    mine = jnp.concatenate(picked, axis=1)
    other = lax.ppermute(mine, "col", core_pairs)
    first = jnp.where(core == 0, mine, other)
    second = jnp.where(core == 0, other, mine)
    tokens_t = jnp.concatenate([first, second], axis=0)

    partial = dot(tokens_t, proj_weight, ((0,), (0,))).astype(BF16)
    n_tok, width = partial.shape
    share = n_tok // (n_vis * n_row)
    partial = lax.all_to_all(partial.reshape(n_vis * n_row, share, width), ("vis", "row"), 0, 0)
    preact = jnp.sum(partial.reshape(n_vis, n_row, share, width).astype(F32), axis=1)
    preact = jnp.transpose(preact, (1, 0, 2)).reshape(share, n_vis * width)
    hidden = gelu_exact(preact).astype(BF16)
    slope = gelu_slope(preact)
    hidden = lax.all_to_all(jnp.broadcast_to(hidden[None], (n_row,) + hidden.shape), "row", 0, 0)
    hidden = hidden.reshape(TILE, n_vis * width)

    parts = []
    for block in (gate_block, up_block):
        parts.append(jnp.stack([dot(block[k], hidden, ((1,), (1,))) for k in range(n_vis)]))
    both = jnp.stack(parts, axis=1)
    lane = TILE // 2
    keep = lax.dynamic_slice_in_dim(both, core * lane, lane, 3)
    give = lax.dynamic_slice_in_dim(both, (1 - core) * lane, lane, 3).astype(BF16)
    got = lax.ppermute(give, "col", core_pairs)
    pair_sum = (keep + got.astype(F32)).astype(BF16)
    pieces = lax.all_to_all(pair_sum, "col", 0, 0, axis_index_groups=quarter_groups)
    gate_sum, up_sum = jnp.sum(pieces.astype(F32), axis=0)

    unit = gate_t.shape[0]
    cot = lax.dynamic_slice(cotangent.T, (quarter * unit, core * lane), (unit, lane)).astype(F32)
    sig = jax.nn.sigmoid(gate_sum)
    d_gate = (cot * up_sum * sig * (1.0 + gate_sum * (1.0 - sig))).astype(BF16)
    d_up = (cot * gate_sum * sig).astype(BF16)
    d_both = jnp.stack([d_gate, d_up])
    d_all = lax.all_to_all(
        jnp.broadcast_to(d_both[None], (n_quarter,) + d_both.shape), "col", 0, 0,
        axis_index_groups=quarter_groups,
    )
    d_other = lax.ppermute(d_all, "col", core_pairs)
    d_first = jnp.where(core == 0, d_all, d_other)
    d_second = jnp.where(core == 0, d_other, d_all)
    d_all = jnp.concatenate([d_first, d_second], axis=3)

    dact = 0.0
    for k in range(n_vis):
        dact = dact + dot(d_all[k, 0], gate_block[k], ((0,), (0,)))
        dact = dact + dot(d_all[k, 1], up_block[k], ((0,), (0,)))
    dact = dact.astype(BF16).reshape(n_row, share, n_vis * width)
    dact = lax.all_to_all(dact, "row", 0, 0)
    dact = jnp.sum(dact.astype(F32), axis=0)
    dpre = (dact * slope).astype(BF16)
    dpre = jnp.transpose(dpre.reshape(share, n_vis, width), (1, 0, 2))
    dpre = jnp.broadcast_to(dpre[:, None], (n_vis, n_row, share, width))
    dpre = lax.all_to_all(dpre.reshape(n_vis * n_row, share, width), ("vis", "row"), 0, 0)
    dpre = dpre.reshape(n_tok, width)
    return dot(tokens_t, dpre, ((1,), (0,))).astype(BF16)


def solution(mesh):
    in_specs = (
        P("vis", "row"),
        P(),
        P("row", ("col", "vis")),
        P("col", ("row", "vis")),
        P("col", ("row", "vis")),
        P("vis", "row"),
    )
    out_specs = P("row", ("col", "vis"))
    return jax.shard_map(shards, mesh=mesh, in_specs=in_specs, out_specs=out_specs, check_vma=False)
```

time: 729 us -> 262 us (0.36)
  waiting for transfers between devices: 685 us -> 92.3 us
  blocking collectives: 0 us -> 72.5 us
  starting transfers between devices: 0.28 us -> 51 us
  between operations: 15.5 us -> 24 us
    psum x3 -> x0, waiting for transfers between devices: 464 us -> none  [the longest x1 163 us: shards(): preact = lax.psum(partial_value, 'row')]
    all_gather x4 -> x2, waiting for transfers between devices: 162 us -> 33.3 us  [the longest x1 27.7 us: shards(): gate_block = lax.all_gather(gate_t, 'vis', axis=0)]
    all_to_all x0 -> x3, blocking collectives: none -> 72.5 us  [the longest x1 26.8 us: shards(): dact = lax.all_to_all(dact, 'row', 0, 0)]
    reduce_scatter x1 -> x0, waiting for transfers between devices: 55.9 us -> none  [shards(): lax.psum_scatter(grad_term, 'vis', scatter_dimension=1, tiled=True)]
    all_to_all x0 -> x4, waiting for transfers between devices: none -> 53.3 us  [the longest x1 24.4 us: shards(): lax.all_to_all(pair_sum, 'col', 0, 0, axis_index_groups=quarter_groups)]
    all_to_all x0 -> x4, starting transfers between devices: none -> 30.3 us  [the longest x1 11.9 us: shards(): lax.all_to_all(pair_sum, 'col', 0, 0, axis_index_groups=quarter_groups)]
    ppermute x0 -> x3, starting transfers between devices: none -> 20.7 us  [the longest x1 9.56 us: shards(): d_other = lax.ppermute(d_all, 'col', core_pairs)]
  transfers between devices with their start and end apart: 8 -> 9, of which waited for: 8 -> 9; matrix products, arithmetic and copies ran while one was open for 2% -> 3% of each run, Pallas kernels for 0% -> 0%
where the time goes in v1:
time: 262 us; the launch traced here: 261 us
  waiting for transfers between devices  92.3 us (35%)
  blocking collectives  72.5 us (28%)
  starting transfers between devices  51 us (19%)
  between operations  24 us (9%)
  matrix products  12.5 us (5%)
  local copies, waits for them, and re-layouts  5.88 us (2%)
  other arithmetic  3.31 us (1%)
    all_gather x1, waiting for transfers between devices, shards(): gate_block = lax.all_gather(gate_t, 'vis', axis=0)  27.7 us
    all_to_all x1, blocking collectives, shards(): dact = lax.all_to_all(dact, 'row', 0, 0)  26.8 us
    all_to_all x1, waiting for transfers between devices, shards(): lax.all_to_all(pair_sum, 'col', 0, 0, axis_index_groups=quarter_groups)  24.4 us
    all_to_all x1, blocking collectives, shards(): lax.all_to_all(dpre.reshape(n_vis * n_row, share, width), ('vis', 'row'),...  23.7 us
    all_to_all x1, blocking collectives, shards(): lax.all_to_all(jnp.broadcast_to(d_both[None], (n_quarter,) + d_both.shape...  22 us
    all_to_all x1, waiting for transfers between devices, shards(): lax.all_to_all(partial.reshape(n_vis * n_row, share, width), ('vis', 'row...  16.6 us
    dot_general x18, matrix products, dot(): lax.dot_general(a, b, (contract, ((), ())), preferred_element_type=F32)  12.5 us
    all_to_all x1, starting transfers between devices, shards(): lax.all_to_all(pair_sum, 'col', 0, 0, axis_index_groups=quarter_groups)  11.9 us
  transfers between devices with their start and end apart: 9, of which 9 were waited for; matrix products, arithmetic and copies ran while one was open for 3% of the time, Pallas kernels for 0%

profile of v1, /device:TPU:1, one launch (start us, length us, event | category | flops | bytes accessed | tf_op | source)
XLA Modules:
  0.0 261.4 jit_solution(10877798163720177810)
XLA Ops:
  6.5 1.1 copy-done
  7.7 1.3 broadcast_in_dim.8
  9.0 5.1 %all-to-all-start = ((bf16[4,400,512]{2,1,0:T(8,128)(2,1)}), bf16[4,400,512]{2,1,0:T(8,128)(2,1)S(1)}, u32[]{:S(2)}, u32[]{:S(2)}) async-start(bf16[4,400,512]{2,1,0:T(8,128)(2,1)} %broadcast_in_dim.8), calls=%async_computation | async-start | bytes 3276800 | tf_op jit(solution)/shard_map/all_to_all | solution.py:42
  25.0 4.9 %all-to-all-done = bf16[4,400,512]{2,1,0:T(8,128)(2,1)S(1)} async-done(((bf16[4,400,512]{2,1,0:T(8,128)(2,1)}), bf16[4,400,512]{2,1,0:T(8,128)(2,1)S(1)}, u32[]{:S(2)}, u32[]{:S(2)}) %all-to-all-start) | async-done | bytes 1638432 | tf_op jit(solution)/shard_map/all_to_all | solution.py:42
  30.1 8.5 %collective-permute-start = (bf16[400,1024]{1,0:T(8,128)(2,1)S(1)}, bf16[400,1024]{1,0:T(8,128)(2,1)S(1)}, u32[]{:S(2)}, u32[]{:S(2)}) collective-permute-start(bf16[400,1024]{1,0:T(8,128)(2,1)S(1)} %pad_maximum_fusion.3), channel_id=1, source_target_pairs={{0,4},{4,0},{8,12},{12,8},{16,20},{20,16},{24,28},{28,24},{1,5},{5... | collective-permute-start | bytes 2457608 | tf_op jit(solution)/shard_map/ppermute | solution.py:50
  38.7 1.9 collective-permute-done
  41.0 1.6 convolution_convert_fusion
  42.6 9.7 %all-to-all-start.1 = ((bf16[64,16,256]{2,1,0:T(8,128)(2,1)}), bf16[64,16,256]{2,1,0:T(8,128)(2,1)S(1)}, u32[]{:S(2)}, u32[]{:S(2)}) async-start(bf16[64,16,256]{2,1,0:T(8,128)(2,1)} %bitcast.10), calls=%async_computation.1 | async-start | bytes 1048576 | tf_op jit(solution)/shard_map/all_to_all | solution.py:58
  52.3 0.7 all-gather.7.cloned.1.call-update
  53.0 16.6 %all-to-all-done.1 = bf16[64,16,256]{2,1,0:T(8,128)(2,1)S(1)} async-done(((bf16[64,16,256]{2,1,0:T(8,128)(2,1)}), bf16[64,16,256]{2,1,0:T(8,128)(2,1)S(1)}, u32[]{:S(2)}, u32[]{:S(2)}) %all-to-all-start.1) | async-done | bytes 524320 | tf_op jit(solution)/shard_map/all_to_all | solution.py:58
  69.7 0.8 broadcast_in_dim.9
  70.6 3.6 %all-to-all-start.2 = ((bf16[16,16,1024]{2,1,0:T(8,128)(2,1)}), bf16[16,16,1024]{2,1,0:T(8,128)(2,1)S(1)}, u32[]{:S(2)}, u32[]{:S(2)}) async-start(bf16[16,16,1024]{2,1,0:T(8,128)(2,1)} %broadcast_in_dim.9), calls=%async_computation.2 | async-start | bytes 1048576 | tf_op jit(solution)/shard_map/all_to_all | solution.py:63
  74.2 5.6 %all-gather.9.cloned.1.call-done = bf16[4,231,1024]{2,1,0:T(8,128)(2,1)} async-done(((bf16[1,231,1024]{2,1,0:T(8,128)(2,1)}), bf16[4,231,1024]{2,1,0:T(8,128)(2,1)}) %all-gather.9.cloned.1.call-update) | async-done | bytes 1892368 | tf_op jit(solution)/shard_map/all_gather | solution.py:38
  79.8 7.4 %all-to-all-done.2 = bf16[16,16,1024]{2,1,0:T(8,128)(2,1)S(1)} async-done(((bf16[16,16,1024]{2,1,0:T(8,128)(2,1)}), bf16[16,16,1024]{2,1,0:T(8,128)(2,1)S(1)}, u32[]{:S(2)}, u32[]{:S(2)}) %all-to-all-start.2) | async-done | bytes 524320 | tf_op jit(solution)/shard_map/all_to_all | solution.py:63
  87.2 1.4 convolution_bitcast_fusion
  88.6 1.4 convolution_bitcast_fusion.1
  90.7 27.7 %all-gather.7.cloned.1.call-done = bf16[4,231,1024]{2,1,0:T(8,128)(2,1)} async-done(((bf16[1,231,1024]{2,1,0:T(8,128)(2,1)}), bf16[4,231,1024]{2,1,0:T(8,128)(2,1)}) %all-gather.7.cloned.1.call-update) | async-done | bytes 1892368 | tf_op jit(solution)/shard_map/all_gather | solution.py:37
  118.4 1.5 convolution_bitcast_fusion.4
  119.9 1.4 convolution_bitcast_fusion.5
  122.1 0.8 fusion.2
  123.0 2.6 collective-permute-start.1
  125.5 1.6 collective-permute-done.1
  127.3 1.1 copy.20
  128.4 11.9 %all-to-all-start.3 = ((bf16[4,2,231,128]{3,1,2,0:T(2,128)(2,1)}), bf16[4,2,231,128]{3,1,2,0:T(2,128)(2,1)S(1)}, u32[]{:S(2)}, u32[]{:S(2)}) async-start(bf16[4,2,231,128]{3,1,2,0:T(2,128)(2,1)} %copy.20), calls=%async_computation.3 | async-start | bytes 946176 | tf_op jit(solution)/shard_map/all_to_all | solution.py:75
  140.3 24.4 %all-to-all-done.3 = bf16[4,2,231,128]{3,1,2,0:T(2,128)(2,1)S(1)} async-done(((bf16[4,2,231,128]{3,1,2,0:T(2,128)(2,1)}), bf16[4,2,231,128]{3,1,2,0:T(2,128)(2,1)S(1)}, u32[]{:S(2)}, u32[]{:S(2)}) %all-to-all-start.3) | async-done | bytes 473120 | tf_op jit(solution)/shard_map/all_to_all | solution.py:75
  165.4 1.0 fusion.52
  166.7 22.0 %all_to_all.35 = bf16[4,2,231,128]{3,1,2,0:T(2,128)(2,1)S(1)} all-to-all(bf16[4,2,231,128]{3,1,2,0:T(2,128)(2,1)S(1)} %broadcast_in_dim.10), channel_id=1, replica_groups={{0,8,16,24},{4,12,20,28},{1,9,17,25},{5,13,21,29},{2,10,18,26},{6,14,22..., dimensions={0} | all-to-all | bytes 946176 | tf_op jit(solution)/shard_map/all_to_all | solution.py:84
  188.8 9.6 %collective-permute-start.2 = (bf16[4,2,231,128]{3,2,1,0:T(8,128)(2,1)S(1)}, bf16[4,2,231,128]{3,2,1,0:T(8,128)(2,1)S(1)}, u32[]{:S(2)}, u32[]{:S(2)}) collective-permute-start(bf16[4,2,231,128]{3,2,1,0:T(8,128)(2,1)S(1)} %copy.24), channel_id=1, source_target_pairs={{0,4},{4,0},{8,12},{12,8},{16,20},{20,16},{24,28},{28,24},{1,5},{5... | collective-permute-start | bytes 1419272 | tf_op jit(solution)/shard_map/ppermute | solution.py:88
  198.4 1.4 collective-permute-done.2
  202.6 26.8 %all_to_all.36 = bf16[16,16,1024]{2,1,0:T(8,128)(2,1)S(1)} all-to-all(bf16[16,16,1024]{2,1,0:T(8,128)(2,1)S(1)} %bitcast.218), channel_id=1, replica_groups=mesh['row'=16,'col'=8,'vis'=4] {'row'}, dimensions={0} | all-to-all | bytes 1048576 | tf_op jit(solution)/shard_map/all_to_all | solution.py:98
  229.6 23.7 %all_to_all.37 = bf16[64,16,256]{2,1,0:T(8,128)(2,1)S(1)} all-to-all(bf16[64,16,256]{2,1,0:T(8,128)(2,1)S(1)} %bitcast.217), channel_id=1, replica_groups=mesh['row'=16,'col'=8,'vis'=4] {'vis','row'}, dimensions={0} | all-to-all | bytes 1048576 | tf_op jit(solution)/shard_map/all_to_all | solution.py:103
  253.2 1.3 convolution_convert_fusion.1
  (57 shorter events, 7.0 us)
Async XLA Ops:
  6.5 1.1 copy-start
  9.0 5.2 %copy-start.9 = (s32[4]{0:T(128)S(1)}, s32[4]{0:T(128)}, u32[]{:S(2)}) copy-start(s32[4]{0:T(128)} %param.7) | copy-start | bytes 52
  9.0 20.9 %all-to-all-start = ((bf16[4,400,512]{2,1,0:T(8,128)(2,1)}), bf16[4,400,512]{2,1,0:T(8,128)(2,1)S(1)}, u32[]{:S(2)}, u32[]{:S(2)}) async-start(bf16[4,400,512]{2,1,0:T(8,128)(2,1)} %broadcast_in_dim.8), calls=%async_computation | async-start | bytes 3276800 | tf_op jit(solution)/shard_map/all_to_all | solution.py:42
  14.2 65.6 %all-gather.9.cloned.1.call-start = ((), (), s32[]{:S(2)}) async-start(), calls=%async_computation.8 | async-start | bytes 2375680 | tf_op jit(solution)/shard_map/all_gather | solution.py:38
  30.1 10.5 %collective-permute-start = (bf16[400,1024]{1,0:T(8,128)(2,1)S(1)}, bf16[400,1024]{1,0:T(8,128)(2,1)S(1)}, u32[]{:S(2)}, u32[]{:S(2)}) collective-permute-start(bf16[400,1024]{1,0:T(8,128)(2,1)S(1)} %pad_maximum_fusion.3), channel_id=1, source_target_pairs={{0,4},{4,0},{8,12},{12,8},{16,20},{20,16},{24,28},{28,24},{1,5},{5... | collective-permute-start | bytes 2457608 | tf_op jit(solution)/shard_map/ppermute | solution.py:50
  38.7 2.3 copy-start.10
  41.0 1.6 copy-start.5
  41.0 1.6 copy-start.7
  42.6 27.1 %all-to-all-start.1 = ((bf16[64,16,256]{2,1,0:T(8,128)(2,1)}), bf16[64,16,256]{2,1,0:T(8,128)(2,1)S(1)}, u32[]{:S(2)}, u32[]{:S(2)}) async-start(bf16[64,16,256]{2,1,0:T(8,128)(2,1)} %bitcast.10), calls=%async_computation.1 | async-start | bytes 1048576 | tf_op jit(solution)/shard_map/all_to_all | solution.py:58
  52.3 66.2 %all-gather.7.cloned.1.call-start = ((), (), s32[]{:S(2)}) async-start(), calls=%async_computation.7 | async-start | bytes 2375680 | tf_op jit(solution)/shard_map/all_gather | solution.py:37
  70.6 16.6 %all-to-all-start.2 = ((bf16[16,16,1024]{2,1,0:T(8,128)(2,1)}), bf16[16,16,1024]{2,1,0:T(8,128)(2,1)S(1)}, u32[]{:S(2)}, u32[]{:S(2)}) async-start(bf16[16,16,1024]{2,1,0:T(8,128)(2,1)} %broadcast_in_dim.9), calls=%async_computation.2 | async-start | bytes 1048576 | tf_op jit(solution)/shard_map/all_to_all | solution.py:63
  79.8 10.2 %copy-start.3 = (bf16[4,231,1024]{2,1,0:T(8,128)(2,1)S(1)}, bf16[4,231,1024]{2,1,0:T(8,128)(2,1)}, u32[]{:S(2)}) copy-start(bf16[4,231,1024]{2,1,0:T(8,128)(2,1)} %all-gather.9.cloned.1.call-done) | copy-start | bytes 5677060
  118.4 2.9 %copy-start.1 = (bf16[4,231,1024]{2,1,0:T(8,128)(2,1)S(1)}, bf16[4,231,1024]{2,1,0:T(8,128)(2,1)}, u32[]{:S(2)}) copy-start(bf16[4,231,1024]{2,1,0:T(8,128)(2,1)} %all-gather.7.cloned.1.call-done) | copy-start | bytes 5677060
  123.0 4.2 %collective-permute-start.1 = (bf16[4,2,231,128]{3,2,0,1:T(8,128)(2,1)}, bf16[4,2,231,128]{3,2,0,1:T(8,128)(2,1)S(1)}, u32[]{:S(2)}, u32[]{:S(2)}) collective-permute-start(bf16[4,2,231,128]{3,2,0,1:T(8,128)(2,1)} %fusion.2), channel_id=1, source_target_pairs={{0,4},{4,0},{8,12},{12,8},{16,20},{20,16},{24,28},{28,24},{1,5},{5... | collective-permute-start | bytes 1419272 | tf_op jit(solution)/shard_map/ppermute | solution.py:73
  128.4 36.3 %all-to-all-start.3 = ((bf16[4,2,231,128]{3,1,2,0:T(2,128)(2,1)}), bf16[4,2,231,128]{3,1,2,0:T(2,128)(2,1)S(1)}, u32[]{:S(2)}, u32[]{:S(2)}) async-start(bf16[4,2,231,128]{3,1,2,0:T(2,128)(2,1)} %copy.20), calls=%async_computation.3 | async-start | bytes 946176 | tf_op jit(solution)/shard_map/all_to_all | solution.py:75
  166.7 33.2 %copy-start.4 = (bf16[4,231,1024]{2,1,0:T(8,128)(2,1)S(1)}, bf16[4,231,1024]{2,1,0:T(8,128)(2,1)}, u32[]{:S(2)}) copy-start(bf16[4,231,1024]{2,1,0:T(8,128)(2,1)} %all-gather.9.cloned.1.call-done) | copy-start | bytes 5677060
  188.8 11.4 %copy-start.2 = (bf16[4,231,1024]{2,1,0:T(8,128)(2,1)S(1)}, bf16[4,231,1024]{2,1,0:T(8,128)(2,1)}, u32[]{:S(2)}) copy-start(bf16[4,231,1024]{2,1,0:T(8,128)(2,1)} %all-gather.7.cloned.1.call-done) | copy-start | bytes 5677060
  188.8 11.0 %collective-permute-start.2 = (bf16[4,2,231,128]{3,2,1,0:T(8,128)(2,1)S(1)}, bf16[4,2,231,128]{3,2,1,0:T(8,128)(2,1)S(1)}, u32[]{:S(2)}, u32[]{:S(2)}) collective-permute-start(bf16[4,2,231,128]{3,2,1,0:T(8,128)(2,1)S(1)} %copy.24), channel_id=1, source_target_pairs={{0,4},{4,0},{8,12},{12,8},{16,20},{20,16},{24,28},{28,24},{1,5},{5... | collective-permute-start | bytes 1419272 | tf_op jit(solution)/shard_map/ppermute | solution.py:88
  202.6 50.6 %copy-start.6 = (bf16[400,1024]{1,0:T(8,128)(2,1)S(1)}, bf16[400,1024]{1,0:T(8,128)(2,1)}, u32[]{:S(2)}) copy-start(bf16[400,1024]{1,0:T(8,128)(2,1)} %copy-done.5) | copy-start | bytes 2457604
  202.6 50.6 %copy-start.8 = (bf16[400,1024]{1,0:T(8,128)(2,1)S(1)}, bf16[400,1024]{1,0:T(8,128)(2,1)}, u32[]{:S(2)}) copy-start(bf16[400,1024]{1,0:T(8,128)(2,1)} %copy-done.7) | copy-start | bytes 2457604
Sparse Core Ops, SparseCore 0:
  38.8 40.9 all-gather.8
  81.9 36.5 all-gather.6

commit v2 on v1

v2 whole, which is shorter than its diff:
```python
import jax
import jax.numpy as jnp
from jax import lax
from jax.experimental import pallas as pl
from jax.experimental.pallas import tpu as pltpu
from jax.sharding import PartitionSpec as P

TILE = 256
F32 = jnp.float32
BF16 = jnp.bfloat16


def gelu_exact(value):
    return 0.5 * value * (1.0 + lax.erf(value * 0.7071067811865476))


def gelu_slope(value):
    normal_cdf = 0.5 * (1.0 + lax.erf(value * 0.7071067811865476))
    return normal_cdf + value * jnp.exp(-0.5 * value * value) * 0.3989422804014327


def dot(a, b, contract):
    return lax.dot_general(a, b, (contract, ((), ())), preferred_element_type=F32)


def pick_kernel(slot_ref, arrived_ref, out_ref):
    out_ref[...] = arrived_ref[0]


def pick_tiles(tile_slot, arrived, slots):
    _, rows, _ = arrived.shape
    tiles = tile_slot.shape[0]
    return pl.pallas_call(
        pick_kernel,
        grid_spec=pltpu.PrefetchScalarGridSpec(
            num_scalar_prefetch=1,
            grid=(tiles,),
            in_specs=[
                pl.BlockSpec((1, rows, TILE), lambda t, slot: (slot[t] // slots, 0, slot[t] % slots))
            ],
            out_specs=pl.BlockSpec((rows, TILE), lambda t, slot: (0, t)),
        ),
        out_shape=jax.ShapeDtypeStruct((rows, tiles * TILE), BF16),
        cost_estimate=pl.CostEstimate(flops=0, bytes_accessed=4 * rows * tiles * TILE, transcendentals=0),
    )(tile_slot, arrived)


def weight_copies(weights, held, sems):
    return [pltpu.make_async_copy(w, b, sems.at[i]) for i, (w, b) in enumerate(zip(weights, held))]


def gate_body(place_ref, h_ref, weights, out_ref, held, sems):
    n = len(weights) // 2
    copies = weight_copies(weights, held, sems)
    for i in range(n):
        copies[i].start()
        copies[i + n].start()
    core, blocks, rows = place_ref[0], out_ref.shape[0], out_ref.shape[1]
    block, at = 0, 0
    for i in range(n):
        size = held[i].shape[0]
        copies[i].wait()
        total = dot(held[i][...], h_ref[core], ((1,), (1,)))
        copies[i + n].wait()
        total = total + dot(held[i + n][...], h_ref[1 - core], ((1,), (1,)))
        chunk = (block + blocks - place_ref[1]) % blocks
        out_ref[chunk, at : at + size, :] = total.astype(BF16)
        at += size
        block, at = block + at // rows, at % rows


def dact_body(place_ref, d_ref, weights, out_ref, held, sems):
    n = len(weights) // 2
    copies = weight_copies(weights, held, sems)
    for copy in copies:
        copy.start()
    core, blocks, rows = place_ref[0], d_ref.shape[0], d_ref.shape[1]
    step = 256
    for j in range(2):
        for i in range(n):
            copies[j * n + i].wait()
        slot = core if j == 0 else 1 - core
        for c in range(0, out_ref.shape[2], step):
            total, block, at = None, 0, 0
            for i in range(n):
                w = held[j * n + i]
                size = w.shape[0]
                chunk = (block + blocks - place_ref[1]) % blocks
                term = dot(d_ref[chunk, at : at + size, :], w[:, c : c + step], ((0,), (0,)))
                total = term if total is None else total + term
                at += size
                block, at = block + at // rows, at % rows
            out_ref[slot, :, c : c + step] = total.astype(BF16)


def with_weights(body, place, operand, weights, out_shape, flops):
    n = len(weights)

    def kernel(place_ref, operand_ref, *refs):
        body(place_ref, operand_ref, refs[:n], refs[n], refs[n + 1 : -1], refs[-1])

    moved = sum(w.size for w in weights) + operand.size
    return pl.pallas_call(
        kernel,
        in_specs=[pl.BlockSpec(memory_space=pltpu.SMEM), pl.BlockSpec(memory_space=pltpu.VMEM)]
        + [pl.BlockSpec(memory_space=pl.ANY)] * n,
        out_specs=pl.BlockSpec(memory_space=pltpu.VMEM),
        out_shape=jax.ShapeDtypeStruct(out_shape, BF16),
        scratch_shapes=[pltpu.VMEM(w.shape, BF16) for w in weights] + [pltpu.SemaphoreType.DMA((n,))],
        compiler_params=pltpu.CompilerParams(vmem_limit_bytes=60 * 2**20),
        cost_estimate=pl.CostEstimate(flops=flops, bytes_accessed=2 * moved, transcendentals=0),
    )(place, operand, *weights)


def shards(tile_rows, tile_slot, proj_weight, gate_weight, up_weight, cotangent):
    n_vis, n_row, n_col = lax.axis_size("vis"), lax.axis_size("row"), lax.axis_size("col")
    n_x = tile_slot.shape[0]
    n_low = n_row // n_x
    n_quarter = n_col // 2
    row, col, vis = lax.axis_index("row"), lax.axis_index("col"), lax.axis_index("vis")
    core, quarter, x = col % 2, col // 2, row % n_x
    features = tile_rows.shape[1]
    half = features // 2
    slots = tile_rows.shape[0] // TILE
    core_pairs = [(2 * i + k, 2 * i + 1 - k) for i in range(n_quarter) for k in range(2)]
    quarter_groups = [[2 * i + k for i in range(n_quarter)] for k in range(2)]
    sheet_groups = [
        [(low * n_x + i) * n_vis + v for i in range(n_x) for low in range(n_low) for v in range(n_vis)]
    ]
    column_groups = [
        [
            ((low * n_x + i) * n_col + 2 * q + k) * n_vis + v
            for k in range(2)
            for low in range(n_low)
            for v in range(n_vis)
        ]
        for i in range(n_x)
        for q in range(n_quarter)
    ]
    shifts = [0, 1, 3, 2]

    rows_t = tile_rows.T
    own_half = lax.dynamic_slice_in_dim(rows_t, core * half, half, 0)
    own_half = jnp.broadcast_to(own_half[None], (n_vis,) + own_half.shape)

    unit = gate_weight.shape[1]
    pad = -unit % 8
    weights = jnp.stack([gate_weight.T, up_weight.T])
    weights = jnp.pad(weights, ((0, 0), (0, pad), (0, 0))).reshape(2 * (unit + pad), -1)

    def from_x(value, shift):
        pairs = [
            (low * n_x + i, low * n_x + (i - shift) % n_x) for low in range(n_low) for i in range(n_x)
        ]
        return lax.ppermute(value, "row", pairs)

    def from_core(value):
        return lax.ppermute(value, "col", core_pairs)

    arrived = lax.all_to_all(own_half, "vis", 0, 0)
    right, left, weights_o = from_x(weights, 1), from_x(weights, -1), from_core(weights)
    mine = pick_tiles(tile_slot, arrived, slots)
    other = from_core(mine)
    other, right, left, weights_o = lax.optimization_barrier((other, right, left, weights_o))
    far_gate, far_up = right[: unit + pad], left[unit + pad :]
    first = jnp.where(core == 0, mine, other)
    second = jnp.where(core == 0, other, mine)
    tokens_t = jnp.concatenate([first, second], axis=0)

    partial = dot(tokens_t, proj_weight, ((0,), (0,))).astype(BF16)
    n_tok, width = partial.shape
    spread = n_low * n_vis
    share = TILE // spread
    few = share // 2
    lane = TILE // 2
    model = n_vis * width
    partial = jnp.transpose(partial.reshape(n_x, 2, spread, few, width), (0, 2, 1, 3, 4))
    partial = partial.reshape(n_x * spread, share, width)
    partial = lax.all_to_all(partial, ("row", "vis"), 0, 0, axis_index_groups=sheet_groups)
    far_gate, far_up = from_x(far_gate, 1), from_x(far_up, -1)
    partial, far_gate, far_up = lax.optimization_barrier((partial, far_gate, far_up))
    preact = jnp.sum(partial.reshape(n_row, n_vis, share, width).astype(F32), axis=0)
    preact = jnp.transpose(preact, (1, 0, 2)).reshape(share, model)
    hidden = gelu_exact(preact).astype(BF16)
    slope = gelu_slope(preact)
    hidden = jnp.broadcast_to(hidden.reshape(2, 1, few, model), (2, spread, few, model))
    hidden = hidden.reshape(2 * spread, few, model)
    hidden = lax.all_to_all(hidden, ("row", "col", "vis"), 0, 0, axis_index_groups=column_groups)
    right_o, left_o, far_gate_o, far_up_o = [from_core(w) for w in (right, left, far_gate, far_up)]
    pieces = [weights, right, left, far_gate, far_up, weights_o, right_o, left_o, far_gate_o, far_up_o]
    hidden = hidden.reshape(2, lane, model)

    offset = (x + n_x - vis) % n_x
    part = sum(jnp.where(offset == shifts[k], k, 0) for k in range(n_x))
    part = (part + n_x - quarter) % n_x
    cot = lax.dynamic_slice(cotangent.T, (part * unit, core * lane), (unit, lane))
    cot_pairs = []
    for low in range(n_low):
        for i in range(n_x):
            for v in range(n_vis):
                for q in range(n_quarter):
                    for k in range(2):
                        there = (low * n_x + (i + shifts[(v + q) % n_x]) % n_x) * n_col + 2 * q + k
                        here = (low * n_x + i) * n_col + 2 * q + k
                        cot_pairs.append((there * n_vis + i, here * n_vis + v))
    cot = lax.ppermute(cot, ("row", "col", "vis"), cot_pairs)
    cot = jnp.pad(cot.astype(F32), ((0, pad), (0, 0)))

    rows = 2 * (unit + pad)
    flops = 4 * lane * n_x * rows * model
    place = jnp.stack([core, vis])
    both = with_weights(gate_body, place, hidden, pieces, (n_x, rows, lane), flops)
    sums = lax.all_to_all(both, "col", 0, 0, axis_index_groups=quarter_groups)
    sums = jnp.sum(sums.astype(F32), axis=0)
    gate_sum, up_sum = sums[: unit + pad], sums[unit + pad :]
    sig = jax.nn.sigmoid(gate_sum)
    d_gate = (cot * up_sum * sig * (1.0 + gate_sum * (1.0 - sig))).astype(BF16)
    d_up = (cot * gate_sum * sig).astype(BF16)
    d_both = jnp.concatenate([d_gate, d_up], axis=0)
    d_all = lax.all_gather(d_both, "col", axis=0, axis_index_groups=quarter_groups)

    dact = with_weights(dact_body, place, d_all, pieces, (2, lane, model), flops)
    dact = lax.all_to_all(
        dact.reshape(2 * spread, few, model), ("row", "col", "vis"), 0, 0, axis_index_groups=column_groups
    )
    dact = jnp.sum(dact.reshape(2, spread, few, model).astype(F32), axis=1).reshape(share, model)
    dpre = (dact * slope).astype(BF16)
    dpre = jnp.transpose(dpre.reshape(share, n_vis, width), (1, 0, 2))
    dpre = jnp.broadcast_to(dpre[None], (n_row, n_vis, share, width))
    dpre = lax.all_to_all(
        dpre.reshape(n_x * spread, share, width), ("row", "vis"), 0, 0, axis_index_groups=sheet_groups
    )
    dpre = jnp.transpose(dpre.reshape(n_x, spread, 2, few, width), (0, 2, 1, 3, 4))
    dpre = dpre.reshape(n_tok, width)
    return dot(tokens_t, dpre, ((1,), (0,))).astype(BF16)


def solution(mesh):
    in_specs = (
        P("vis", "row"),
        P(),
        P("row", ("col", "vis")),
        P("col", ("row", "vis")),
        P("col", ("row", "vis")),
        P("vis", "row"),
    )
    out_specs = P("row", ("col", "vis"))
    return jax.shard_map(shards, mesh=mesh, in_specs=in_specs, out_specs=out_specs, check_vma=False)
```

time: 262 us -> 227 us (0.87)
  waiting for transfers between devices: 92.3 us -> 48.5 us
  between operations: 24 us -> 0.35 us
  starting transfers between devices: 51 us -> 72.7 us
  Pallas kernels: 0 us -> 18.3 us
  matrix products: 12.5 us -> 2.11 us
  local copies, waits for them, and re-layouts: 5.88 us -> 10.6 us
    all_gather x2 -> x0, waiting for transfers between devices: 33.3 us -> none  [the longest x1 27.7 us: shards(): gate_block = lax.all_gather(gate_t, 'vis', axis=0)]
    all_to_all x3 -> x2, blocking collectives: 72.5 us -> 48.2 us  [the longest x1 26.9 us: shards(): lax.all_to_all(dact.reshape(2 * spread, few, model), ('row', 'col', 'vis'...]
    all_gather x0 -> x1, blocking collectives: none -> 21.8 us  [shards(): lax.all_gather(d_both, 'col', axis=0, axis_index_groups=quarter_groups)]
    all_to_all x4, waiting for transfers between devices: 53.3 us -> 32.3 us  [the longest x1 25.4 us: shards(): sums = lax.all_to_all(both, 'col', 0, 0, axis_index_groups=quarter_groups)]
    pallas_call x0 -> x3, Pallas kernels: none -> 18.3 us  [the longest x2 14.3 us: with_weights(): pl.pallas_call(kernel, in_specs=[pl.BlockSpec(memory_space=pltpu.SMEM), p...]
    ppermute x3 -> x11, starting transfers between devices: 20.7 us -> 37.3 us  [the longest x6 24.1 us: from_core(): return lax.ppermute(value, 'col', core_pairs)]
    ppermute x3 -> x11, waiting for transfers between devices: 4.99 us -> 16.2 us  [the longest x4 12.8 us: from_x(): return lax.ppermute(value, 'row', pairs)]
    dot_general x18 -> x2, matrix products: 12.5 us -> 2.11 us  [dot(): lax.dot_general(a, b, (contract, ((), ())), preferred_element_type=F32)]
  transfers between devices with their start and end apart: 9 -> 15, of which waited for: 9 -> 7; matrix products, arithmetic and copies ran while one was open for 3% -> 2% of each run, Pallas kernels for 0% -> 2%
where the time goes in v2:
time: 227 us; the launch traced here: 226 us
  starting transfers between devices  72.7 us (32%)
  blocking collectives  70 us (31%)
  waiting for transfers between devices  48.5 us (21%)
  Pallas kernels  18.3 us (8%)
  local copies, waits for them, and re-layouts  10.6 us (5%)
  other arithmetic  3.46 us (2%)
    all_to_all x1, blocking collectives, shards(): lax.all_to_all(dact.reshape(2 * spread, few, model), ('row', 'col', 'vis'...  26.9 us
    all_to_all x1, waiting for transfers between devices, shards(): sums = lax.all_to_all(both, 'col', 0, 0, axis_index_groups=quarter_groups)  25.4 us
    ppermute x6, starting transfers between devices, from_core(): return lax.ppermute(value, 'col', core_pairs)  24.1 us
    all_gather x1, blocking collectives, shards(): lax.all_gather(d_both, 'col', axis=0, axis_index_groups=quarter_groups)  21.8 us
    all_to_all x1, blocking collectives, shards(): lax.all_to_all(dpre.reshape(n_x * spread, share, width), ('row', 'vis'),...  21.2 us
    pallas_call x2, Pallas kernels, with_weights(): pl.pallas_call(kernel, in_specs=[pl.BlockSpec(memory_space=pltpu.SMEM), p...  14.3 us
    ppermute x4, waiting for transfers between devices, from_x(): return lax.ppermute(value, 'row', pairs)  12.8 us
    ppermute x4, starting transfers between devices, from_x(): return lax.ppermute(value, 'row', pairs)  12.6 us
  transfers between devices with their start and end apart: 15, of which 7 were waited for; matrix products, arithmetic and copies ran while one was open for 2% of the time, Pallas kernels for 2%

profile of v2, /device:TPU:1, one launch (start us, length us, event | category | flops | bytes accessed | tf_op | source)
XLA Modules:
  0.0 226.1 jit_solution(16388067293977943858)
XLA Ops:
  1.2 1.3 broadcast_in_dim.6
  2.5 5.0 %all-to-all-start = ((bf16[4,400,512]{2,1,0:T(8,128)(2,1)}), bf16[4,400,512]{2,1,0:T(8,128)(2,1)S(1)}, u32[]{:S(2)}, u32[]{:S(2)}) async-start(bf16[4,400,512]{2,1,0:T(8,128)(2,1)} %broadcast_in_dim.6), calls=%async_computation | async-start | bytes 3276800 | tf_op jit(solution)/shard_map/all_to_all | solution.py:160
  7.5 1.3 fusion.2
  8.8 4.4 %collective-permute-start.1 = (bf16[464,1024]{1,0:T(8,128)(2,1)S(1)}, bf16[464,1024]{1,0:T(8,128)(2,1)}, u32[]{:S(2)}, u32[]{:S(2)}) collective-permute-start(bf16[464,1024]{1,0:T(8,128)(2,1)S(1)} %bitcast.53), channel_id=1, source_target_pairs={{0,96},{32,0},{64,32},{96,64},{128,224},{160,128},{192,160},{224,1... | collective-permute-start | bytes 2850824 | tf_op jit(solution)/shard_map/ppermute | solution.py:155
  13.2 1.9 collective-permute-start.2
  15.1 6.9 %collective-permute-start.3 = (bf16[464,1024]{1,0:T(8,128)(2,1)S(1)}, bf16[464,1024]{1,0:T(8,128)(2,1)}, u32[]{:S(2)}, u32[]{:S(2)}) collective-permute-start(bf16[464,1024]{1,0:T(8,128)(2,1)S(1)} %bitcast.55), channel_id=1, source_target_pairs={{0,4},{4,0},{8,12},{12,8},{16,20},{20,16},{24,28},{28,24},{1,5},{5... | collective-permute-start | bytes 2850824 | tf_op jit(solution)/shard_map/ppermute | solution.py:158
  22.0 1.3 all-to-all-done.arrived_ref
  23.3 1.2 copy-done.2
  24.4 4.1 %shard_map.64 = bf16[400,1024]{1,0:T(8,128)(2,1)} custom-call(s32[4]{0:T(128)} %slot_ref.1, bf16[4,400,512]{2,1,0:T(8,128)(2,1)} %copy-done.2), custom_call_target="tpu_custom_call" | custom-call | bytes 1638400 | tf_op jit(solution)/shard_map/pallas_call | solution.py:33
  28.5 8.5 %collective-permute-start = (bf16[400,1024]{1,0:T(8,128)(2,1)}, bf16[400,1024]{1,0:T(8,128)(2,1)S(1)}, u32[]{:S(2)}, u32[]{:S(2)}) collective-permute-start(bf16[400,1024]{1,0:T(8,128)(2,1)} %shard_map.64), channel_id=1, source_target_pairs={{0,4},{4,0},{8,12},{12,8},{16,20},{20,16},{24,28},{28,24},{1,5},{5... | collective-permute-start | bytes 2457608 | tf_op jit(solution)/shard_map/ppermute | solution.py:158
  37.1 2.1 collective-permute-done
  39.2 1.3 broadcast_select_fusion.1
  42.5 9.7 %all-to-all-start.1 = ((bf16[64,16,256]{2,1,0:T(8,128)(2,1)}), bf16[64,16,256]{2,1,0:T(8,128)(2,1)S(1)}, u32[]{:S(2)}, u32[]{:S(2)}) async-start(bf16[64,16,256]{2,1,0:T(8,128)(2,1)} %bitcast.11), calls=%async_computation.1 | async-start | bytes 1048576 | tf_op jit(solution)/shard_map/all_to_all | solution.py:179
  53.3 4.3 %collective-permute-start.5 = (bf16[232,1024]{1,0:T(8,128)(2,1)S(1)}, bf16[232,1024]{1,0:T(8,128)(2,1)S(1)}, u32[]{:S(2)}, u32[]{:S(2)}) collective-permute-start(bf16[232,1024]{1,0:T(8,128)(2,1)S(1)} %slice.12), channel_id=1, source_target_pairs={{0,96},{32,0},{64,32},{96,64},{128,224},{160,128},{192,160},{224,1... | collective-permute-start | bytes 1425416 | tf_op jit(solution)/shard_map/ppermute | solution.py:155
  58.7 1.9 collective-permute-start.6
  60.6 9.8 %collective-permute-done.5.refs_3_ = bf16[232,1024]{1,0:T(8,128)(2,1)S(1)} collective-permute-done((bf16[232,1024]{1,0:T(8,128)(2,1)S(1)}, bf16[232,1024]{1,0:T(8,128)(2,1)S(1)}, u32[]{:S(2)}, u32[]{:S(2)}) %collective-permute-start.5) | collective-permute-done | bytes 475168 | tf_op jit(solution)/shard_map/ppermute | solution.py:155
  71.2 3.0 %collective-permute-done.6.refs_4_ = bf16[232,1024]{1,0:T(8,128)(2,1)} collective-permute-done((bf16[232,1024]{1,0:T(8,128)(2,1)S(1)}, bf16[232,1024]{1,0:T(8,128)(2,1)}, u32[]{:S(2)}, u32[]{:S(2)}) %collective-permute-start.6) | collective-permute-done | bytes 475168 | tf_op jit(solution)/shard_map/ppermute | solution.py:155
  75.2 8.6 %all-to-all-start.2 = ((bf16[32,8,1024]{2,1,0:T(8,128)(2,1)}), bf16[32,8,1024]{2,1,0:T(8,128)(2,1)S(1)}, u32[]{:S(2)}, u32[]{:S(2)}) async-start(bf16[32,8,1024]{2,1,0:T(8,128)(2,1)} %bitcast.14), calls=%async_computation.2 | async-start | bytes 1048576 | tf_op jit(solution)/shard_map/all_to_all | solution.py:188
  83.8 2.1 collective-permute-start.7
  86.0 2.2 collective-permute-start.8
  88.2 2.1 collective-permute-start.9
  90.3 2.2 collective-permute-start.10
  93.1 1.2 collective-permute-done.10.refs_9_
  94.4 5.7 %all-to-all-done.2 = bf16[32,8,1024]{2,1,0:T(8,128)(2,1)S(1)} async-done(((bf16[32,8,1024]{2,1,0:T(8,128)(2,1)}), bf16[32,8,1024]{2,1,0:T(8,128)(2,1)S(1)}, u32[]{:S(2)}, u32[]{:S(2)}) %all-to-all-start.2) | async-done | bytes 524320 | tf_op jit(solution)/shard_map/all_to_all | solution.py:188
  100.9 8.4 %shard_map.65 = bf16[4,464,128]{2,1,0:T(8,128)(2,1)} custom-call(s32[2]{0:T(128)} %pad_add_fusion.place_ref, bf16[2,128,1024]{2,1,0:T(8,128)(2,1)} %bitcast.58, bf16[464,1024]{1,0:T(8,128)(2,1)} %bitcast.56, bf16[464,1024]{1,0:T(8,128)(2,1)} %collective-permute-done.1.refs_1_, bf16[464,1024]{1,0:T(8,128)(2,1)} %collective-permute-done.2.refs_2_, ...), custom_call_target="tpu_custom_call" | custom-call | flops 973078528 | bytes 8126464 | tf_op jit(solution)/shard_map/pallas_call | solution.py:103
  109.3 12.1 %all-to-all-start.3 = ((bf16[4,464,128]{2,1,0:T(8,128)(2,1)}), bf16[4,464,128]{2,1,0:T(8,128)(2,1)S(1)}, u32[]{:S(2)}, u32[]{:S(2)}) async-start(bf16[4,464,128]{2,1,0:T(8,128)(2,1)} %shard_map.65), calls=%async_computation.3 | async-start | bytes 950272 | tf_op jit(solution)/shard_map/all_to_all | solution.py:213
  123.0 25.4 %all-to-all-done.3 = bf16[4,464,128]{2,1,0:T(8,128)(2,1)S(1)} async-done(((bf16[4,464,128]{2,1,0:T(8,128)(2,1)}), bf16[4,464,128]{2,1,0:T(8,128)(2,1)S(1)}, u32[]{:S(2)}, u32[]{:S(2)}) %all-to-all-start.3) | async-done | bytes 475168 | tf_op jit(solution)/shard_map/all_to_all | solution.py:213
  148.5 21.8 %all-gather = bf16[1856,128]{1,0:T(8,128)(2,1)} all-gather(bf16[464,128]{1,0:T(8,128)(2,1)S(1)} %pad_maximum_fusion.3), channel_id=2, replica_groups={{0,8,16,24},{4,12,20,28},{1,9,17,25},{5,13,21,29},{2,10,18,26},{6,14,22..., dimensions={0}, use_global_device_ids=true | all-gather | bytes 593920 | tf_op jit(solution)/shard_map/all_gather | solution.py:220
  170.4 5.9 %shard_map.66 = bf16[2,128,1024]{2,1,0:T(8,128)(2,1)} custom-call(s32[2]{0:T(128)} %pad_add_fusion.place_ref, bf16[4,464,128]{2,1,0:T(8,128)(2,1)} %bitcast.63, bf16[464,1024]{1,0:T(8,128)(2,1)} %bitcast.57, bf16[464,1024]{1,0:T(8,128)(2,1)} %collective-permute-done.1.refs_1_, bf16[464,1024]{1,0:T(8,128)(2,1)} %collective-permute-done.2.refs_2_, ...), custom_call_target="tpu_custom_call" | custom-call | flops 973078528 | bytes 8077312 | tf_op jit(solution)/shard_map/pallas_call | solution.py:103
  176.3 26.9 %all_to_all.30 = bf16[32,8,1024]{2,1,0:T(8,128)(2,1)S(1)} all-to-all(bf16[32,8,1024]{2,1,0:T(8,128)(2,1)} %bitcast.59), channel_id=1, replica_groups={{0,1,2,3,128,129,130,131,256,257,258,259,384,385,386,387,4,5,6,7,132,13..., dimensions={0} | all-to-all | bytes 1048576 | tf_op jit(solution)/shard_map/all_to_all | solution.py:223
  203.4 21.2 %all_to_all.31 = bf16[64,16,256]{2,1,0:T(8,128)(2,1)S(1)} all-to-all(bf16[64,16,256]{2,1,0:T(8,128)(2,1)S(1)} %bitcast.61), channel_id=1, replica_groups={{0,1,2,3,128,129,130,131,256,257,258,259,384,385,386,387,32,33,34,35,16..., dimensions={0} | all-to-all | bytes 1048576 | tf_op jit(solution)/shard_map/all_to_all | solution.py:230
  224.7 1.3 convolution_convert_fusion.1
  (52 shorter events, 10.5 us)
Async XLA Ops:
  0.0 1.1 copy-start
  2.5 20.8 %all-to-all-start = ((bf16[4,400,512]{2,1,0:T(8,128)(2,1)}), bf16[4,400,512]{2,1,0:T(8,128)(2,1)S(1)}, u32[]{:S(2)}, u32[]{:S(2)}) async-start(bf16[4,400,512]{2,1,0:T(8,128)(2,1)} %broadcast_in_dim.6), calls=%async_computation | async-start | bytes 3276800 | tf_op jit(solution)/shard_map/all_to_all | solution.py:160
  8.8 31.7 %copy-start.1 = (bf16[2,232,1024]{2,1,0:T(8,128)(2,1)}, bf16[2,232,1024]{2,1,0:T(8,128)(2,1)S(1)}, u32[]{:S(2)}) copy-start(bf16[2,232,1024]{2,1,0:T(8,128)(2,1)S(1)} %fusion.2) | copy-start | bytes 2850820
  8.8 28.3 %collective-permute-start.1 = (bf16[464,1024]{1,0:T(8,128)(2,1)S(1)}, bf16[464,1024]{1,0:T(8,128)(2,1)}, u32[]{:S(2)}, u32[]{:S(2)}) collective-permute-start(bf16[464,1024]{1,0:T(8,128)(2,1)S(1)} %bitcast.53), channel_id=1, source_target_pairs={{0,96},{32,0},{64,32},{96,64},{128,224},{160,128},{192,160},{224,1... | collective-permute-start | bytes 2850824 | tf_op jit(solution)/shard_map/ppermute | solution.py:155
  13.2 23.9 %collective-permute-start.2 = (bf16[464,1024]{1,0:T(8,128)(2,1)S(1)}, bf16[464,1024]{1,0:T(8,128)(2,1)}, u32[]{:S(2)}, u32[]{:S(2)}) collective-permute-start(bf16[464,1024]{1,0:T(8,128)(2,1)S(1)} %bitcast.54), channel_id=1, source_target_pairs={{0,32},{32,64},{64,96},{96,0},{128,160},{160,192},{192,224},{224,1... | collective-permute-start | bytes 2850824 | tf_op jit(solution)/shard_map/ppermute | solution.py:155
  15.1 22.0 %collective-permute-start.3 = (bf16[464,1024]{1,0:T(8,128)(2,1)S(1)}, bf16[464,1024]{1,0:T(8,128)(2,1)}, u32[]{:S(2)}, u32[]{:S(2)}) collective-permute-start(bf16[464,1024]{1,0:T(8,128)(2,1)S(1)} %bitcast.55), channel_id=1, source_target_pairs={{0,4},{4,0},{8,12},{12,8},{16,20},{20,16},{24,28},{28,24},{1,5},{5... | collective-permute-start | bytes 2850824 | tf_op jit(solution)/shard_map/ppermute | solution.py:158
  23.3 1.2 copy-start.2
  28.5 10.7 %collective-permute-start = (bf16[400,1024]{1,0:T(8,128)(2,1)}, bf16[400,1024]{1,0:T(8,128)(2,1)S(1)}, u32[]{:S(2)}, u32[]{:S(2)}) collective-permute-start(bf16[400,1024]{1,0:T(8,128)(2,1)} %shard_map.64), channel_id=1, source_target_pairs={{0,4},{4,0},{8,12},{12,8},{16,20},{20,16},{24,28},{28,24},{1,5},{5... | collective-permute-start | bytes 2457608 | tf_op jit(solution)/shard_map/ppermute | solution.py:158
  37.1 3.4 %copy-start.11 = (bf16[800,256]{1,0:T(8,128)(2,1)S(1)}, bf16[800,256]{1,0:T(8,128)(2,1)}, u32[]{:S(2)}) copy-start(bf16[800,256]{1,0:T(8,128)(2,1)} %param.8) | copy-start | bytes 1228804
  40.5 0.9 copy-start.7
  40.5 1.2 copy-start.9
  42.5 31.7 %all-to-all-start.1 = ((bf16[64,16,256]{2,1,0:T(8,128)(2,1)}), bf16[64,16,256]{2,1,0:T(8,128)(2,1)S(1)}, u32[]{:S(2)}, u32[]{:S(2)}) async-start(bf16[64,16,256]{2,1,0:T(8,128)(2,1)} %bitcast.11), calls=%async_computation.1 | async-start | bytes 1048576 | tf_op jit(solution)/shard_map/all_to_all | solution.py:179
  53.3 17.1 %collective-permute-start.5 = (bf16[232,1024]{1,0:T(8,128)(2,1)S(1)}, bf16[232,1024]{1,0:T(8,128)(2,1)S(1)}, u32[]{:S(2)}, u32[]{:S(2)}) collective-permute-start(bf16[232,1024]{1,0:T(8,128)(2,1)S(1)} %slice.12), channel_id=1, source_target_pairs={{0,96},{32,0},{64,32},{96,64},{128,224},{160,128},{192,160},{224,1... | collective-permute-start | bytes 1425416 | tf_op jit(solution)/shard_map/ppermute | solution.py:155
  58.7 15.5 %collective-permute-start.6 = (bf16[232,1024]{1,0:T(8,128)(2,1)S(1)}, bf16[232,1024]{1,0:T(8,128)(2,1)}, u32[]{:S(2)}, u32[]{:S(2)}) collective-permute-start(bf16[232,1024]{1,0:T(8,128)(2,1)S(1)} %slice.13), channel_id=1, source_target_pairs={{0,32},{32,64},{64,96},{96,0},{128,160},{160,192},{192,224},{224,1... | collective-permute-start | bytes 1425416 | tf_op jit(solution)/shard_map/ppermute | solution.py:155
  70.4 0.8 copy-start.6
  75.2 24.9 %all-to-all-start.2 = ((bf16[32,8,1024]{2,1,0:T(8,128)(2,1)}), bf16[32,8,1024]{2,1,0:T(8,128)(2,1)S(1)}, u32[]{:S(2)}, u32[]{:S(2)}) async-start(bf16[32,8,1024]{2,1,0:T(8,128)(2,1)} %bitcast.14), calls=%async_computation.2 | async-start | bytes 1048576 | tf_op jit(solution)/shard_map/all_to_all | solution.py:188
  83.8 9.3 %collective-permute-start.7 = (bf16[464,1024]{1,0:T(8,128)(2,1)}, bf16[464,1024]{1,0:T(8,128)(2,1)S(1)}, u32[]{:S(2)}, u32[]{:S(2)}) collective-permute-start(bf16[464,1024]{1,0:T(8,128)(2,1)} %collective-permute-done.1.refs_1_), channel_id=1, source_target_pairs={{0,4},{4,0},{8,12},{12,8},{16,20},{20,16},{24,28},{28,24},{1,5},{5... | collective-permute-start | bytes 2850824 | tf_op jit(solution)/shard_map/ppermute | solution.py:158
  86.0 7.2 %collective-permute-start.8 = (bf16[464,1024]{1,0:T(8,128)(2,1)}, bf16[464,1024]{1,0:T(8,128)(2,1)S(1)}, u32[]{:S(2)}, u32[]{:S(2)}) collective-permute-start(bf16[464,1024]{1,0:T(8,128)(2,1)} %collective-permute-done.2.refs_2_), channel_id=1, source_target_pairs={{0,4},{4,0},{8,12},{12,8},{16,20},{20,16},{24,28},{28,24},{1,5},{5... | collective-permute-start | bytes 2850824 | tf_op jit(solution)/shard_map/ppermute | solution.py:158
  88.2 5.0 %collective-permute-start.9 = (bf16[232,1024]{1,0:T(8,128)(2,1)}, bf16[232,1024]{1,0:T(8,128)(2,1)}, u32[]{:S(2)}, u32[]{:S(2)}) collective-permute-start(bf16[232,1024]{1,0:T(8,128)(2,1)} %copy-done.6), channel_id=1, source_target_pairs={{0,4},{4,0},{8,12},{12,8},{16,20},{20,16},{24,28},{28,24},{1,5},{5... | collective-permute-start | bytes 1425416 | tf_op jit(solution)/shard_map/ppermute | solution.py:158
  90.3 4.1 %collective-permute-start.10 = (bf16[232,1024]{1,0:T(8,128)(2,1)}, bf16[232,1024]{1,0:T(8,128)(2,1)}, u32[]{:S(2)}, u32[]{:S(2)}) collective-permute-start(bf16[232,1024]{1,0:T(8,128)(2,1)} %collective-permute-done.6.refs_4_), channel_id=1, source_target_pairs={{0,4},{4,0},{8,12},{12,8},{16,20},{20,16},{24,28},{28,24},{1,5},{5... | collective-permute-start | bytes 1425416 | tf_op jit(solution)/shard_map/ppermute | solution.py:158
  93.1 7.0 %copy-start.3 = (bf16[464,1024]{1,0:T(8,128)(2,1)}, bf16[464,1024]{1,0:T(8,128)(2,1)S(1)}, u32[]{:S(2)}) copy-start(bf16[464,1024]{1,0:T(8,128)(2,1)S(1)} %collective-permute-done.7.refs_6_) | copy-start | bytes 2850820
  93.1 7.0 %copy-start.4 = (bf16[464,1024]{1,0:T(8,128)(2,1)}, bf16[464,1024]{1,0:T(8,128)(2,1)S(1)}, u32[]{:S(2)}) copy-start(bf16[464,1024]{1,0:T(8,128)(2,1)S(1)} %collective-permute-done.8.refs_7_) | copy-start | bytes 2850820
  100.1 0.8 copy-start.5
  109.3 39.1 %all-to-all-start.3 = ((bf16[4,464,128]{2,1,0:T(8,128)(2,1)}), bf16[4,464,128]{2,1,0:T(8,128)(2,1)S(1)}, u32[]{:S(2)}, u32[]{:S(2)}) async-start(bf16[4,464,128]{2,1,0:T(8,128)(2,1)} %shard_map.65), calls=%async_computation.3 | async-start | bytes 950272 | tf_op jit(solution)/shard_map/all_to_all | solution.py:213
  122.3 26.1 %collective-permute-start.4 = (bf16[231,128]{1,0:T(8,128)(2,1)S(1)}, bf16[231,128]{1,0:T(8,128)(2,1)S(1)}, u32[]{:S(2)}, u32[]{:S(2)}) collective-permute-start(bf16[231,128]{1,0:T(8,128)(2,1)S(1)} %dynamic-slice_bitcast_fusion.1), channel_id=1, source_target_pairs={{0,0},{4,4},{40,8},{44,12},{112,16},{116,20},{88,24},{92,28},{32,1... | collective-permute-start | bytes 177416 | tf_op jit(solution)/shard_map/ppermute | solution.py:206
  203.2 21.5 %copy-start.8 = (bf16[400,1024]{1,0:T(8,128)(2,1)S(1)}, bf16[400,1024]{1,0:T(8,128)(2,1)}, u32[]{:S(2)}) copy-start(bf16[400,1024]{1,0:T(8,128)(2,1)} %copy-done.7) | copy-start | bytes 2457604
  203.2 21.5 %copy-start.10 = (bf16[400,1024]{1,0:T(8,128)(2,1)S(1)}, bf16[400,1024]{1,0:T(8,128)(2,1)}, u32[]{:S(2)}) copy-start(bf16[400,1024]{1,0:T(8,128)(2,1)} %copy-done.9) | copy-start | bytes 2457604

commit v3 on v2

v3 whole, which is shorter than its diff:
```python
import jax
import jax.numpy as jnp
from jax import lax
from jax.experimental import pallas as pl
from jax.experimental.pallas import tpu as pltpu
from jax.sharding import PartitionSpec as P

TILE = 256
F32 = jnp.float32
BF16 = jnp.bfloat16
KERNEL_VMEM = 60 * 2**20
SMALL_VMEM = 24 * 2**20


def gelu_exact(value):
    return 0.5 * value * (1.0 + lax.erf(value * 0.7071067811865476))


def gelu_slope(value):
    normal_cdf = 0.5 * (1.0 + lax.erf(value * 0.7071067811865476))
    return normal_cdf + value * jnp.exp(-0.5 * value * value) * 0.3989422804014327


def dot(a, b, contract):
    return lax.dot_general(a, b, (contract, ((), ())), preferred_element_type=F32)


def in_vmem(body, n_scalars, out_shape, operands, flops, scratch=()):
    spaces = [pltpu.SMEM] * n_scalars + [pltpu.VMEM] * (len(operands) - n_scalars)
    moved = 2 * sum(a.size for a in operands[n_scalars:])
    return pl.pallas_call(
        body,
        in_specs=[pl.BlockSpec(memory_space=space) for space in spaces],
        out_specs=pl.BlockSpec(memory_space=pltpu.VMEM),
        out_shape=jax.ShapeDtypeStruct(out_shape, BF16),
        scratch_shapes=list(scratch),
        compiler_params=pltpu.CompilerParams(vmem_limit_bytes=SMALL_VMEM),
        cost_estimate=pl.CostEstimate(flops=flops, bytes_accessed=moved, transcendentals=0),
    )(*operands)


def pick_kernel(slot_ref, arrived_ref, out_ref):
    per_group = arrived_ref.shape[2] // TILE
    for t in range(slot_ref.shape[0]):
        slot = slot_ref[t]
        lanes = pl.multiple_of(lax.rem(slot, per_group) * TILE, TILE)
        out_ref[:, t * TILE : (t + 1) * TILE] = arrived_ref[lax.div(slot, per_group), :, pl.ds(lanes, TILE)]


def proj_kernel(place_ref, mine_ref, other_ref, weight_ref, right_hbm, left_hbm, out_ref, low_ref, high_ref, sems):
    first = low_ref.shape[0]
    low_copy = pltpu.make_async_copy(right_hbm.at[pl.ds(0, first)], low_ref, sems.at[0])
    high_copy = pltpu.make_async_copy(left_hbm.at[pl.ds(first, high_ref.shape[0])], high_ref, sems.at[1])
    low_copy.start()
    high_copy.start()
    half = mine_ref.shape[0]
    core = place_ref[0]
    w_mine = weight_ref[pl.ds(pl.multiple_of(core * half, 16), half), :]
    w_other = weight_ref[pl.ds(pl.multiple_of((1 - core) * half, 16), half), :]
    tiles = mine_ref.shape[1] // TILE
    lows, few = out_ref.shape[0] // tiles, out_ref.shape[1] // 2
    for t in range(tiles):
        tokens = slice(t * TILE, (t + 1) * TILE)
        total = dot(mine_ref[:, tokens], w_mine, ((0,), (0,)))
        total = (total + dot(other_ref[:, tokens], w_other, ((0,), (0,)))).astype(BF16)
        for k in range(2):
            for low in range(lows):
                at = (k * lows + low) * few
                out_ref[t * lows + low, k * few : (k + 1) * few, :] = total[at : at + few]
    low_copy.wait()
    high_copy.wait()


def project(place, mine, other, weight, right, left, out_shape, flops):
    rows, model = right.shape
    first = -(rows // -32) * 16
    hbm, vmem = pl.BlockSpec(memory_space=pltpu.HBM), pl.BlockSpec(memory_space=pltpu.VMEM)
    moved = 2 * (mine.size + other.size + weight.size + right.size)
    return pl.pallas_call(
        proj_kernel,
        in_specs=[pl.BlockSpec(memory_space=pltpu.SMEM), vmem, vmem, vmem, hbm, hbm],
        out_specs=(vmem,) * 3,
        out_shape=(
            jax.ShapeDtypeStruct(out_shape, BF16),
            jax.ShapeDtypeStruct((first, model), BF16),
            jax.ShapeDtypeStruct((rows - first, model), BF16),
        ),
        scratch_shapes=[pltpu.SemaphoreType.DMA((2,))],
        compiler_params=pltpu.CompilerParams(vmem_limit_bytes=SMALL_VMEM),
        cost_estimate=pl.CostEstimate(flops=flops, bytes_accessed=moved, transcendentals=0),
    )(place, mine, other, weight, right, left)


def final_kernel(place_ref, mine_ref, other_ref, dpre_ref, out_ref, ordered_ref):
    half = mine_ref.shape[0]
    core = place_ref[0]
    tiles = mine_ref.shape[1] // TILE
    lows, few = dpre_ref.shape[0] // tiles, dpre_ref.shape[1] // 2
    for t in range(tiles):
        for k in range(2):
            for low in range(lows):
                at = t * TILE + (k * lows + low) * few
                ordered_ref[at : at + few, :] = dpre_ref[t * lows + low, k * few : (k + 1) * few, :]
    dpre = ordered_ref[...]
    first = pl.ds(pl.multiple_of(core * half, 16), half)
    second = pl.ds(pl.multiple_of((1 - core) * half, 16), half)
    out_ref[first, :] = dot(mine_ref[...], dpre, ((1,), (0,))).astype(BF16)
    out_ref[second, :] = dot(other_ref[...], dpre, ((1,), (0,))).astype(BF16)


def gate_body(place_ref, h_ref, weights, out_ref, held, sems, turned):
    n = len(weights) // 2
    copies = weight_copies(weights, held, sems)
    for i in range(n):
        copies[i].start()
        copies[i + n].start()
    core, blocks, rows = place_ref[0], out_ref.shape[0], out_ref.shape[1]
    _, lows, n_vis, few, width = h_ref.shape
    for j in range(2):
        slot = core if j == 0 else 1 - core
        for v in range(n_vis):
            block = h_ref[slot, :, v].reshape(lows * few, width)
            at = (j * n_vis + v) * width
            turned[at : at + width, :] = block.astype(F32).T.astype(BF16)
    model = n_vis * width
    block, at = 0, 0
    for i in range(n):
        size = held[i].shape[0]
        copies[i].wait()
        copies[i + n].wait()
        total = dot(held[i][...], turned[:model, :], ((1,), (0,)))
        total = total + dot(held[i + n][...], turned[model:, :], ((1,), (0,)))
        chunk = lax.rem(block + blocks - place_ref[1], blocks)
        out_ref[chunk, at : at + size, :] = total.astype(BF16)
        at += size
        block, at = block + at // rows, at % rows


def dact_body(place_ref, d_ref, weights, out_ref, held, sems, turned):
    n = len(weights) // 2
    copies = weight_copies(weights, held, sems)
    for copy in copies:
        copy.start()
    core, blocks, rows = place_ref[0], d_ref.shape[0], d_ref.shape[1]
    _, lows, n_vis, few, width = out_ref.shape
    for j in range(2):
        for i in range(n):
            copies[j * n + i].wait()
        slot = core if j == 0 else 1 - core
        for v in range(n_vis):
            total, block, at = None, 0, 0
            for i in range(n):
                w = held[j * n + i]
                size = w.shape[0]
                chunk = lax.rem(block + blocks - place_ref[1], blocks)
                term = dot(d_ref[chunk, at : at + size, :], w[:, v * width : (v + 1) * width], ((0,), (0,)))
                total = term if total is None else total + term
                at += size
                block, at = block + at // rows, at % rows
            out_ref[slot, :, v] = total.astype(BF16).reshape(lows, few, width)


def weight_copies(weights, held, sems):
    return [pltpu.make_async_copy(w, b, sems.at[i]) for i, (w, b) in enumerate(zip(weights, held))]


def with_weights(body, place, operand, weights, out_shape, flops, turned):
    n = len(weights)

    def kernel(place_ref, operand_ref, *refs):
        body(place_ref, operand_ref, refs[:n], refs[n], refs[n + 1 : -2], refs[-2], refs[-1])

    moved = sum(w.size for w in weights) + operand.size
    return pl.pallas_call(
        kernel,
        in_specs=[pl.BlockSpec(memory_space=pltpu.SMEM), pl.BlockSpec(memory_space=pltpu.VMEM)]
        + [pl.BlockSpec(memory_space=pltpu.HBM)] * n,
        out_specs=pl.BlockSpec(memory_space=pltpu.VMEM),
        out_shape=jax.ShapeDtypeStruct(out_shape, BF16),
        scratch_shapes=[pltpu.VMEM(w.shape, BF16) for w in weights]
        + [pltpu.SemaphoreType.DMA((n,)), pltpu.VMEM(turned, BF16)],
        compiler_params=pltpu.CompilerParams(vmem_limit_bytes=KERNEL_VMEM),
        cost_estimate=pl.CostEstimate(flops=flops, bytes_accessed=2 * moved, transcendentals=0),
    )(place, operand, *weights)


def shards(tile_rows, tile_slot, proj_weight, gate_weight, up_weight, cotangent):
    n_vis, n_row, n_col = lax.axis_size("vis"), lax.axis_size("row"), lax.axis_size("col")
    n_x = tile_slot.shape[0]
    n_low = n_row // n_x
    n_quarter = n_col // 2
    row, col, vis = lax.axis_index("row"), lax.axis_index("col"), lax.axis_index("vis")
    core, quarter, x = col % 2, col // 2, row % n_x
    place = jnp.stack([core, vis])
    features = tile_rows.shape[1]
    half = features // 2
    core_pairs = [(2 * i + k, 2 * i + 1 - k) for i in range(n_quarter) for k in range(2)]
    quarter_groups = [[2 * i + k for i in range(n_quarter)] for k in range(2)]
    row_groups = [[low * n_x + i for i in range(n_x) for low in range(n_low)]]
    column_groups = [
        [
            ((low * n_x + i) * n_col + 2 * q + k) * n_vis + v
            for k in range(2)
            for low in range(n_low)
            for v in range(n_vis)
        ]
        for i in range(n_x)
        for q in range(n_quarter)
    ]
    shifts = [0, 1, 3, 2]

    def from_x(value, shift):
        pairs = [
            (low * n_x + i, low * n_x + (i - shift) % n_x) for low in range(n_low) for i in range(n_x)
        ]
        return lax.ppermute(value, "row", pairs)

    def from_core(value):
        return lax.ppermute(value, "col", core_pairs)

    own_half = lax.dynamic_slice_in_dim(tile_rows.T, core * half, half, 0)
    own_half = jnp.broadcast_to(own_half[None], (n_vis,) + own_half.shape)
    arrived = lax.all_to_all(own_half, "vis", 0, 0)
    unit = gate_weight.shape[1]
    pad = -unit % 8
    weights = jnp.stack([gate_weight.T, up_weight.T])
    weights = jnp.pad(weights, ((0, 0), (0, pad), (0, 0))).reshape(2 * (unit + pad), -1)
    right, left, weights_o = from_x(weights, 1), from_x(weights, -1), from_core(weights)
    mine = in_vmem(pick_kernel, 1, (half, n_x * TILE), (tile_slot, arrived), 0)
    other = from_core(mine)
    other, right, left, weights_o = lax.optimization_barrier((other, right, left, weights_o))

    n_tok, width = n_x * TILE, proj_weight.shape[1]
    share, lane, model = n_tok // n_row, TILE // 2, n_vis * width
    few = share // 2
    flops = 2 * n_tok * features * width
    partial, far_low, far_high = project(
        place, mine, other, proj_weight, right, left, (n_row, share, width), flops
    )
    partial = lax.all_to_all(partial, "row", 0, 0, axis_index_groups=row_groups)
    far_low, far_high = from_x(far_low, 1), from_x(far_high, -1)
    preact = jnp.sum(partial.astype(F32), axis=0)
    hidden = gelu_exact(preact).astype(BF16)
    slope = gelu_slope(preact)

    spread = n_low * n_vis
    hidden = jnp.broadcast_to(hidden.reshape(2, 1, few, width), (2, spread, few, width))
    hidden, far_low, far_high = lax.optimization_barrier((hidden, far_low, far_high))
    hidden = lax.all_to_all(
        hidden.reshape(2 * spread, few, width), ("row", "col", "vis"), 0, 0, axis_index_groups=column_groups
    )
    hidden = hidden.reshape(2, n_low, n_vis, few, width)
    pieces = [weights, right, left, far_low, far_high]
    pieces += [weights_o] + [from_core(w) for w in pieces[1:]]

    offset = (x + n_x - vis) % n_x
    part = sum(jnp.where(offset == shifts[k], k, 0) for k in range(n_x))
    part = (part + n_x - quarter) % n_x
    cot = lax.dynamic_slice(cotangent.T, (part * unit, core * lane), (unit, lane))
    cot_pairs = []
    for low in range(n_low):
        for i in range(n_x):
            for v in range(n_vis):
                for q in range(n_quarter):
                    for k in range(2):
                        there = (low * n_x + (i + shifts[(v + q) % n_x]) % n_x) * n_col + 2 * q + k
                        here = (low * n_x + i) * n_col + 2 * q + k
                        cot_pairs.append((there * n_vis + i, here * n_vis + v))
    cot = lax.ppermute(cot, ("row", "col", "vis"), cot_pairs)
    cot = jnp.pad(cot.astype(F32), ((0, pad), (0, 0)))

    rows = 2 * (unit + pad)
    flops = 4 * lane * n_x * rows * model
    both = with_weights(gate_body, place, hidden, pieces, (n_x, rows, lane), flops, (2 * model, lane))
    sums = lax.all_to_all(both, "col", 0, 0, axis_index_groups=quarter_groups)
    sums = jnp.sum(sums.astype(F32), axis=0)
    gate_sum, up_sum = sums[: unit + pad], sums[unit + pad :]
    sig = jax.nn.sigmoid(gate_sum)
    d_gate = (cot * up_sum * sig * (1.0 + gate_sum * (1.0 - sig))).astype(BF16)
    d_up = (cot * gate_sum * sig).astype(BF16)
    d_both = jnp.concatenate([d_gate, d_up], axis=0)
    d_all = lax.all_gather(d_both, "col", axis=0, axis_index_groups=quarter_groups)

    shape = (2, n_low, n_vis, few, width)
    dact = with_weights(dact_body, place, d_all, pieces, shape, flops, (16, lane))
    dact = lax.all_to_all(
        dact.reshape(2 * spread, few, width), ("row", "col", "vis"), 0, 0, axis_index_groups=column_groups
    )
    dact = jnp.sum(dact.reshape(2, spread, few, width).astype(F32), axis=1).reshape(share, width)
    dpre = (dact * slope).astype(BF16)
    dpre = lax.all_to_all(
        jnp.broadcast_to(dpre[None], (n_row, share, width)), "row", 0, 0, axis_index_groups=row_groups
    )
    flops = 2 * n_tok * features * width
    return in_vmem(
        final_kernel, 1, (features, width), (place, mine, other, dpre), flops,
        scratch=[pltpu.VMEM((n_tok, width), BF16)],
    )


def solution(mesh):
    in_specs = (
        P("vis", "row"),
        P(),
        P("row", ("col", "vis")),
        P("col", ("row", "vis")),
        P("col", ("row", "vis")),
        P("vis", "row"),
    )
    out_specs = P("row", ("col", "vis"))
    return jax.shard_map(shards, mesh=mesh, in_specs=in_specs, out_specs=out_specs, check_vma=False)
```

time: 227 us -> 222 us (0.978)
  waiting for transfers between devices: 48.5 us -> 44.5 us
  blocking collectives: 70 us -> 67.6 us
  starting transfers between devices: 72.7 us -> 75.1 us
  Pallas kernels: 18.3 us -> 20.6 us
    ppermute x4, waiting for transfers between devices: 12.8 us -> 3.85 us  [from_x(): return lax.ppermute(value, 'row', pairs)]
    all_to_all x2, waiting for transfers between devices: 5.69 us -> 14 us  [the longest x1 9.1 us: shards(): partial = lax.all_to_all(partial, 'row', 0, 0, axis_index_groups=row_groups)]
    unnamed x24 -> x34, local copies, waits for them, and re-layouts: 4.33 us -> 7.17 us
    pallas_call x1 -> x3, Pallas kernels: 4.07 us -> 6.61 us  [the longest x2 4.06 us: in_vmem(): pl.pallas_call(body, in_specs=[pl.BlockSpec(memory_space=space) for space...]
    all_to_all x2, blocking collectives: 48.2 us -> 45.7 us  [the longest x1 26.7 us: shards(): lax.all_to_all(dact.reshape(2 * spread, few, width), ('row', 'col', 'vis'...]
    ppermute x6, waiting for transfers between devices: 3.35 us -> 1.03 us  [from_core(): return lax.ppermute(value, 'col', core_pairs)]
  transfers between devices with their start and end apart: 15 -> 15, of which waited for: 7 -> 8; matrix products, arithmetic and copies ran while one was open for 2% -> 1% of each run, Pallas kernels for 2% -> 1%
where the time goes in v3:
time: 222 us; the launch traced here: 221 us
  starting transfers between devices  75.1 us (34%)
  blocking collectives  67.6 us (30%)
  waiting for transfers between devices  44.5 us (20%)
  Pallas kernels  20.6 us (9%)
  local copies, waits for them, and re-layouts  10.3 us (5%)
  other arithmetic  2.52 us (1%)
    all_to_all x1, blocking collectives, shards(): lax.all_to_all(dact.reshape(2 * spread, few, width), ('row', 'col', 'vis'...  26.7 us
    all_to_all x1, waiting for transfers between devices, shards(): sums = lax.all_to_all(both, 'col', 0, 0, axis_index_groups=quarter_groups)  25.4 us
    ppermute x6, starting transfers between devices, from_core(): return lax.ppermute(value, 'col', core_pairs)  25.4 us
    all_gather x1, blocking collectives, shards(): lax.all_gather(d_both, 'col', axis=0, axis_index_groups=quarter_groups)  21.8 us
    all_to_all x1, blocking collectives, shards(): lax.all_to_all(jnp.broadcast_to(dpre[None], (n_row, share, width)), 'row'...  19 us
    pallas_call x2, Pallas kernels, with_weights(): pl.pallas_call(kernel, in_specs=[pl.BlockSpec(memory_space=pltpu.SMEM), p...  14 us
    all_to_all x1, starting transfers between devices, shards(): sums = lax.all_to_all(both, 'col', 0, 0, axis_index_groups=quarter_groups)  13.3 us
    ppermute x4, starting transfers between devices, from_x(): return lax.ppermute(value, 'row', pairs)  12.8 us
  transfers between devices with their start and end apart: 15, of which 8 were waited for; matrix products, arithmetic and copies ran while one was open for 1% of the time, Pallas kernels for 1%

profile of v3, /device:TPU:1, one launch (start us, length us, event | category | flops | bytes accessed | tf_op | source)
XLA Modules:
  0.0 220.9 jit_solution(17342653286949949652)
XLA Ops:
  0.0 1.1 copy-done
  1.2 1.3 broadcast_in_dim.6
  2.5 5.1 %all-to-all-start = ((bf16[4,400,512]{2,1,0:T(8,128)(2,1)}), bf16[4,400,512]{2,1,0:T(8,128)(2,1)}, u32[]{:S(2)}, u32[]{:S(2)}) async-start(bf16[4,400,512]{2,1,0:T(8,128)(2,1)} %broadcast_in_dim.6), calls=%async_computation | async-start | bytes 3276800 | tf_op jit(solution)/shard_map/all_to_all | solution.py:223
  7.7 1.1 fusion.2
  8.7 4.6 %collective-permute-start.1 = (bf16[464,1024]{1,0:T(8,128)(2,1)}, bf16[464,1024]{1,0:T(8,128)(2,1)S(1)}, u32[]{:S(2)}, u32[]{:S(2)}) collective-permute-start(bf16[464,1024]{1,0:T(8,128)(2,1)} %bitcast.7.refs_0_), channel_id=1, source_target_pairs={{0,96},{32,0},{64,32},{96,64},{128,224},{160,128},{192,160},{224,1... | collective-permute-start | bytes 2850824 | tf_op jit(solution)/shard_map/ppermute | solution.py:216
  13.3 1.9 collective-permute-start.2
  15.2 7.5 %collective-permute-start.3 = (bf16[464,1024]{1,0:T(8,128)(2,1)}, bf16[464,1024]{1,0:T(8,128)(2,1)}, u32[]{:S(2)}, u32[]{:S(2)}) collective-permute-start(bf16[464,1024]{1,0:T(8,128)(2,1)} %bitcast.7.refs_0_), channel_id=1, source_target_pairs={{0,4},{4,0},{8,12},{12,8},{16,20},{20,16},{24,28},{28,24},{1,5},{5... | collective-permute-start | bytes 2850824 | tf_op jit(solution)/shard_map/ppermute | solution.py:219
  22.9 1.5 shard_map.64.mine_ref
  24.5 9.2 %collective-permute-start = (bf16[400,1024]{1,0:T(8,128)(2,1)S(1)}, bf16[400,1024]{1,0:T(8,128)(2,1)}, u32[]{:S(2)}, u32[]{:S(2)}) collective-permute-start(bf16[400,1024]{1,0:T(8,128)(2,1)S(1)} %shard_map.64.mine_ref), channel_id=1, source_target_pairs={{0,4},{4,0},{8,12},{12,8},{16,20},{20,16},{24,28},{28,24},{1,5},{5... | collective-permute-start | bytes 2457608 | tf_op jit(solution)/shard_map/ppermute | solution.py:219
  33.8 1.8 collective-permute-done.2.left_hbm.refs_2_
  35.8 1.2 copy-done.4
  36.9 2.6 %shard_map.65 = (bf16[16,64,256]{2,1,0:T(8,128)(2,1)S(1)}, bf16[240,1024]{1,0:T(8,128)(2,1)S(1)}, bf16[224,1024]{1,0:T(8,128)(2,1)S(1)}) custom-call(s32[2]{0:T(128)S(1)} %pad_add_fusion.place_ref, bf16[400,1024]{1,0:T(8,128)(2,1)S(1)} %shard_map.64.mine_ref, bf16[400,1024]{1,0:T(8,128)(2,1)} %collective-permute-done.other_ref, ...), custom_call_target="tpu_custom_call" | custom-call | flops 419430400 | bytes 2998272 | tf_op jit(solution)/shard_map/pallas_call | solution.py:79
  41.9 8.3 %all-to-all-start.1 = ((bf16[16,64,256]{2,1,0:T(8,128)(2,1)}), bf16[16,64,256]{2,1,0:T(8,128)(2,1)}, u32[]{:S(2)}, u32[]{:S(2)}) async-start(bf16[16,64,256]{2,1,0:T(8,128)(2,1)} %copy-done.3), calls=%async_computation.1 | async-start | bytes 1048576 | tf_op jit(solution)/shard_map/all_to_all | solution.py:240
  50.2 4.4 %collective-permute-start.5 = (bf16[240,1024]{1,0:T(8,128)(2,1)}, bf16[240,1024]{1,0:T(8,128)(2,1)}, u32[]{:S(2)}, u32[]{:S(2)}) collective-permute-start(bf16[240,1024]{1,0:T(8,128)(2,1)} %copy-done.8), channel_id=1, source_target_pairs={{0,96},{32,0},{64,32},{96,64},{128,224},{160,128},{192,160},{224,1... | collective-permute-start | bytes 1474568 | tf_op jit(solution)/shard_map/ppermute | solution.py:216
  54.6 1.9 collective-permute-start.6
  56.5 9.1 %all-to-all-done.1 = bf16[16,64,256]{2,1,0:T(8,128)(2,1)} async-done(((bf16[16,64,256]{2,1,0:T(8,128)(2,1)}), bf16[16,64,256]{2,1,0:T(8,128)(2,1)}, u32[]{:S(2)}, u32[]{:S(2)}) %all-to-all-start.1) | async-done | bytes 524320 | tf_op jit(solution)/shard_map/all_to_all | solution.py:240
  65.6 1.1 convert_reduce_fusion.1
  67.4 2.0 collective-permute-done.6.refs_4_
  70.3 9.6 %all-to-all-start.2 = ((bf16[32,32,256]{2,1,0:T(8,128)(2,1)}), bf16[32,32,256]{2,1,0:T(8,128)(2,1)}, u32[]{:S(2)}, u32[]{:S(2)}) async-start(bf16[32,32,256]{2,1,0:T(8,128)(2,1)} %bitcast.24), calls=%async_computation.2 | async-start | bytes 1048576 | tf_op jit(solution)/shard_map/all_to_all | solution.py:249
  79.9 2.2 %collective-permute-start.7 = (bf16[464,1024]{1,0:T(8,128)(2,1)S(1)}, bf16[464,1024]{1,0:T(8,128)(2,1)S(1)}, u32[]{:S(2)}, u32[]{:S(2)}) collective-permute-start(bf16[464,1024]{1,0:T(8,128)(2,1)S(1)} %collective-permute-done.1.right_hbm.refs_1_), channel_id=1, source_target_pairs={{0,4},{4,0},{8,12},{12,8},{16,20},{20,16},{24,28},{28,24},{1,5},{5... | collective-permute-start | bytes 2850824 | tf_op jit(solution)/shard_map/ppermute | solution.py:219
  82.2 2.1 collective-permute-start.8
  84.3 2.2 %collective-permute-start.9 = (bf16[240,1024]{1,0:T(8,128)(2,1)}, bf16[240,1024]{1,0:T(8,128)(2,1)}, u32[]{:S(2)}, u32[]{:S(2)}) collective-permute-start(bf16[240,1024]{1,0:T(8,128)(2,1)} %collective-permute-done.5.refs_3_), channel_id=1, source_target_pairs={{0,4},{4,0},{8,12},{12,8},{16,20},{20,16},{24,28},{28,24},{1,5},{5... | collective-permute-start | bytes 1474568 | tf_op jit(solution)/shard_map/ppermute | solution.py:219
  86.5 2.1 collective-permute-start.10
  91.3 4.9 %all-to-all-done.2 = bf16[32,32,256]{2,1,0:T(8,128)(2,1)} async-done(((bf16[32,32,256]{2,1,0:T(8,128)(2,1)}), bf16[32,32,256]{2,1,0:T(8,128)(2,1)}, u32[]{:S(2)}, u32[]{:S(2)}) %all-to-all-start.2) | async-done | bytes 524320 | tf_op jit(solution)/shard_map/all_to_all | solution.py:249
  96.2 8.0 %shard_map.66 = bf16[4,464,128]{2,1,0:T(8,128)(2,1)} custom-call(s32[2]{0:T(128)} %copy-done.5, bf16[2,4,4,32,256]{4,3,2,1,0:T(8,128)(2,1)} %bitcast.11.operand_ref, bf16[464,1024]{1,0:T(8,128)(2,1)} %bitcast.7.refs_0_, bf16[464,1024]{1,0:T(8,128)(2,1)} %copy-done.1, bf16[464,1024]{1,0:T(8,128)(2,1)} %copy-done.2, ...), custom_call_target="tpu_custom_call" | custom-call | flops 973078528 | bytes 8126464 | tf_op jit(solution)/shard_map/pallas_call | solution.py:174
  104.3 13.3 %all-to-all-start.3 = ((bf16[4,464,128]{2,1,0:T(8,128)(2,1)}), bf16[4,464,128]{2,1,0:T(8,128)(2,1)S(1)}, u32[]{:S(2)}, u32[]{:S(2)}) async-start(bf16[4,464,128]{2,1,0:T(8,128)(2,1)} %shard_map.66), calls=%async_computation.3 | async-start | bytes 950272 | tf_op jit(solution)/shard_map/all_to_all | solution.py:275
  119.1 25.4 %all-to-all-done.3 = bf16[4,464,128]{2,1,0:T(8,128)(2,1)S(1)} async-done(((bf16[4,464,128]{2,1,0:T(8,128)(2,1)}), bf16[4,464,128]{2,1,0:T(8,128)(2,1)S(1)}, u32[]{:S(2)}, u32[]{:S(2)}) %all-to-all-start.3) | async-done | bytes 475168 | tf_op jit(solution)/shard_map/all_to_all | solution.py:275
  144.7 21.8 %all-gather = bf16[1856,128]{1,0:T(8,128)(2,1)} all-gather(bf16[464,128]{1,0:T(8,128)(2,1)S(1)} %pad_maximum_fusion), channel_id=2, replica_groups={{0,8,16,24},{4,12,20,28},{1,9,17,25},{5,13,21,29},{2,10,18,26},{6,14,22..., dimensions={0}, use_global_device_ids=true | all-gather | bytes 593920 | tf_op jit(solution)/shard_map/all_gather | solution.py:282
  166.5 5.9 %shard_map.67 = bf16[2,4,4,32,256]{4,3,2,1,0:T(8,128)(2,1)} custom-call(s32[2]{0:T(128)} %copy-done.5, bf16[4,464,128]{2,1,0:T(8,128)(2,1)} %bitcast.25, bf16[464,1024]{1,0:T(8,128)(2,1)} %bitcast.7.refs_0_, bf16[464,1024]{1,0:T(8,128)(2,1)} %copy-done.1, bf16[464,1024]{1,0:T(8,128)(2,1)} %copy-done.2, bf16[240,1024]{1,0:T(8,128)(2,1)} %collective-permute-done.5.refs_3_, ...), custom_call_target="tpu_custom_call" | custom-call | flops 973078528 | bytes 8077312 | tf_op jit(solution)/shard_map/pallas_call | solution.py:174
  172.5 26.7 %all_to_all.30 = bf16[32,32,256]{2,1,0:T(8,128)(2,1)S(1)} all-to-all(bf16[32,32,256]{2,1,0:T(8,128)(2,1)} %bitcast.23), channel_id=1, replica_groups={{0,1,2,3,128,129,130,131,256,257,258,259,384,385,386,387,4,5,6,7,132,13..., dimensions={0} | all-to-all | bytes 1048576 | tf_op jit(solution)/shard_map/all_to_all | solution.py:286
  199.3 19.0 %all_to_all.31.dpre_ref = bf16[16,64,256]{2,1,0:T(8,128)(2,1)S(1)} all-to-all(bf16[16,64,256]{2,1,0:T(8,128)(2,1)S(1)} %broadcast_in_dim.8), channel_id=1, replica_groups={{0,128,256,384,32,160,288,416,64,192,320,448,96,224,352,480},{1,129,257..., dimensions={0} | all-to-all | bytes 1048576 | tf_op jit(solution)/shard_map/all_to_all | solution.py:291
  218.4 2.5 %shard_map.68 = bf16[800,256]{1,0:T(8,128)(2,1)} custom-call(s32[2]{0:T(128)S(1)} %copy-done.6, bf16[400,1024]{1,0:T(8,128)(2,1)S(1)} %shard_map.64.mine_ref, bf16[400,1024]{1,0:T(8,128)(2,1)} %collective-permute-done.other_ref, bf16[16,64,256]{2,1,0:T(8,128)(2,1)S(1)} %all_to_all.31.dpre_ref), custom_call_target="tpu_custom_call" | custom-call | flops 419430400 | bytes 2162688 | tf_op jit(solution)/shard_map/pallas_call | solution.py:31
  (54 shorter events, 9.0 us)
Async XLA Ops:
  0.0 1.1 copy-start
  2.5 5.2 %copy-start.15 = (bf16[1024,231]{0,1:T(8,128)(2,1)S(1)}, bf16[1024,231]{0,1:T(8,128)(2,1)}, u32[]{:S(2)}) copy-start(bf16[1024,231]{0,1:T(8,128)(2,1)} %param.10) | copy-start | bytes 1419268
  2.5 5.2 %copy-start.16 = (bf16[1024,231]{0,1:T(8,128)(2,1)S(1)}, bf16[1024,231]{0,1:T(8,128)(2,1)}, u32[]{:S(2)}) copy-start(bf16[1024,231]{0,1:T(8,128)(2,1)} %param.9) | copy-start | bytes 1419268
  2.5 20.4 %all-to-all-start = ((bf16[4,400,512]{2,1,0:T(8,128)(2,1)}), bf16[4,400,512]{2,1,0:T(8,128)(2,1)}, u32[]{:S(2)}, u32[]{:S(2)}) async-start(bf16[4,400,512]{2,1,0:T(8,128)(2,1)} %broadcast_in_dim.6), calls=%async_computation | async-start | bytes 3276800 | tf_op jit(solution)/shard_map/all_to_all | solution.py:223
  7.7 15.3 %copy-start.7 = (s32[4]{0:T(128)S(1)}, s32[4]{0:T(128)}, u32[]{:S(2)}) copy-start(s32[4]{0:T(128)} %slot_ref.1) | copy-start | bytes 52
  8.7 25.1 %collective-permute-start.1 = (bf16[464,1024]{1,0:T(8,128)(2,1)}, bf16[464,1024]{1,0:T(8,128)(2,1)S(1)}, u32[]{:S(2)}, u32[]{:S(2)}) collective-permute-start(bf16[464,1024]{1,0:T(8,128)(2,1)} %bitcast.7.refs_0_), channel_id=1, source_target_pairs={{0,96},{32,0},{64,32},{96,64},{128,224},{160,128},{192,160},{224,1... | collective-permute-start | bytes 2850824 | tf_op jit(solution)/shard_map/ppermute | solution.py:216
  13.3 22.3 %collective-permute-start.2 = (bf16[464,1024]{1,0:T(8,128)(2,1)}, bf16[464,1024]{1,0:T(8,128)(2,1)S(1)}, u32[]{:S(2)}, u32[]{:S(2)}) collective-permute-start(bf16[464,1024]{1,0:T(8,128)(2,1)} %bitcast.7.refs_0_), channel_id=1, source_target_pairs={{0,32},{32,64},{64,96},{96,0},{128,160},{160,192},{192,224},{224,1... | collective-permute-start | bytes 2850824 | tf_op jit(solution)/shard_map/ppermute | solution.py:216
  15.2 20.4 %collective-permute-start.3 = (bf16[464,1024]{1,0:T(8,128)(2,1)}, bf16[464,1024]{1,0:T(8,128)(2,1)}, u32[]{:S(2)}, u32[]{:S(2)}) collective-permute-start(bf16[464,1024]{1,0:T(8,128)(2,1)} %bitcast.7.refs_0_), channel_id=1, source_target_pairs={{0,4},{4,0},{8,12},{12,8},{16,20},{20,16},{24,28},{28,24},{1,5},{5... | collective-permute-start | bytes 2850824 | tf_op jit(solution)/shard_map/ppermute | solution.py:219
  24.5 11.3 %collective-permute-start = (bf16[400,1024]{1,0:T(8,128)(2,1)S(1)}, bf16[400,1024]{1,0:T(8,128)(2,1)}, u32[]{:S(2)}, u32[]{:S(2)}) collective-permute-start(bf16[400,1024]{1,0:T(8,128)(2,1)S(1)} %shard_map.64.mine_ref), channel_id=1, source_target_pairs={{0,4},{4,0},{8,12},{12,8},{16,20},{20,16},{24,28},{28,24},{1,5},{5... | collective-permute-start | bytes 2457608 | tf_op jit(solution)/shard_map/ppermute | solution.py:219
  33.8 5.7 %copy-start.5 = (s32[2]{0:T(128)}, s32[2]{0:T(128)S(1)}, u32[]{:S(2)}) copy-start(s32[2]{0:T(128)S(1)} %pad_add_fusion.place_ref) | copy-start | bytes 28
  33.8 46.2 %copy-start.1 = (bf16[464,1024]{1,0:T(8,128)(2,1)}, bf16[464,1024]{1,0:T(8,128)(2,1)S(1)}, u32[]{:S(2)}) copy-start(bf16[464,1024]{1,0:T(8,128)(2,1)S(1)} %collective-permute-done.1.right_hbm.refs_1_) | copy-start | bytes 2850820
  35.6 46.6 %copy-start.2 = (bf16[464,1024]{1,0:T(8,128)(2,1)}, bf16[464,1024]{1,0:T(8,128)(2,1)S(1)}, u32[]{:S(2)}) copy-start(bf16[464,1024]{1,0:T(8,128)(2,1)S(1)} %collective-permute-done.2.left_hbm.refs_2_) | copy-start | bytes 2850820
  35.8 1.2 copy-start.4
  39.5 0.8 copy-start.3
  40.3 0.8 copy-start.8
  41.1 0.8 copy-start.9
  41.9 23.8 %all-to-all-start.1 = ((bf16[16,64,256]{2,1,0:T(8,128)(2,1)}), bf16[16,64,256]{2,1,0:T(8,128)(2,1)}, u32[]{:S(2)}, u32[]{:S(2)}) async-start(bf16[16,64,256]{2,1,0:T(8,128)(2,1)} %copy-done.3), calls=%async_computation.1 | async-start | bytes 1048576 | tf_op jit(solution)/shard_map/all_to_all | solution.py:240
  50.2 19.3 %collective-permute-start.5 = (bf16[240,1024]{1,0:T(8,128)(2,1)}, bf16[240,1024]{1,0:T(8,128)(2,1)}, u32[]{:S(2)}, u32[]{:S(2)}) collective-permute-start(bf16[240,1024]{1,0:T(8,128)(2,1)} %copy-done.8), channel_id=1, source_target_pairs={{0,96},{32,0},{64,32},{96,64},{128,224},{160,128},{192,160},{224,1... | collective-permute-start | bytes 1474568 | tf_op jit(solution)/shard_map/ppermute | solution.py:216
  54.6 14.9 %collective-permute-start.6 = (bf16[224,1024]{1,0:T(8,128)(2,1)}, bf16[224,1024]{1,0:T(8,128)(2,1)}, u32[]{:S(2)}, u32[]{:S(2)}) collective-permute-start(bf16[224,1024]{1,0:T(8,128)(2,1)} %copy-done.9), channel_id=1, source_target_pairs={{0,32},{32,64},{64,96},{96,0},{128,160},{160,192},{192,224},{224,1... | collective-permute-start | bytes 1376264 | tf_op jit(solution)/shard_map/ppermute | solution.py:216
  66.7 0.6 copy-start.13
  70.3 25.9 %all-to-all-start.2 = ((bf16[32,32,256]{2,1,0:T(8,128)(2,1)}), bf16[32,32,256]{2,1,0:T(8,128)(2,1)}, u32[]{:S(2)}, u32[]{:S(2)}) async-start(bf16[32,32,256]{2,1,0:T(8,128)(2,1)} %bitcast.24), calls=%async_computation.2 | async-start | bytes 1048576 | tf_op jit(solution)/shard_map/all_to_all | solution.py:249
  79.9 8.7 %collective-permute-start.7 = (bf16[464,1024]{1,0:T(8,128)(2,1)S(1)}, bf16[464,1024]{1,0:T(8,128)(2,1)S(1)}, u32[]{:S(2)}, u32[]{:S(2)}) collective-permute-start(bf16[464,1024]{1,0:T(8,128)(2,1)S(1)} %collective-permute-done.1.right_hbm.refs_1_), channel_id=1, source_target_pairs={{0,4},{4,0},{8,12},{12,8},{16,20},{20,16},{24,28},{28,24},{1,5},{5... | collective-permute-start | bytes 2850824 | tf_op jit(solution)/shard_map/ppermute | solution.py:219
  82.2 6.5 %collective-permute-start.8 = (bf16[464,1024]{1,0:T(8,128)(2,1)S(1)}, bf16[464,1024]{1,0:T(8,128)(2,1)S(1)}, u32[]{:S(2)}, u32[]{:S(2)}) collective-permute-start(bf16[464,1024]{1,0:T(8,128)(2,1)S(1)} %collective-permute-done.2.left_hbm.refs_2_), channel_id=1, source_target_pairs={{0,4},{4,0},{8,12},{12,8},{16,20},{20,16},{24,28},{28,24},{1,5},{5... | collective-permute-start | bytes 2850824 | tf_op jit(solution)/shard_map/ppermute | solution.py:219
  84.3 7.1 %collective-permute-start.9 = (bf16[240,1024]{1,0:T(8,128)(2,1)}, bf16[240,1024]{1,0:T(8,128)(2,1)}, u32[]{:S(2)}, u32[]{:S(2)}) collective-permute-start(bf16[240,1024]{1,0:T(8,128)(2,1)} %collective-permute-done.5.refs_3_), channel_id=1, source_target_pairs={{0,4},{4,0},{8,12},{12,8},{16,20},{20,16},{24,28},{28,24},{1,5},{5... | collective-permute-start | bytes 1474568 | tf_op jit(solution)/shard_map/ppermute | solution.py:219
  86.5 3.9 %collective-permute-start.10 = (bf16[224,1024]{1,0:T(8,128)(2,1)}, bf16[224,1024]{1,0:T(8,128)(2,1)S(1)}, u32[]{:S(2)}, u32[]{:S(2)}) collective-permute-start(bf16[224,1024]{1,0:T(8,128)(2,1)} %collective-permute-done.6.refs_4_), channel_id=1, source_target_pairs={{0,4},{4,0},{8,12},{12,8},{16,20},{20,16},{24,28},{28,24},{1,5},{5... | collective-permute-start | bytes 1376264 | tf_op jit(solution)/shard_map/ppermute | solution.py:219
  88.6 0.9 copy-start.10
  89.6 0.9 copy-start.11
  90.5 0.8 copy-start.12
  104.3 40.2 %all-to-all-start.3 = ((bf16[4,464,128]{2,1,0:T(8,128)(2,1)}), bf16[4,464,128]{2,1,0:T(8,128)(2,1)S(1)}, u32[]{:S(2)}, u32[]{:S(2)}) async-start(bf16[4,464,128]{2,1,0:T(8,128)(2,1)} %shard_map.66), calls=%async_computation.3 | async-start | bytes 950272 | tf_op jit(solution)/shard_map/all_to_all | solution.py:275
  118.5 26.1 %collective-permute-start.4 = (bf16[231,128]{1,0:T(8,128)(2,1)S(1)}, bf16[231,128]{1,0:T(8,128)(2,1)S(1)}, u32[]{:S(2)}, u32[]{:S(2)}) collective-permute-start(bf16[231,128]{1,0:T(8,128)(2,1)S(1)} %dynamic-slice_bitcast_fusion.1), channel_id=1, source_target_pairs={{0,0},{4,4},{40,8},{44,12},{112,16},{116,20},{88,24},{92,28},{32,1... | collective-permute-start | bytes 177416 | tf_op jit(solution)/shard_map/ppermute | solution.py:269
  172.5 26.8 %copy-start.14 = (f32[64,256]{1,0:T(8,128)S(1)}, f32[64,256]{1,0:T(8,128)}, u32[]{:S(2)}) copy-start(f32[64,256]{1,0:T(8,128)} %copy-done.13) | copy-start | bytes 196612
  172.5 45.9 %copy-start.6 = (s32[2]{0:T(128)S(1)}, s32[2]{0:T(128)}, u32[]{:S(2)}) copy-start(s32[2]{0:T(128)} %copy-done.5) | copy-start | bytes 28

commit v4 on v3

--- a/solution.py
+++ b/solution.py
@@ -47,12 +47,7 @@
         out_ref[:, t * TILE : (t + 1) * TILE] = arrived_ref[lax.div(slot, per_group), :, pl.ds(lanes, TILE)]
 
 
-def proj_kernel(place_ref, mine_ref, other_ref, weight_ref, right_hbm, left_hbm, out_ref, low_ref, high_ref, sems):
-    first = low_ref.shape[0]
-    low_copy = pltpu.make_async_copy(right_hbm.at[pl.ds(0, first)], low_ref, sems.at[0])
-    high_copy = pltpu.make_async_copy(left_hbm.at[pl.ds(first, high_ref.shape[0])], high_ref, sems.at[1])
-    low_copy.start()
-    high_copy.start()
+def proj_kernel(place_ref, mine_ref, other_ref, weight_ref, out_ref):
     half = mine_ref.shape[0]
     core = place_ref[0]
     w_mine = weight_ref[pl.ds(pl.multiple_of(core * half, 16), half), :]
@@ -67,28 +62,6 @@
             for low in range(lows):
                 at = (k * lows + low) * few
                 out_ref[t * lows + low, k * few : (k + 1) * few, :] = total[at : at + few]
-    low_copy.wait()
-    high_copy.wait()
-
-
-def project(place, mine, other, weight, right, left, out_shape, flops):
-    rows, model = right.shape
-    first = -(rows // -32) * 16
-    hbm, vmem = pl.BlockSpec(memory_space=pltpu.HBM), pl.BlockSpec(memory_space=pltpu.VMEM)
-    moved = 2 * (mine.size + other.size + weight.size + right.size)
-    return pl.pallas_call(
-        proj_kernel,
-        in_specs=[pl.BlockSpec(memory_space=pltpu.SMEM), vmem, vmem, vmem, hbm, hbm],
-        out_specs=(vmem,) * 3,
-        out_shape=(
-            jax.ShapeDtypeStruct(out_shape, BF16),
-            jax.ShapeDtypeStruct((first, model), BF16),
-            jax.ShapeDtypeStruct((rows - first, model), BF16),
-        ),
-        scratch_shapes=[pltpu.SemaphoreType.DMA((2,))],
-        compiler_params=pltpu.CompilerParams(vmem_limit_bytes=SMALL_VMEM),
-        cost_estimate=pl.CostEstimate(flops=flops, bytes_accessed=moved, transcendentals=0),
-    )(place, mine, other, weight, right, left)
 
 
 def final_kernel(place_ref, mine_ref, other_ref, dpre_ref, out_ref, ordered_ref):
@@ -164,7 +137,7 @@
     return [pltpu.make_async_copy(w, b, sems.at[i]) for i, (w, b) in enumerate(zip(weights, held))]
 
 
-def with_weights(body, place, operand, weights, out_shape, flops, turned):
+def with_weights(body, place, operand, weights, out_shape, flops, turned, limit):
     n = len(weights)
 
     def kernel(place_ref, operand_ref, *refs):
@@ -179,7 +152,7 @@
         out_shape=jax.ShapeDtypeStruct(out_shape, BF16),
         scratch_shapes=[pltpu.VMEM(w.shape, BF16) for w in weights]
         + [pltpu.SemaphoreType.DMA((n,)), pltpu.VMEM(turned, BF16)],
-        compiler_params=pltpu.CompilerParams(vmem_limit_bytes=KERNEL_VMEM),
+        compiler_params=pltpu.CompilerParams(vmem_limit_bytes=limit),
         cost_estimate=pl.CostEstimate(flops=flops, bytes_accessed=2 * moved, transcendentals=0),
     )(place, operand, *weights)
 
@@ -228,15 +201,15 @@
     right, left, weights_o = from_x(weights, 1), from_x(weights, -1), from_core(weights)
     mine = in_vmem(pick_kernel, 1, (half, n_x * TILE), (tile_slot, arrived), 0)
     other = from_core(mine)
-    other, right, left, weights_o = lax.optimization_barrier((other, right, left, weights_o))
 
     n_tok, width = n_x * TILE, proj_weight.shape[1]
     share, lane, model = n_tok // n_row, TILE // 2, n_vis * width
     few = share // 2
     flops = 2 * n_tok * features * width
-    partial, far_low, far_high = project(
-        place, mine, other, proj_weight, right, left, (n_row, share, width), flops
-    )
+    partial = in_vmem(proj_kernel, 1, (n_row, share, width), (place, mine, other, proj_weight), flops)
+    partial, right, left, weights_o = lax.optimization_barrier((partial, right, left, weights_o))
+    first = -((unit + pad) // -16) * 16
+    far_low, far_high = right[:first], left[first:]
     partial = lax.all_to_all(partial, "row", 0, 0, axis_index_groups=row_groups)
     far_low, far_high = from_x(far_low, 1), from_x(far_high, -1)
     preact = jnp.sum(partial.astype(F32), axis=0)
@@ -271,7 +244,7 @@
 
     rows = 2 * (unit + pad)
     flops = 4 * lane * n_x * rows * model
-    both = with_weights(gate_body, place, hidden, pieces, (n_x, rows, lane), flops, (2 * model, lane))
+    both = with_weights(gate_body, place, hidden, pieces, (n_x, rows, lane), flops, (2 * model, lane), KERNEL_VMEM)
     sums = lax.all_to_all(both, "col", 0, 0, axis_index_groups=quarter_groups)
     sums = jnp.sum(sums.astype(F32), axis=0)
     gate_sum, up_sum = sums[: unit + pad], sums[unit + pad :]
@@ -282,7 +255,7 @@
     d_all = lax.all_gather(d_both, "col", axis=0, axis_index_groups=quarter_groups)
 
     shape = (2, n_low, n_vis, few, width)
-    dact = with_weights(dact_body, place, d_all, pieces, shape, flops, (16, lane))
+    dact = with_weights(dact_body, place, d_all, pieces, shape, flops, (16, lane), SMALL_VMEM)
     dact = lax.all_to_all(
         dact.reshape(2 * spread, few, width), ("row", "col", "vis"), 0, 0, axis_index_groups=column_groups
     )

time: 222 us -> 218 us (0.982)
  Pallas kernels: 20.6 us -> 16 us
  starting transfers between devices: 75.1 us -> 71.6 us
  local copies, waits for them, and re-layouts: 10.3 us -> 13.7 us
  blocking collectives: 67.6 us -> 64.6 us
    ppermute x6, waiting for transfers between devices: 1.03 us -> 3.76 us  [from_core(): return lax.ppermute(value, 'col', core_pairs)]
    pallas_call x1 -> x0, Pallas kernels: 2.55 us -> none  [project(): pl.pallas_call(proj_kernel, in_specs=[pl.BlockSpec(memory_space=pltpu.SME...]
    all_to_all x1, starting transfers between devices: 9.6 us -> 7.27 us  [shards(): lax.all_to_all(hidden.reshape(2 * spread, few, width), ('row', 'col', 'vi...]
    unnamed x34 -> x44, local copies, waits for them, and re-layouts: 7.17 us -> 7.69 us
  transfers between devices with their start and end apart: 15 -> 15, of which waited for: 8 -> 7; matrix products, arithmetic and copies ran while one was open for 1% -> 3% of each run, Pallas kernels for 1% -> 1%
where the time goes in v4:
time: 218 us; the launch traced here: 217 us
  starting transfers between devices  71.6 us (33%)
  blocking collectives  64.6 us (30%)
  waiting for transfers between devices  45.6 us (21%)
  Pallas kernels  16 us (7%)
  local copies, waits for them, and re-layouts  13.7 us (6%)
  other arithmetic  4.69 us (2%)
    all_to_all x1, blocking collectives, shards(): lax.all_to_all(dact.reshape(2 * spread, few, width), ('row', 'col', 'vis'...  24.6 us
    ppermute x6, starting transfers between devices, from_core(): return lax.ppermute(value, 'col', core_pairs)  24.1 us
    all_to_all x1, waiting for transfers between devices, shards(): sums = lax.all_to_all(both, 'col', 0, 0, axis_index_groups=quarter_groups)  23.5 us
    all_gather x1, blocking collectives, shards(): lax.all_gather(d_both, 'col', axis=0, axis_index_groups=quarter_groups)  21.6 us
    all_to_all x1, blocking collectives, shards(): lax.all_to_all(jnp.broadcast_to(dpre[None], (n_row, share, width)), 'row'...  18.4 us
    ppermute x4, starting transfers between devices, from_x(): return lax.ppermute(value, 'row', pairs)  12.7 us
    all_to_all x1, starting transfers between devices, shards(): sums = lax.all_to_all(both, 'col', 0, 0, axis_index_groups=quarter_groups)  12.3 us
    pallas_call x2, Pallas kernels, with_weights(): pl.pallas_call(kernel, in_specs=[pl.BlockSpec(memory_space=pltpu.SMEM), p...  12.2 us
  transfers between devices with their start and end apart: 15, of which 7 were waited for; matrix products, arithmetic and copies ran while one was open for 3% of the time, Pallas kernels for 1%

profile of v4, /device:TPU:1, one launch (start us, length us, event | category | flops | bytes accessed | tf_op | source)
XLA Modules:
  0.0 216.7 jit_solution(17820790808259316374)
XLA Ops:
  1.2 1.4 broadcast_in_dim.6
  2.5 5.0 %all-to-all-start = ((bf16[4,400,512]{2,1,0:T(8,128)(2,1)}), bf16[4,400,512]{2,1,0:T(8,128)(2,1)S(1)}, u32[]{:S(2)}, u32[]{:S(2)}) async-start(bf16[4,400,512]{2,1,0:T(8,128)(2,1)} %broadcast_in_dim.6), calls=%async_computation | async-start | bytes 3276800 | tf_op jit(solution)/shard_map/all_to_all | solution.py:196
  7.6 1.3 fusion.2
  8.8 4.4 %collective-permute-start.2 = (bf16[464,1024]{1,0:T(8,128)(2,1)S(1)}, bf16[464,1024]{1,0:T(8,128)(2,1)}, u32[]{:S(2)}, u32[]{:S(2)}) collective-permute-start(bf16[464,1024]{1,0:T(8,128)(2,1)S(1)} %bitcast.23), channel_id=1, source_target_pairs={{0,96},{32,0},{64,32},{96,64},{128,224},{160,128},{192,160},{224,1... | collective-permute-start | bytes 2850824 | tf_op jit(solution)/shard_map/ppermute | solution.py:189
  13.2 1.9 collective-permute-start.3
  15.2 6.9 %collective-permute-start.4 = (bf16[464,1024]{1,0:T(8,128)(2,1)S(1)}, bf16[464,1024]{1,0:T(8,128)(2,1)}, u32[]{:S(2)}, u32[]{:S(2)}) collective-permute-start(bf16[464,1024]{1,0:T(8,128)(2,1)S(1)} %bitcast.25), channel_id=1, source_target_pairs={{0,4},{4,0},{8,12},{12,8},{16,20},{20,16},{24,28},{28,24},{1,5},{5... | collective-permute-start | bytes 2850824 | tf_op jit(solution)/shard_map/ppermute | solution.py:192
  24.5 1.4 copy-done.4
  26.6 8.5 %collective-permute-start = (bf16[400,1024]{1,0:T(8,128)(2,1)S(1)}, bf16[400,1024]{1,0:T(8,128)(2,1)S(1)}, u32[]{:S(2)}, u32[]{:S(2)}) collective-permute-start(bf16[400,1024]{1,0:T(8,128)(2,1)S(1)} %shard_map.64.mine_ref), channel_id=1, source_target_pairs={{0,4},{4,0},{8,12},{12,8},{16,20},{20,16},{24,28},{28,24},{1,5},{5... | collective-permute-start | bytes 2457608 | tf_op jit(solution)/shard_map/ppermute | solution.py:192
  35.2 1.9 collective-permute-done.other_ref
  38.1 1.3 shard_map.65
  40.2 8.2 %all-to-all-start.1 = ((bf16[16,64,256]{2,1,0:T(8,128)(2,1)}), bf16[16,64,256]{2,1,0:T(8,128)(2,1)}, u32[]{:S(2)}, u32[]{:S(2)}) async-start(bf16[16,64,256]{2,1,0:T(8,128)(2,1)} %copy-done.11), calls=%async_computation.1 | async-start | bytes 1048576 | tf_op jit(solution)/shard_map/all_to_all | solution.py:213
  49.6 4.4 %collective-permute-start.5 = (bf16[240,1024]{1,0:T(8,128)(2,1)S(1)}, bf16[240,1024]{1,0:T(8,128)(2,1)S(1)}, u32[]{:S(2)}, u32[]{:S(2)}) collective-permute-start(bf16[240,1024]{1,0:T(8,128)(2,1)S(1)} %slice.12), channel_id=1, source_target_pairs={{0,96},{32,0},{64,32},{96,64},{128,224},{160,128},{192,160},{224,1... | collective-permute-start | bytes 1474568 | tf_op jit(solution)/shard_map/ppermute | solution.py:189
  55.1 1.9 collective-permute-start.6
  57.0 7.3 %all-to-all-done.1 = bf16[16,64,256]{2,1,0:T(8,128)(2,1)} async-done(((bf16[16,64,256]{2,1,0:T(8,128)(2,1)}), bf16[16,64,256]{2,1,0:T(8,128)(2,1)}, u32[]{:S(2)}, u32[]{:S(2)}) %all-to-all-start.1) | async-done | bytes 524320 | tf_op jit(solution)/shard_map/all_to_all | solution.py:213
  65.5 4.2 %collective-permute-done.6.refs_4_ = bf16[224,1024]{1,0:T(8,128)(2,1)S(1)} collective-permute-done((bf16[224,1024]{1,0:T(8,128)(2,1)S(1)}, bf16[224,1024]{1,0:T(8,128)(2,1)S(1)}, u32[]{:S(2)}, u32[]{:S(2)}) %collective-permute-start.6) | collective-permute-done | bytes 458784 | tf_op jit(solution)/shard_map/ppermute | solution.py:189
  70.6 7.3 %all-to-all-start.2 = ((bf16[32,32,256]{2,1,0:T(8,128)(2,1)}), bf16[32,32,256]{2,1,0:T(8,128)(2,1)}, u32[]{:S(2)}, u32[]{:S(2)}) async-start(bf16[32,32,256]{2,1,0:T(8,128)(2,1)} %bitcast.10), calls=%async_computation.2 | async-start | bytes 1048576 | tf_op jit(solution)/shard_map/all_to_all | solution.py:222
  77.9 2.2 %collective-permute-start.7 = (bf16[464,1024]{1,0:T(8,128)(2,1)}, bf16[464,1024]{1,0:T(8,128)(2,1)S(1)}, u32[]{:S(2)}, u32[]{:S(2)}) collective-permute-start(bf16[464,1024]{1,0:T(8,128)(2,1)} %collective-permute-done.2.refs_1_), channel_id=1, source_target_pairs={{0,4},{4,0},{8,12},{12,8},{16,20},{20,16},{24,28},{28,24},{1,5},{5... | collective-permute-start | bytes 2850824 | tf_op jit(solution)/shard_map/ppermute | solution.py:192
  80.1 2.1 collective-permute-start.8
  82.3 2.2 %collective-permute-start.9 = (bf16[240,1024]{1,0:T(8,128)(2,1)}, bf16[240,1024]{1,0:T(8,128)(2,1)}, u32[]{:S(2)}, u32[]{:S(2)}) collective-permute-start(bf16[240,1024]{1,0:T(8,128)(2,1)} %copy-done.12), channel_id=1, source_target_pairs={{0,4},{4,0},{8,12},{12,8},{16,20},{20,16},{24,28},{28,24},{1,5},{5... | collective-permute-start | bytes 1474568 | tf_op jit(solution)/shard_map/ppermute | solution.py:192
  84.5 2.1 collective-permute-start.10
  86.6 1.9 collective-permute-done.10.refs_9_
  88.5 5.7 %all-to-all-done.2 = bf16[32,32,256]{2,1,0:T(8,128)(2,1)} async-done(((bf16[32,32,256]{2,1,0:T(8,128)(2,1)}), bf16[32,32,256]{2,1,0:T(8,128)(2,1)}, u32[]{:S(2)}, u32[]{:S(2)}) %all-to-all-start.2) | async-done | bytes 524320 | tf_op jit(solution)/shard_map/all_to_all | solution.py:222
  94.2 8.0 %shard_map.66 = bf16[4,464,128]{2,1,0:T(8,128)(2,1)} custom-call(s32[2]{0:T(128)} %copy-done.17, bf16[2,4,4,32,256]{4,3,2,1,0:T(8,128)(2,1)} %bitcast.11.operand_ref, bf16[464,1024]{1,0:T(8,128)(2,1)} %bitcast.26, bf16[464,1024]{1,0:T(8,128)(2,1)} %collective-permute-done.2.refs_1_, bf16[464,1024]{1,0:T(8,128)(2,1)} %collective-permute-done.3.refs_2_, ...), custom_call_target="tpu_custom_call" | custom-call | flops 973078528 | bytes 8126464 | tf_op jit(solution)/shard_map/pallas_call | solution.py:147
  102.3 12.3 %all-to-all-start.3 = ((bf16[4,464,128]{2,1,0:T(8,128)(2,1)}), bf16[4,464,128]{2,1,0:T(8,128)(2,1)}, u32[]{:S(2)}, u32[]{:S(2)}) async-start(bf16[4,464,128]{2,1,0:T(8,128)(2,1)} %shard_map.66), calls=%async_computation.3 | async-start | bytes 950272 | tf_op jit(solution)/shard_map/all_to_all | solution.py:248
  114.5 1.5 dynamic-slice_bitcast_fusion.1
  116.1 2.1 collective-permute-start.1
  118.1 23.5 %all-to-all-done.3 = bf16[4,464,128]{2,1,0:T(8,128)(2,1)} async-done(((bf16[4,464,128]{2,1,0:T(8,128)(2,1)}), bf16[4,464,128]{2,1,0:T(8,128)(2,1)}, u32[]{:S(2)}, u32[]{:S(2)}) %all-to-all-start.3) | async-done | bytes 475168 | tf_op jit(solution)/shard_map/all_to_all | solution.py:248
  143.7 21.6 %all-gather = bf16[1856,128]{1,0:T(8,128)(2,1)S(1)} all-gather(bf16[464,128]{1,0:T(8,128)(2,1)S(1)} %pad_maximum_fusion), channel_id=2, replica_groups={{0,8,16,24},{4,12,20,28},{1,9,17,25},{5,13,21,29},{2,10,18,26},{6,14,22..., dimensions={0}, use_global_device_ids=true | all-gather | bytes 593920 | tf_op jit(solution)/shard_map/all_gather | solution.py:255
  167.4 4.1 %shard_map.67 = bf16[2,4,4,32,256]{4,3,2,1,0:T(8,128)(2,1)S(1)} custom-call(s32[2]{0:T(128)S(1)} %copy-done.18, bf16[4,464,128]{2,1,0:T(8,128)(2,1)S(1)} %bitcast.29, bf16[464,1024]{1,0:T(8,128)(2,1)S(1)} %bitcast.27, bf16[464,1024]{1,0:T(8,128)(2,1)} %collective-permute-done.2.refs_1_, bf16[464,1024]{1,0:T(8,128)(2,1)} %collective-permute-done.3.refs_2_, ...), custom_call_target="tpu_custom_call" | custom-call | flops 973078528 | bytes 8077312 | tf_op jit(solution)/shard_map/pallas_call | solution.py:147
  171.6 24.6 %all_to_all.30 = bf16[32,32,256]{2,1,0:T(8,128)(2,1)S(1)} all-to-all(bf16[32,32,256]{2,1,0:T(8,128)(2,1)S(1)} %bitcast.28), channel_id=1, replica_groups={{0,1,2,3,128,129,130,131,256,257,258,259,384,385,386,387,4,5,6,7,132,13..., dimensions={0} | all-to-all | bytes 1048576 | tf_op jit(solution)/shard_map/all_to_all | solution.py:259
  196.4 18.4 %all_to_all.31.dpre_ref = bf16[16,64,256]{2,1,0:T(8,128)(2,1)S(1)} all-to-all(bf16[16,64,256]{2,1,0:T(8,128)(2,1)S(1)} %broadcast_in_dim.8), channel_id=1, replica_groups={{0,128,256,384,32,160,288,416,64,192,320,448,96,224,352,480},{1,129,257..., dimensions={0} | all-to-all | bytes 1048576 | tf_op jit(solution)/shard_map/all_to_all | solution.py:264
  214.8 1.9 shard_map.68
  (66 shorter events, 14.7 us)
Async XLA Ops:
  2.5 20.8 %all-to-all-start = ((bf16[4,400,512]{2,1,0:T(8,128)(2,1)}), bf16[4,400,512]{2,1,0:T(8,128)(2,1)S(1)}, u32[]{:S(2)}, u32[]{:S(2)}) async-start(bf16[4,400,512]{2,1,0:T(8,128)(2,1)} %broadcast_in_dim.6), calls=%async_computation | async-start | bytes 3276800 | tf_op jit(solution)/shard_map/all_to_all | solution.py:196
  7.6 17.0 %copy-start.19 = (s32[4]{0:T(128)S(1)}, s32[4]{0:T(128)}, u32[]{:S(2)}) copy-start(s32[4]{0:T(128)} %slot_ref.1) | copy-start | bytes 52
  8.8 30.6 %copy-start.1 = (bf16[2,232,1024]{2,1,0:T(8,128)(2,1)}, bf16[2,232,1024]{2,1,0:T(8,128)(2,1)S(1)}, u32[]{:S(2)}) copy-start(bf16[2,232,1024]{2,1,0:T(8,128)(2,1)S(1)} %fusion.2) | copy-start | bytes 2850820
  8.8 30.6 %collective-permute-start.2 = (bf16[464,1024]{1,0:T(8,128)(2,1)S(1)}, bf16[464,1024]{1,0:T(8,128)(2,1)}, u32[]{:S(2)}, u32[]{:S(2)}) collective-permute-start(bf16[464,1024]{1,0:T(8,128)(2,1)S(1)} %bitcast.23), channel_id=1, source_target_pairs={{0,96},{32,0},{64,32},{96,64},{128,224},{160,128},{192,160},{224,1... | collective-permute-start | bytes 2850824 | tf_op jit(solution)/shard_map/ppermute | solution.py:189
  13.2 26.2 %collective-permute-start.3 = (bf16[464,1024]{1,0:T(8,128)(2,1)S(1)}, bf16[464,1024]{1,0:T(8,128)(2,1)}, u32[]{:S(2)}, u32[]{:S(2)}) collective-permute-start(bf16[464,1024]{1,0:T(8,128)(2,1)S(1)} %bitcast.24), channel_id=1, source_target_pairs={{0,32},{32,64},{64,96},{96,0},{128,160},{160,192},{192,224},{224,1... | collective-permute-start | bytes 2850824 | tf_op jit(solution)/shard_map/ppermute | solution.py:189
  15.2 25.1 %collective-permute-start.4 = (bf16[464,1024]{1,0:T(8,128)(2,1)S(1)}, bf16[464,1024]{1,0:T(8,128)(2,1)}, u32[]{:S(2)}, u32[]{:S(2)}) collective-permute-start(bf16[464,1024]{1,0:T(8,128)(2,1)S(1)} %bitcast.25), channel_id=1, source_target_pairs={{0,4},{4,0},{8,12},{12,8},{16,20},{20,16},{24,28},{28,24},{1,5},{5... | collective-permute-start | bytes 2850824 | tf_op jit(solution)/shard_map/ppermute | solution.py:192
  23.3 1.2 copy-start.3
  24.5 1.4 copy-start.4
  26.6 10.5 %collective-permute-start = (bf16[400,1024]{1,0:T(8,128)(2,1)S(1)}, bf16[400,1024]{1,0:T(8,128)(2,1)S(1)}, u32[]{:S(2)}, u32[]{:S(2)}) collective-permute-start(bf16[400,1024]{1,0:T(8,128)(2,1)S(1)} %shard_map.64.mine_ref), channel_id=1, source_target_pairs={{0,4},{4,0},{8,12},{12,8},{16,20},{20,16},{24,28},{28,24},{1,5},{5... | collective-permute-start | bytes 2457608 | tf_op jit(solution)/shard_map/ppermute | solution.py:192
  35.2 5.0 %copy-start.17 = (s32[2]{0:T(128)}, s32[2]{0:T(128)S(1)}, u32[]{:S(2)}) copy-start(s32[2]{0:T(128)S(1)} %pad_add_fusion.place_ref) | copy-start | bytes 28
  38.1 2.1 copy-start.9
  40.2 24.1 %all-to-all-start.1 = ((bf16[16,64,256]{2,1,0:T(8,128)(2,1)}), bf16[16,64,256]{2,1,0:T(8,128)(2,1)}, u32[]{:S(2)}, u32[]{:S(2)}) async-start(bf16[16,64,256]{2,1,0:T(8,128)(2,1)} %copy-done.11), calls=%async_computation.1 | async-start | bytes 1048576 | tf_op jit(solution)/shard_map/all_to_all | solution.py:213
  49.6 20.1 %collective-permute-start.5 = (bf16[240,1024]{1,0:T(8,128)(2,1)S(1)}, bf16[240,1024]{1,0:T(8,128)(2,1)S(1)}, u32[]{:S(2)}, u32[]{:S(2)}) collective-permute-start(bf16[240,1024]{1,0:T(8,128)(2,1)S(1)} %slice.12), channel_id=1, source_target_pairs={{0,96},{32,0},{64,32},{96,64},{128,224},{160,128},{192,160},{224,1... | collective-permute-start | bytes 1474568 | tf_op jit(solution)/shard_map/ppermute | solution.py:189
  55.1 14.6 %collective-permute-start.6 = (bf16[224,1024]{1,0:T(8,128)(2,1)S(1)}, bf16[224,1024]{1,0:T(8,128)(2,1)S(1)}, u32[]{:S(2)}, u32[]{:S(2)}) collective-permute-start(bf16[224,1024]{1,0:T(8,128)(2,1)S(1)} %slice.13), channel_id=1, source_target_pairs={{0,32},{32,64},{64,96},{96,0},{128,160},{160,192},{192,224},{224,1... | collective-permute-start | bytes 1376264 | tf_op jit(solution)/shard_map/ppermute | solution.py:189
  65.4 4.2 %copy-start.20 = (f32[64,256]{1,0:T(8,128)}, f32[64,256]{1,0:T(8,128)S(1)}, u32[]{:S(2)}) copy-start(f32[64,256]{1,0:T(8,128)S(1)} %convert_reduce_fusion.1) | copy-start | bytes 196612
  69.7 8.2 %copy-start.14 = (bf16[224,1024]{1,0:T(8,128)(2,1)}, bf16[224,1024]{1,0:T(8,128)(2,1)S(1)}, u32[]{:S(2)}) copy-start(bf16[224,1024]{1,0:T(8,128)(2,1)S(1)} %collective-permute-done.6.refs_4_) | copy-start | bytes 1376260
  69.7 8.2 %copy-start.12 = (bf16[240,1024]{1,0:T(8,128)(2,1)}, bf16[240,1024]{1,0:T(8,128)(2,1)S(1)}, u32[]{:S(2)}) copy-start(bf16[240,1024]{1,0:T(8,128)(2,1)S(1)} %collective-permute-done.5.refs_3_) | copy-start | bytes 1474564
  70.6 23.6 %all-to-all-start.2 = ((bf16[32,32,256]{2,1,0:T(8,128)(2,1)}), bf16[32,32,256]{2,1,0:T(8,128)(2,1)}, u32[]{:S(2)}, u32[]{:S(2)}) async-start(bf16[32,32,256]{2,1,0:T(8,128)(2,1)} %bitcast.10), calls=%async_computation.2 | async-start | bytes 1048576 | tf_op jit(solution)/shard_map/all_to_all | solution.py:222
  77.9 8.7 %collective-permute-start.7 = (bf16[464,1024]{1,0:T(8,128)(2,1)}, bf16[464,1024]{1,0:T(8,128)(2,1)S(1)}, u32[]{:S(2)}, u32[]{:S(2)}) collective-permute-start(bf16[464,1024]{1,0:T(8,128)(2,1)} %collective-permute-done.2.refs_1_), channel_id=1, source_target_pairs={{0,4},{4,0},{8,12},{12,8},{16,20},{20,16},{24,28},{28,24},{1,5},{5... | collective-permute-start | bytes 2850824 | tf_op jit(solution)/shard_map/ppermute | solution.py:192
  80.1 6.5 %collective-permute-start.8 = (bf16[464,1024]{1,0:T(8,128)(2,1)}, bf16[464,1024]{1,0:T(8,128)(2,1)S(1)}, u32[]{:S(2)}, u32[]{:S(2)}) collective-permute-start(bf16[464,1024]{1,0:T(8,128)(2,1)} %collective-permute-done.3.refs_2_), channel_id=1, source_target_pairs={{0,4},{4,0},{8,12},{12,8},{16,20},{20,16},{24,28},{28,24},{1,5},{5... | collective-permute-start | bytes 2850824 | tf_op jit(solution)/shard_map/ppermute | solution.py:192
  82.3 6.3 %collective-permute-start.9 = (bf16[240,1024]{1,0:T(8,128)(2,1)}, bf16[240,1024]{1,0:T(8,128)(2,1)}, u32[]{:S(2)}, u32[]{:S(2)}) collective-permute-start(bf16[240,1024]{1,0:T(8,128)(2,1)} %copy-done.12), channel_id=1, source_target_pairs={{0,4},{4,0},{8,12},{12,8},{16,20},{20,16},{24,28},{28,24},{1,5},{5... | collective-permute-start | bytes 1474568 | tf_op jit(solution)/shard_map/ppermute | solution.py:192
  84.5 4.1 %collective-permute-start.10 = (bf16[224,1024]{1,0:T(8,128)(2,1)}, bf16[224,1024]{1,0:T(8,128)(2,1)}, u32[]{:S(2)}, u32[]{:S(2)}) collective-permute-start(bf16[224,1024]{1,0:T(8,128)(2,1)} %copy-done.14), channel_id=1, source_target_pairs={{0,4},{4,0},{8,12},{12,8},{16,20},{20,16},{24,28},{28,24},{1,5},{5... | collective-permute-start | bytes 1376264 | tf_op jit(solution)/shard_map/ppermute | solution.py:192
  86.6 7.6 %copy-start.5 = (bf16[464,1024]{1,0:T(8,128)(2,1)}, bf16[464,1024]{1,0:T(8,128)(2,1)S(1)}, u32[]{:S(2)}) copy-start(bf16[464,1024]{1,0:T(8,128)(2,1)S(1)} %collective-permute-done.7.refs_6_) | copy-start | bytes 2850820
  86.6 7.6 %copy-start.7 = (bf16[464,1024]{1,0:T(8,128)(2,1)}, bf16[464,1024]{1,0:T(8,128)(2,1)S(1)}, u32[]{:S(2)}) copy-start(bf16[464,1024]{1,0:T(8,128)(2,1)S(1)} %collective-permute-done.8.refs_7_) | copy-start | bytes 2850820
  102.2 63.1 %copy-start.2 = (bf16[2,232,1024]{2,1,0:T(8,128)(2,1)S(1)}, bf16[2,232,1024]{2,1,0:T(8,128)(2,1)}, u32[]{:S(2)}) copy-start(bf16[2,232,1024]{2,1,0:T(8,128)(2,1)} %copy-done.1) | copy-start | bytes 2850820
  102.3 63.1 %copy-start.6 = (bf16[464,1024]{1,0:T(8,128)(2,1)S(1)}, bf16[464,1024]{1,0:T(8,128)(2,1)}, u32[]{:S(2)}) copy-start(bf16[464,1024]{1,0:T(8,128)(2,1)} %copy-done.5) | copy-start | bytes 2850820
  102.3 63.1 %copy-start.18 = (s32[2]{0:T(128)S(1)}, s32[2]{0:T(128)}, u32[]{:S(2)}) copy-start(s32[2]{0:T(128)} %copy-done.17) | copy-start | bytes 28
  102.3 39.3 %all-to-all-start.3 = ((bf16[4,464,128]{2,1,0:T(8,128)(2,1)}), bf16[4,464,128]{2,1,0:T(8,128)(2,1)}, u32[]{:S(2)}, u32[]{:S(2)}) async-start(bf16[4,464,128]{2,1,0:T(8,128)(2,1)} %shard_map.66), calls=%async_computation.3 | async-start | bytes 950272 | tf_op jit(solution)/shard_map/all_to_all | solution.py:248
  116.1 26.8 %collective-permute-start.1 = (bf16[231,128]{1,0:T(8,128)(2,1)}, bf16[231,128]{1,0:T(8,128)(2,1)}, u32[]{:S(2)}, u32[]{:S(2)}) collective-permute-start(bf16[231,128]{1,0:T(8,128)(2,1)} %dynamic-slice_bitcast_fusion.1), channel_id=1, source_target_pairs={{0,0},{4,4},{40,8},{44,12},{112,16},{116,20},{88,24},{92,28},{32,1... | collective-permute-start | bytes 177416 | tf_op jit(solution)/shard_map/ppermute | solution.py:242
  141.6 23.7 %copy-start.8 = (bf16[464,1024]{1,0:T(8,128)(2,1)S(1)}, bf16[464,1024]{1,0:T(8,128)(2,1)}, u32[]{:S(2)}) copy-start(bf16[464,1024]{1,0:T(8,128)(2,1)} %copy-done.7) | copy-start | bytes 2850820
  171.6 24.7 %copy-start.21 = (f32[64,256]{1,0:T(8,128)S(1)}, f32[64,256]{1,0:T(8,128)}, u32[]{:S(2)}) copy-start(f32[64,256]{1,0:T(8,128)} %copy-done.20) | copy-start | bytes 196612
  171.6 43.2 %copy-start.10 = (bf16[400,1024]{1,0:T(8,128)(2,1)S(1)}, bf16[400,1024]{1,0:T(8,128)(2,1)}, u32[]{:S(2)}) copy-start(bf16[400,1024]{1,0:T(8,128)(2,1)} %copy-done.9) | copy-start | bytes 2457604
  (5 other events, 5.0 us)

commit v5 on v4

--- a/solution.py
+++ b/solution.py
@@ -9,7 +9,8 @@
 F32 = jnp.float32
 BF16 = jnp.bfloat16
 KERNEL_VMEM = 60 * 2**20
-SMALL_VMEM = 24 * 2**20
+SMALL_VMEM = 48 * 2**20
+PICK_VMEM = 52 * 2**20
 
 
 def gelu_exact(value):
@@ -25,7 +26,7 @@
     return lax.dot_general(a, b, (contract, ((), ())), preferred_element_type=F32)
 
 
-def in_vmem(body, n_scalars, out_shape, operands, flops, scratch=()):
+def in_vmem(body, n_scalars, out_shape, operands, flops, scratch=(), limit=SMALL_VMEM):
     spaces = [pltpu.SMEM] * n_scalars + [pltpu.VMEM] * (len(operands) - n_scalars)
     moved = 2 * sum(a.size for a in operands[n_scalars:])
     return pl.pallas_call(
@@ -34,7 +35,7 @@
         out_specs=pl.BlockSpec(memory_space=pltpu.VMEM),
         out_shape=jax.ShapeDtypeStruct(out_shape, BF16),
         scratch_shapes=list(scratch),
-        compiler_params=pltpu.CompilerParams(vmem_limit_bytes=SMALL_VMEM),
+        compiler_params=pltpu.CompilerParams(vmem_limit_bytes=limit),
         cost_estimate=pl.CostEstimate(flops=flops, bytes_accessed=moved, transcendentals=0),
     )(*operands)
 
@@ -81,32 +82,60 @@
     out_ref[second, :] = dot(other_ref[...], dpre, ((1,), (0,))).astype(BF16)
 
 
-def gate_body(place_ref, h_ref, weights, out_ref, held, sems, turned):
-    n = len(weights) // 2
-    copies = weight_copies(weights, held, sems)
+def gate_kernel(place_ref, h_hbm, *refs):
+    n = (len(refs) - 5) // 4
+    weights, out_hbm, held = refs[: 2 * n], refs[2 * n], refs[2 * n + 1 : 4 * n + 1]
+    h, turned, out, sems = refs[4 * n + 1 :]
+    loads = weight_copies(weights, held, sems)
+    load_h = pltpu.make_async_copy(h_hbm, h, sems.at[2 * n])
+    load_h.start()
     for i in range(n):
-        copies[i].start()
-        copies[i + n].start()
-    core, blocks, rows = place_ref[0], out_ref.shape[0], out_ref.shape[1]
-    _, lows, n_vis, few, width = h_ref.shape
+        loads[i].start()
+        loads[i + n].start()
+    core, blocks, rows = place_ref[0], out.shape[0], out.shape[1]
+    _, lows, n_vis, few, width = h.shape
+    model = n_vis * width
+    load_h.wait()
     for j in range(2):
         slot = core if j == 0 else 1 - core
         for v in range(n_vis):
-            block = h_ref[slot, :, v].reshape(lows * few, width)
+            block = h[slot, :, v].reshape(lows * few, width)
             at = (j * n_vis + v) * width
             turned[at : at + width, :] = block.astype(F32).T.astype(BF16)
-    model = n_vis * width
+    stores = []
     block, at = 0, 0
     for i in range(n):
         size = held[i].shape[0]
-        copies[i].wait()
-        copies[i + n].wait()
+        loads[i].wait()
+        loads[i + n].wait()
         total = dot(held[i][...], turned[:model, :], ((1,), (0,)))
         total = total + dot(held[i + n][...], turned[model:, :], ((1,), (0,)))
-        chunk = lax.rem(block + blocks - place_ref[1], blocks)
-        out_ref[chunk, at : at + size, :] = total.astype(BF16)
+        out[block, at : at + size, :] = total.astype(BF16)
         at += size
-        block, at = block + at // rows, at % rows
+        if at == rows:
+            chunk = lax.rem(block + blocks - place_ref[1], blocks)
+            stores.append(pltpu.make_async_copy(out.at[block], out_hbm.at[chunk], sems.at[2 * n + 1 + block]))
+            stores[-1].start()
+            block, at = block + 1, 0
+    for store in stores:
+        store.wait()
+
+
+def gate_up(place, hidden, weights, out_shape, flops, turned):
+    n = len(weights)
+    hbm = pl.BlockSpec(memory_space=pltpu.HBM)
+    moved = sum(w.size for w in weights) + hidden.size
+    return pl.pallas_call(
+        gate_kernel,
+        in_specs=[pl.BlockSpec(memory_space=pltpu.SMEM)] + [hbm] * (n + 1),
+        out_specs=hbm,
+        out_shape=jax.ShapeDtypeStruct(out_shape, BF16),
+        scratch_shapes=[pltpu.VMEM(w.shape, BF16) for w in weights]
+        + [pltpu.VMEM(hidden.shape, BF16), pltpu.VMEM(turned, BF16), pltpu.VMEM(out_shape, BF16)]
+        + [pltpu.SemaphoreType.DMA((n + 1 + out_shape[0],))],
+        compiler_params=pltpu.CompilerParams(vmem_limit_bytes=KERNEL_VMEM),
+        cost_estimate=pl.CostEstimate(flops=flops, bytes_accessed=2 * moved, transcendentals=0),
+    )(place, hidden, *weights)
 
 
 def dact_body(place_ref, d_ref, weights, out_ref, held, sems, turned):
@@ -199,7 +228,7 @@
     weights = jnp.stack([gate_weight.T, up_weight.T])
     weights = jnp.pad(weights, ((0, 0), (0, pad), (0, 0))).reshape(2 * (unit + pad), -1)
     right, left, weights_o = from_x(weights, 1), from_x(weights, -1), from_core(weights)
-    mine = in_vmem(pick_kernel, 1, (half, n_x * TILE), (tile_slot, arrived), 0)
+    mine = in_vmem(pick_kernel, 1, (half, n_x * TILE), (tile_slot, arrived), 0, limit=PICK_VMEM)
     other = from_core(mine)
 
     n_tok, width = n_x * TILE, proj_weight.shape[1]
@@ -208,7 +237,7 @@
     flops = 2 * n_tok * features * width
     partial = in_vmem(proj_kernel, 1, (n_row, share, width), (place, mine, other, proj_weight), flops)
     partial, right, left, weights_o = lax.optimization_barrier((partial, right, left, weights_o))
-    first = -((unit + pad) // -16) * 16
+    first = -(weights.shape[0] * 11 // -320) * 16
     far_low, far_high = right[:first], left[first:]
     partial = lax.all_to_all(partial, "row", 0, 0, axis_index_groups=row_groups)
     far_low, far_high = from_x(far_low, 1), from_x(far_high, -1)
@@ -244,7 +273,7 @@
 
     rows = 2 * (unit + pad)
     flops = 4 * lane * n_x * rows * model
-    both = with_weights(gate_body, place, hidden, pieces, (n_x, rows, lane), flops, (2 * model, lane), KERNEL_VMEM)
+    both = gate_up(place, hidden, pieces, (n_x, rows, lane), flops, (2 * model, lane))
     sums = lax.all_to_all(both, "col", 0, 0, axis_index_groups=quarter_groups)
     sums = jnp.sum(sums.astype(F32), axis=0)
     gate_sum, up_sum = sums[: unit + pad], sums[unit + pad :]

time: 218 us -> 218 us (level)
  local copies, waits for them, and re-layouts: 13.7 us -> 11.3 us
    pallas_call x2 -> x1, Pallas kernels: 12.2 us -> 4.2 us  [with_weights(): pl.pallas_call(kernel, in_specs=[pl.BlockSpec(memory_space=pltpu.SMEM), p...]
    pallas_call x0 -> x1, Pallas kernels: none -> 7.73 us  [gate_up(): pl.pallas_call(gate_kernel, in_specs=[pl.BlockSpec(memory_space=pltpu.SME...]
    unnamed x44, local copies, waits for them, and re-layouts: 7.69 us -> 4.81 us
  transfers between devices with their start and end apart: 15 -> 15, of which waited for: 7 -> 7; matrix products, arithmetic and copies ran while one was open for 3% -> 3% of each run, Pallas kernels for 1% -> 2%
where the time goes in v5:
time: 218 us; the launch traced here: 216 us
  starting transfers between devices  72.8 us (33%)
  blocking collectives  65.9 us (30%)
  waiting for transfers between devices  44.4 us (20%)
  Pallas kernels  17.9 us (8%)
  local copies, waits for them, and re-layouts  11.3 us (5%)
  other arithmetic  3.51 us (2%)
    ppermute x6, starting transfers between devices, from_core(): return lax.ppermute(value, 'col', core_pairs)  25.4 us
    all_to_all x1, blocking collectives, shards(): lax.all_to_all(dact.reshape(2 * spread, few, width), ('row', 'col', 'vis'...  25.2 us
    all_to_all x1, waiting for transfers between devices, shards(): sums = lax.all_to_all(both, 'col', 0, 0, axis_index_groups=quarter_groups)  23.5 us
    all_gather x1, blocking collectives, shards(): lax.all_gather(d_both, 'col', axis=0, axis_index_groups=quarter_groups)  21.6 us
    all_to_all x1, blocking collectives, shards(): lax.all_to_all(jnp.broadcast_to(dpre[None], (n_row, share, width)), 'row'...  19.1 us
    ppermute x4, starting transfers between devices, from_x(): return lax.ppermute(value, 'row', pairs)  12.8 us
    all_to_all x1, starting transfers between devices, shards(): sums = lax.all_to_all(both, 'col', 0, 0, axis_index_groups=quarter_groups)  12.2 us
    all_to_all x1, starting transfers between devices, shards(): partial = lax.all_to_all(partial, 'row', 0, 0, axis_index_groups=row_groups)  8.29 us
  transfers between devices with their start and end apart: 15, of which 7 were waited for; matrix products, arithmetic and copies ran while one was open for 3% of the time, Pallas kernels for 2%

profile of v5, /device:TPU:1, one launch (start us, length us, event | category | flops | bytes accessed | tf_op | source)
XLA Modules:
  0.0 216.2 jit_solution(1930865735557016532)
XLA Ops:
  1.2 1.3 broadcast_in_dim.6
  2.5 5.1 %all-to-all-start = ((bf16[4,400,512]{2,1,0:T(8,128)(2,1)}), bf16[4,400,512]{2,1,0:T(8,128)(2,1)}, u32[]{:S(2)}, u32[]{:S(2)}) async-start(bf16[4,400,512]{2,1,0:T(8,128)(2,1)} %broadcast_in_dim.6), calls=%async_computation | async-start | bytes 3276800 | tf_op jit(solution)/shard_map/all_to_all | solution.py:225
  7.8 4.6 %collective-permute-start.2 = (bf16[464,1024]{1,0:T(8,128)(2,1)S(1)}, bf16[464,1024]{1,0:T(8,128)(2,1)S(1)}, u32[]{:S(2)}, u32[]{:S(2)}) collective-permute-start(bf16[464,1024]{1,0:T(8,128)(2,1)S(1)} %bitcast.23), channel_id=1, source_target_pairs={{0,96},{32,0},{64,32},{96,64},{128,224},{160,128},{192,160},{224,1... | collective-permute-start | bytes 2850824 | tf_op jit(solution)/shard_map/ppermute | solution.py:218
  12.4 1.9 collective-permute-start.3
  14.3 7.5 %collective-permute-start.4 = (bf16[464,1024]{1,0:T(8,128)(2,1)S(1)}, bf16[464,1024]{1,0:T(8,128)(2,1)}, u32[]{:S(2)}, u32[]{:S(2)}) collective-permute-start(bf16[464,1024]{1,0:T(8,128)(2,1)S(1)} %bitcast.25), channel_id=1, source_target_pairs={{0,4},{4,0},{8,12},{12,8},{16,20},{20,16},{24,28},{28,24},{1,5},{5... | collective-permute-start | bytes 2850824 | tf_op jit(solution)/shard_map/ppermute | solution.py:221
  22.9 1.5 shard_map.64.mine_ref
  24.5 9.2 %collective-permute-start = (bf16[400,1024]{1,0:T(8,128)(2,1)S(1)}, bf16[400,1024]{1,0:T(8,128)(2,1)}, u32[]{:S(2)}, u32[]{:S(2)}) collective-permute-start(bf16[400,1024]{1,0:T(8,128)(2,1)S(1)} %shard_map.64.mine_ref), channel_id=1, source_target_pairs={{0,4},{4,0},{8,12},{12,8},{16,20},{20,16},{24,28},{28,24},{1,5},{5... | collective-permute-start | bytes 2457608 | tf_op jit(solution)/shard_map/ppermute | solution.py:221
  33.8 2.0 collective-permute-done.other_ref
  36.8 1.9 shard_map.65
  39.5 8.3 %all-to-all-start.1 = ((bf16[16,64,256]{2,1,0:T(8,128)(2,1)}), bf16[16,64,256]{2,1,0:T(8,128)(2,1)}, u32[]{:S(2)}, u32[]{:S(2)}) async-start(bf16[16,64,256]{2,1,0:T(8,128)(2,1)} %copy-done.7), calls=%async_computation.1 | async-start | bytes 1048576 | tf_op jit(solution)/shard_map/all_to_all | solution.py:242
  48.7 4.4 %collective-permute-start.5 = (bf16[256,1024]{1,0:T(8,128)(2,1)}, bf16[256,1024]{1,0:T(8,128)(2,1)S(1)}, u32[]{:S(2)}, u32[]{:S(2)}) collective-permute-start(bf16[256,1024]{1,0:T(8,128)(2,1)} %slice.12), channel_id=1, source_target_pairs={{0,96},{32,0},{64,32},{96,64},{128,224},{160,128},{192,160},{224,1... | collective-permute-start | bytes 1572872 | tf_op jit(solution)/shard_map/ppermute | solution.py:218
  53.1 1.8 slice.13
  54.9 1.9 collective-permute-start.6
  56.8 6.8 %all-to-all-done.1 = bf16[16,64,256]{2,1,0:T(8,128)(2,1)} async-done(((bf16[16,64,256]{2,1,0:T(8,128)(2,1)}), bf16[16,64,256]{2,1,0:T(8,128)(2,1)}, u32[]{:S(2)}, u32[]{:S(2)}) %all-to-all-start.1) | async-done | bytes 524320 | tf_op jit(solution)/shard_map/all_to_all | solution.py:242
  64.8 4.2 %collective-permute-done.6.refs_4_ = bf16[208,1024]{1,0:T(8,128)(2,1)S(1)} collective-permute-done((bf16[208,1024]{1,0:T(8,128)(2,1)}, bf16[208,1024]{1,0:T(8,128)(2,1)S(1)}, u32[]{:S(2)}, u32[]{:S(2)}) %collective-permute-start.6) | collective-permute-done | bytes 426016 | tf_op jit(solution)/shard_map/ppermute | solution.py:218
  70.0 6.8 %all-to-all-start.2 = ((bf16[32,32,256]{2,1,0:T(8,128)(2,1)}), bf16[32,32,256]{2,1,0:T(8,128)(2,1)}, u32[]{:S(2)}, u32[]{:S(2)}) async-start(bf16[32,32,256]{2,1,0:T(8,128)(2,1)} %bitcast.30), calls=%async_computation.2 | async-start | bytes 1048576 | tf_op jit(solution)/shard_map/all_to_all | solution.py:251
  76.8 2.2 %collective-permute-start.7 = (bf16[464,1024]{1,0:T(8,128)(2,1)S(1)}, bf16[464,1024]{1,0:T(8,128)(2,1)S(1)}, u32[]{:S(2)}, u32[]{:S(2)}) collective-permute-start(bf16[464,1024]{1,0:T(8,128)(2,1)S(1)} %collective-permute-done.2.refs_1_), channel_id=1, source_target_pairs={{0,4},{4,0},{8,12},{12,8},{16,20},{20,16},{24,28},{28,24},{1,5},{5... | collective-permute-start | bytes 2850824 | tf_op jit(solution)/shard_map/ppermute | solution.py:221
  79.0 2.1 collective-permute-start.8
  81.1 2.2 %collective-permute-start.9 = (bf16[256,1024]{1,0:T(8,128)(2,1)S(1)}, bf16[256,1024]{1,0:T(8,128)(2,1)}, u32[]{:S(2)}, u32[]{:S(2)}) collective-permute-start(bf16[256,1024]{1,0:T(8,128)(2,1)S(1)} %collective-permute-done.5.refs_3_), channel_id=1, source_target_pairs={{0,4},{4,0},{8,12},{12,8},{16,20},{20,16},{24,28},{28,24},{1,5},{5... | collective-permute-start | bytes 1572872 | tf_op jit(solution)/shard_map/ppermute | solution.py:221
  83.3 2.1 collective-permute-start.10
  85.5 1.5 collective-permute-done.10.refs_9_
  87.8 5.3 %all-to-all-done.2 = bf16[32,32,256]{2,1,0:T(8,128)(2,1)} async-done(((bf16[32,32,256]{2,1,0:T(8,128)(2,1)}), bf16[32,32,256]{2,1,0:T(8,128)(2,1)}, u32[]{:S(2)}, u32[]{:S(2)}) %all-to-all-start.2) | async-done | bytes 524320 | tf_op jit(solution)/shard_map/all_to_all | solution.py:251
  93.1 7.7 %shard_map.66 = bf16[4,464,128]{2,1,0:T(8,128)(2,1)} custom-call(s32[2]{0:T(128)} %copy-done.13, bf16[2,4,4,32,256]{4,3,2,1,0:T(8,128)(2,1)} %bitcast.11.h_hbm, bf16[464,1024]{1,0:T(8,128)(2,1)} %bitcast.26, bf16[464,1024]{1,0:T(8,128)(2,1)} %copy-done.3, bf16[464,1024]{1,0:T(8,128)(2,1)} %collective-permute-done.3.refs_2_, bf16[256,1024]{1,0:T(8,128)(2,1)} %copy-done.5, ...), custom_call_target="tpu_custom_call" | custom-call | flops 973078528 | bytes 8126464 | tf_op jit(solution)/shard_map/pallas_call | solution.py:128
  100.8 12.2 %all-to-all-start.3 = ((bf16[4,464,128]{2,1,0:T(8,128)(2,1)}), bf16[4,464,128]{2,1,0:T(8,128)(2,1)}, u32[]{:S(2)}, u32[]{:S(2)}) async-start(bf16[4,464,128]{2,1,0:T(8,128)(2,1)} %shard_map.66), calls=%async_computation.3 | async-start | bytes 950272 | tf_op jit(solution)/shard_map/all_to_all | solution.py:277
  113.1 1.5 dynamic-slice_bitcast_fusion.1
  114.6 2.1 collective-permute-start.1
  116.7 23.5 %all-to-all-done.3 = bf16[4,464,128]{2,1,0:T(8,128)(2,1)} async-done(((bf16[4,464,128]{2,1,0:T(8,128)(2,1)}), bf16[4,464,128]{2,1,0:T(8,128)(2,1)}, u32[]{:S(2)}, u32[]{:S(2)}) %all-to-all-start.3) | async-done | bytes 475168 | tf_op jit(solution)/shard_map/all_to_all | solution.py:277
  142.3 21.6 %all-gather = bf16[1856,128]{1,0:T(8,128)(2,1)S(1)} all-gather(bf16[464,128]{1,0:T(8,128)(2,1)S(1)} %pad_maximum_fusion), channel_id=2, replica_groups={{0,8,16,24},{4,12,20,28},{1,9,17,25},{5,13,21,29},{2,10,18,26},{6,14,22..., dimensions={0}, use_global_device_ids=true | all-gather | bytes 593920 | tf_op jit(solution)/shard_map/all_gather | solution.py:284
  165.0 4.2 %shard_map.67 = bf16[2,4,4,32,256]{4,3,2,1,0:T(8,128)(2,1)S(1)} custom-call(s32[2]{0:T(128)S(1)} %copy-done.14, bf16[4,464,128]{2,1,0:T(8,128)(2,1)S(1)} %bitcast.29, bf16[464,1024]{1,0:T(8,128)(2,1)S(1)} %bitcast.27, bf16[464,1024]{1,0:T(8,128)(2,1)S(1)} %copy-done.4, bf16[464,1024]{1,0:T(8,128)(2,1)} %collective-permute-done.3.refs_2_, ...), custom_call_target="tpu_custom_call" | custom-call | flops 973078528 | bytes 8077312 | tf_op jit(solution)/shard_map/pallas_call | solution.py:176
  169.2 25.2 %all_to_all.30 = bf16[32,32,256]{2,1,0:T(8,128)(2,1)S(1)} all-to-all(bf16[32,32,256]{2,1,0:T(8,128)(2,1)S(1)} %bitcast.28), channel_id=1, replica_groups={{0,1,2,3,128,129,130,131,256,257,258,259,384,385,386,387,4,5,6,7,132,13..., dimensions={0} | all-to-all | bytes 1048576 | tf_op jit(solution)/shard_map/all_to_all | solution.py:288
  194.6 19.1 %all_to_all.31.dpre_ref = bf16[16,64,256]{2,1,0:T(8,128)(2,1)S(1)} all-to-all(bf16[16,64,256]{2,1,0:T(8,128)(2,1)S(1)} %broadcast_in_dim.8), channel_id=1, replica_groups={{0,128,256,384,32,160,288,416,64,192,320,448,96,224,352,480},{1,129,257..., dimensions={0} | all-to-all | bytes 1048576 | tf_op jit(solution)/shard_map/all_to_all | solution.py:293
  213.6 2.5 %shard_map.68 = bf16[800,256]{1,0:T(8,128)(2,1)} custom-call(s32[2]{0:T(128)S(1)} %copy-done.14, bf16[400,1024]{1,0:T(8,128)(2,1)S(1)} %shard_map.64.mine_ref, bf16[400,1024]{1,0:T(8,128)(2,1)} %collective-permute-done.other_ref, bf16[16,64,256]{2,1,0:T(8,128)(2,1)S(1)} %all_to_all.31.dpre_ref), custom_call_target="tpu_custom_call" | custom-call | flops 419430400 | bytes 2162688 | tf_op jit(solution)/shard_map/pallas_call | solution.py:32
  (66 shorter events, 11.3 us)
Async XLA Ops:
  2.5 5.2 %copy-start.20 = (bf16[1024,231]{0,1:T(8,128)(2,1)S(1)}, bf16[1024,231]{0,1:T(8,128)(2,1)}, u32[]{:S(2)}) copy-start(bf16[1024,231]{0,1:T(8,128)(2,1)} %param.10) | copy-start | bytes 1419268
  2.5 5.2 %copy-start.21 = (bf16[1024,231]{0,1:T(8,128)(2,1)S(1)}, bf16[1024,231]{0,1:T(8,128)(2,1)}, u32[]{:S(2)}) copy-start(bf16[1024,231]{0,1:T(8,128)(2,1)} %param.9) | copy-start | bytes 1419268
  2.5 20.4 %all-to-all-start = ((bf16[4,400,512]{2,1,0:T(8,128)(2,1)}), bf16[4,400,512]{2,1,0:T(8,128)(2,1)}, u32[]{:S(2)}, u32[]{:S(2)}) async-start(bf16[4,400,512]{2,1,0:T(8,128)(2,1)} %broadcast_in_dim.6), calls=%async_computation | async-start | bytes 3276800 | tf_op jit(solution)/shard_map/all_to_all | solution.py:225
  7.6 15.3 %copy-start.15 = (s32[4]{0:T(128)S(1)}, s32[4]{0:T(128)}, u32[]{:S(2)}) copy-start(s32[4]{0:T(128)} %slot_ref.1) | copy-start | bytes 52
  7.7 30.9 %copy-start.1 = (bf16[2,232,1024]{2,1,0:T(8,128)(2,1)}, bf16[2,232,1024]{2,1,0:T(8,128)(2,1)S(1)}, u32[]{:S(2)}) copy-start(bf16[2,232,1024]{2,1,0:T(8,128)(2,1)S(1)} %fusion.2) | copy-start | bytes 2850820
  7.8 31.8 %collective-permute-start.2 = (bf16[464,1024]{1,0:T(8,128)(2,1)S(1)}, bf16[464,1024]{1,0:T(8,128)(2,1)S(1)}, u32[]{:S(2)}, u32[]{:S(2)}) collective-permute-start(bf16[464,1024]{1,0:T(8,128)(2,1)S(1)} %bitcast.23), channel_id=1, source_target_pairs={{0,96},{32,0},{64,32},{96,64},{128,224},{160,128},{192,160},{224,1... | collective-permute-start | bytes 2850824 | tf_op jit(solution)/shard_map/ppermute | solution.py:218
  12.4 27.2 %collective-permute-start.3 = (bf16[464,1024]{1,0:T(8,128)(2,1)S(1)}, bf16[464,1024]{1,0:T(8,128)(2,1)}, u32[]{:S(2)}, u32[]{:S(2)}) collective-permute-start(bf16[464,1024]{1,0:T(8,128)(2,1)S(1)} %bitcast.24), channel_id=1, source_target_pairs={{0,32},{32,64},{64,96},{96,0},{128,160},{160,192},{192,224},{224,1... | collective-permute-start | bytes 2850824 | tf_op jit(solution)/shard_map/ppermute | solution.py:218
  14.3 25.2 %collective-permute-start.4 = (bf16[464,1024]{1,0:T(8,128)(2,1)S(1)}, bf16[464,1024]{1,0:T(8,128)(2,1)}, u32[]{:S(2)}, u32[]{:S(2)}) collective-permute-start(bf16[464,1024]{1,0:T(8,128)(2,1)S(1)} %bitcast.25), channel_id=1, source_target_pairs={{0,4},{4,0},{8,12},{12,8},{16,20},{20,16},{24,28},{28,24},{1,5},{5... | collective-permute-start | bytes 2850824 | tf_op jit(solution)/shard_map/ppermute | solution.py:221
  24.5 11.3 %collective-permute-start = (bf16[400,1024]{1,0:T(8,128)(2,1)S(1)}, bf16[400,1024]{1,0:T(8,128)(2,1)}, u32[]{:S(2)}, u32[]{:S(2)}) collective-permute-start(bf16[400,1024]{1,0:T(8,128)(2,1)S(1)} %shard_map.64.mine_ref), channel_id=1, source_target_pairs={{0,4},{4,0},{8,12},{12,8},{16,20},{20,16},{24,28},{28,24},{1,5},{5... | collective-permute-start | bytes 2457608 | tf_op jit(solution)/shard_map/ppermute | solution.py:221
  33.8 5.8 %copy-start.13 = (s32[2]{0:T(128)}, s32[2]{0:T(128)S(1)}, u32[]{:S(2)}) copy-start(s32[2]{0:T(128)S(1)} %pad_add_fusion.place_ref) | copy-start | bytes 28
  39.5 37.2 %copy-start.3 = (bf16[464,1024]{1,0:T(8,128)(2,1)}, bf16[464,1024]{1,0:T(8,128)(2,1)S(1)}, u32[]{:S(2)}) copy-start(bf16[464,1024]{1,0:T(8,128)(2,1)S(1)} %collective-permute-done.2.refs_1_) | copy-start | bytes 2850820
  39.5 24.1 %all-to-all-start.1 = ((bf16[16,64,256]{2,1,0:T(8,128)(2,1)}), bf16[16,64,256]{2,1,0:T(8,128)(2,1)}, u32[]{:S(2)}, u32[]{:S(2)}) async-start(bf16[16,64,256]{2,1,0:T(8,128)(2,1)} %copy-done.7), calls=%async_computation.1 | async-start | bytes 1048576 | tf_op jit(solution)/shard_map/all_to_all | solution.py:242
  48.7 20.3 %collective-permute-start.5 = (bf16[256,1024]{1,0:T(8,128)(2,1)}, bf16[256,1024]{1,0:T(8,128)(2,1)S(1)}, u32[]{:S(2)}, u32[]{:S(2)}) collective-permute-start(bf16[256,1024]{1,0:T(8,128)(2,1)} %slice.12), channel_id=1, source_target_pairs={{0,96},{32,0},{64,32},{96,64},{128,224},{160,128},{192,160},{224,1... | collective-permute-start | bytes 1572872 | tf_op jit(solution)/shard_map/ppermute | solution.py:218
  54.9 14.1 %collective-permute-start.6 = (bf16[208,1024]{1,0:T(8,128)(2,1)}, bf16[208,1024]{1,0:T(8,128)(2,1)S(1)}, u32[]{:S(2)}, u32[]{:S(2)}) collective-permute-start(bf16[208,1024]{1,0:T(8,128)(2,1)} %slice.13), channel_id=1, source_target_pairs={{0,32},{32,64},{64,96},{96,0},{128,160},{160,192},{192,224},{224,1... | collective-permute-start | bytes 1277960 | tf_op jit(solution)/shard_map/ppermute | solution.py:218
  64.8 4.2 %copy-start.18 = (f32[64,256]{1,0:T(8,128)}, f32[64,256]{1,0:T(8,128)S(1)}, u32[]{:S(2)}) copy-start(f32[64,256]{1,0:T(8,128)S(1)} %convert_reduce_fusion.1) | copy-start | bytes 196612
  69.0 24.1 %copy-start.8 = (bf16[208,1024]{1,0:T(8,128)(2,1)}, bf16[208,1024]{1,0:T(8,128)(2,1)S(1)}, u32[]{:S(2)}) copy-start(bf16[208,1024]{1,0:T(8,128)(2,1)S(1)} %collective-permute-done.6.refs_4_) | copy-start | bytes 1277956
  69.0 24.1 %copy-start.5 = (bf16[256,1024]{1,0:T(8,128)(2,1)}, bf16[256,1024]{1,0:T(8,128)(2,1)S(1)}, u32[]{:S(2)}) copy-start(bf16[256,1024]{1,0:T(8,128)(2,1)S(1)} %collective-permute-done.5.refs_3_) | copy-start | bytes 1572868
  70.0 23.1 %all-to-all-start.2 = ((bf16[32,32,256]{2,1,0:T(8,128)(2,1)}), bf16[32,32,256]{2,1,0:T(8,128)(2,1)}, u32[]{:S(2)}, u32[]{:S(2)}) async-start(bf16[32,32,256]{2,1,0:T(8,128)(2,1)} %bitcast.30), calls=%async_computation.2 | async-start | bytes 1048576 | tf_op jit(solution)/shard_map/all_to_all | solution.py:251
  76.8 8.7 %collective-permute-start.7 = (bf16[464,1024]{1,0:T(8,128)(2,1)S(1)}, bf16[464,1024]{1,0:T(8,128)(2,1)S(1)}, u32[]{:S(2)}, u32[]{:S(2)}) collective-permute-start(bf16[464,1024]{1,0:T(8,128)(2,1)S(1)} %collective-permute-done.2.refs_1_), channel_id=1, source_target_pairs={{0,4},{4,0},{8,12},{12,8},{16,20},{20,16},{24,28},{28,24},{1,5},{5... | collective-permute-start | bytes 2850824 | tf_op jit(solution)/shard_map/ppermute | solution.py:221
  79.0 6.5 %collective-permute-start.8 = (bf16[464,1024]{1,0:T(8,128)(2,1)}, bf16[464,1024]{1,0:T(8,128)(2,1)S(1)}, u32[]{:S(2)}, u32[]{:S(2)}) collective-permute-start(bf16[464,1024]{1,0:T(8,128)(2,1)} %collective-permute-done.3.refs_2_), channel_id=1, source_target_pairs={{0,4},{4,0},{8,12},{12,8},{16,20},{20,16},{24,28},{28,24},{1,5},{5... | collective-permute-start | bytes 2850824 | tf_op jit(solution)/shard_map/ppermute | solution.py:221
  81.1 6.7 %collective-permute-start.9 = (bf16[256,1024]{1,0:T(8,128)(2,1)S(1)}, bf16[256,1024]{1,0:T(8,128)(2,1)}, u32[]{:S(2)}, u32[]{:S(2)}) collective-permute-start(bf16[256,1024]{1,0:T(8,128)(2,1)S(1)} %collective-permute-done.5.refs_3_), channel_id=1, source_target_pairs={{0,4},{4,0},{8,12},{12,8},{16,20},{20,16},{24,28},{28,24},{1,5},{5... | collective-permute-start | bytes 1572872 | tf_op jit(solution)/shard_map/ppermute | solution.py:221
  83.3 3.7 %collective-permute-start.10 = (bf16[208,1024]{1,0:T(8,128)(2,1)S(1)}, bf16[208,1024]{1,0:T(8,128)(2,1)S(1)}, u32[]{:S(2)}, u32[]{:S(2)}) collective-permute-start(bf16[208,1024]{1,0:T(8,128)(2,1)S(1)} %collective-permute-done.6.refs_4_), channel_id=1, source_target_pairs={{0,4},{4,0},{8,12},{12,8},{16,20},{20,16},{24,28},{28,24},{1,5},{5... | collective-permute-start | bytes 1277960 | tf_op jit(solution)/shard_map/ppermute | solution.py:221
  85.5 1.5 copy-start.16
  85.5 1.5 copy-start.17
  100.8 63.1 %copy-start.2 = (bf16[2,232,1024]{2,1,0:T(8,128)(2,1)S(1)}, bf16[2,232,1024]{2,1,0:T(8,128)(2,1)}, u32[]{:S(2)}) copy-start(bf16[2,232,1024]{2,1,0:T(8,128)(2,1)} %copy-done.1) | copy-start | bytes 2850820
  100.8 63.1 %copy-start.4 = (bf16[464,1024]{1,0:T(8,128)(2,1)S(1)}, bf16[464,1024]{1,0:T(8,128)(2,1)}, u32[]{:S(2)}) copy-start(bf16[464,1024]{1,0:T(8,128)(2,1)} %copy-done.3) | copy-start | bytes 2850820
  100.8 63.1 %copy-start.14 = (s32[2]{0:T(128)S(1)}, s32[2]{0:T(128)}, u32[]{:S(2)}) copy-start(s32[2]{0:T(128)} %copy-done.13) | copy-start | bytes 28
  100.8 39.3 %all-to-all-start.3 = ((bf16[4,464,128]{2,1,0:T(8,128)(2,1)}), bf16[4,464,128]{2,1,0:T(8,128)(2,1)}, u32[]{:S(2)}, u32[]{:S(2)}) async-start(bf16[4,464,128]{2,1,0:T(8,128)(2,1)} %shard_map.66), calls=%async_computation.3 | async-start | bytes 950272 | tf_op jit(solution)/shard_map/all_to_all | solution.py:277
  114.6 26.8 %collective-permute-start.1 = (bf16[231,128]{1,0:T(8,128)(2,1)}, bf16[231,128]{1,0:T(8,128)(2,1)}, u32[]{:S(2)}, u32[]{:S(2)}) collective-permute-start(bf16[231,128]{1,0:T(8,128)(2,1)} %dynamic-slice_bitcast_fusion.1), channel_id=1, source_target_pairs={{0,0},{4,4},{40,8},{44,12},{112,16},{116,20},{88,24},{92,28},{32,1... | collective-permute-start | bytes 177416 | tf_op jit(solution)/shard_map/ppermute | solution.py:271
  140.2 23.7 %copy-start.6 = (bf16[256,1024]{1,0:T(8,128)(2,1)S(1)}, bf16[256,1024]{1,0:T(8,128)(2,1)}, u32[]{:S(2)}) copy-start(bf16[256,1024]{1,0:T(8,128)(2,1)} %copy-done.5) | copy-start | bytes 1572868
  140.2 23.8 %copy-start.9 = (bf16[208,1024]{1,0:T(8,128)(2,1)S(1)}, bf16[208,1024]{1,0:T(8,128)(2,1)}, u32[]{:S(2)}) copy-start(bf16[208,1024]{1,0:T(8,128)(2,1)} %copy-done.8) | copy-start | bytes 1277956
  169.2 25.3 %copy-start.19 = (f32[64,256]{1,0:T(8,128)S(1)}, f32[64,256]{1,0:T(8,128)}, u32[]{:S(2)}) copy-start(f32[64,256]{1,0:T(8,128)} %copy-done.18) | copy-start | bytes 196612
  (5 other events, 4.8 us)

commit v6 on v5

--- a/solution.py
+++ b/solution.py
@@ -9,7 +9,8 @@
 F32 = jnp.float32
 BF16 = jnp.bfloat16
 KERNEL_VMEM = 60 * 2**20
-SMALL_VMEM = 48 * 2**20
+SMALL_VMEM = 24 * 2**20
+DACT_VMEM = 48 * 2**20
 PICK_VMEM = 52 * 2**20
 
 
@@ -284,7 +285,7 @@
     d_all = lax.all_gather(d_both, "col", axis=0, axis_index_groups=quarter_groups)
 
     shape = (2, n_low, n_vis, few, width)
-    dact = with_weights(dact_body, place, d_all, pieces, shape, flops, (16, lane), SMALL_VMEM)
+    dact = with_weights(dact_body, place, d_all, pieces, shape, flops, (16, lane), DACT_VMEM)
     dact = lax.all_to_all(
         dact.reshape(2 * spread, few, width), ("row", "col", "vis"), 0, 0, axis_index_groups=column_groups
     )

time: 218 us -> 218 us (level)
  no operation moved by 1% of the time
where the time goes in v6:
time: 218 us; the launch traced here: 216 us
  starting transfers between devices  72.8 us (33%)
  blocking collectives  66 us (30%)
  waiting for transfers between devices  44.4 us (20%)
  Pallas kernels  17.9 us (8%)
  local copies, waits for them, and re-layouts  11.3 us (5%)
  other arithmetic  3.51 us (2%)
    ppermute x6, starting transfers between devices, from_core(): return lax.ppermute(value, 'col', core_pairs)  25.4 us
    all_to_all x1, blocking collectives, shards(): lax.all_to_all(dact.reshape(2 * spread, few, width), ('row', 'col', 'vis'...  25.2 us
    all_to_all x1, waiting for transfers between devices, shards(): sums = lax.all_to_all(both, 'col', 0, 0, axis_index_groups=quarter_groups)  23.5 us
    all_gather x1, blocking collectives, shards(): lax.all_gather(d_both, 'col', axis=0, axis_index_groups=quarter_groups)  21.6 us
    all_to_all x1, blocking collectives, shards(): lax.all_to_all(jnp.broadcast_to(dpre[None], (n_row, share, width)), 'row'...  19.3 us
    ppermute x4, starting transfers between devices, from_x(): return lax.ppermute(value, 'row', pairs)  12.8 us
    all_to_all x1, starting transfers between devices, shards(): sums = lax.all_to_all(both, 'col', 0, 0, axis_index_groups=quarter_groups)  12.3 us
    all_to_all x1, starting transfers between devices, shards(): partial = lax.all_to_all(partial, 'row', 0, 0, axis_index_groups=row_groups)  8.29 us
  transfers between devices with their start and end apart: 15, of which 7 were waited for; matrix products, arithmetic and copies ran while one was open for 3% of the time, Pallas kernels for 2%

profile of v6, /device:TPU:1, one launch (start us, length us, event | category | flops | bytes accessed | tf_op | source)
XLA Modules:
  0.0 216.3 jit_solution(2190223287418385955)
XLA Ops:
  1.2 1.3 broadcast_in_dim.6
  2.5 5.1 %all-to-all-start = ((bf16[4,400,512]{2,1,0:T(8,128)(2,1)}), bf16[4,400,512]{2,1,0:T(8,128)(2,1)}, u32[]{:S(2)}, u32[]{:S(2)}) async-start(bf16[4,400,512]{2,1,0:T(8,128)(2,1)} %broadcast_in_dim.6), calls=%async_computation | async-start | bytes 3276800 | tf_op jit(solution)/shard_map/all_to_all | solution.py:226
  7.8 4.6 %collective-permute-start.2 = (bf16[464,1024]{1,0:T(8,128)(2,1)S(1)}, bf16[464,1024]{1,0:T(8,128)(2,1)S(1)}, u32[]{:S(2)}, u32[]{:S(2)}) collective-permute-start(bf16[464,1024]{1,0:T(8,128)(2,1)S(1)} %bitcast.23), channel_id=1, source_target_pairs={{0,96},{32,0},{64,32},{96,64},{128,224},{160,128},{192,160},{224,1... | collective-permute-start | bytes 2850824 | tf_op jit(solution)/shard_map/ppermute | solution.py:219
  12.4 1.9 collective-permute-start.3
  14.3 7.5 %collective-permute-start.4 = (bf16[464,1024]{1,0:T(8,128)(2,1)S(1)}, bf16[464,1024]{1,0:T(8,128)(2,1)}, u32[]{:S(2)}, u32[]{:S(2)}) collective-permute-start(bf16[464,1024]{1,0:T(8,128)(2,1)S(1)} %bitcast.25), channel_id=1, source_target_pairs={{0,4},{4,0},{8,12},{12,8},{16,20},{20,16},{24,28},{28,24},{1,5},{5... | collective-permute-start | bytes 2850824 | tf_op jit(solution)/shard_map/ppermute | solution.py:222
  22.9 1.5 shard_map.64.mine_ref
  24.5 9.2 %collective-permute-start = (bf16[400,1024]{1,0:T(8,128)(2,1)S(1)}, bf16[400,1024]{1,0:T(8,128)(2,1)}, u32[]{:S(2)}, u32[]{:S(2)}) collective-permute-start(bf16[400,1024]{1,0:T(8,128)(2,1)S(1)} %shard_map.64.mine_ref), channel_id=1, source_target_pairs={{0,4},{4,0},{8,12},{12,8},{16,20},{20,16},{24,28},{28,24},{1,5},{5... | collective-permute-start | bytes 2457608 | tf_op jit(solution)/shard_map/ppermute | solution.py:222
  33.8 2.0 collective-permute-done.other_ref
  36.8 1.9 shard_map.65
  39.5 8.3 %all-to-all-start.1 = ((bf16[16,64,256]{2,1,0:T(8,128)(2,1)}), bf16[16,64,256]{2,1,0:T(8,128)(2,1)}, u32[]{:S(2)}, u32[]{:S(2)}) async-start(bf16[16,64,256]{2,1,0:T(8,128)(2,1)} %copy-done.7), calls=%async_computation.1 | async-start | bytes 1048576 | tf_op jit(solution)/shard_map/all_to_all | solution.py:243
  48.7 4.4 %collective-permute-start.5 = (bf16[256,1024]{1,0:T(8,128)(2,1)}, bf16[256,1024]{1,0:T(8,128)(2,1)S(1)}, u32[]{:S(2)}, u32[]{:S(2)}) collective-permute-start(bf16[256,1024]{1,0:T(8,128)(2,1)} %slice.12), channel_id=1, source_target_pairs={{0,96},{32,0},{64,32},{96,64},{128,224},{160,128},{192,160},{224,1... | collective-permute-start | bytes 1572872 | tf_op jit(solution)/shard_map/ppermute | solution.py:219
  53.1 1.8 slice.13
  54.9 1.9 collective-permute-start.6
  56.8 6.8 %all-to-all-done.1 = bf16[16,64,256]{2,1,0:T(8,128)(2,1)} async-done(((bf16[16,64,256]{2,1,0:T(8,128)(2,1)}), bf16[16,64,256]{2,1,0:T(8,128)(2,1)}, u32[]{:S(2)}, u32[]{:S(2)}) %all-to-all-start.1) | async-done | bytes 524320 | tf_op jit(solution)/shard_map/all_to_all | solution.py:243
  64.8 4.2 %collective-permute-done.6.refs_4_ = bf16[208,1024]{1,0:T(8,128)(2,1)S(1)} collective-permute-done((bf16[208,1024]{1,0:T(8,128)(2,1)}, bf16[208,1024]{1,0:T(8,128)(2,1)S(1)}, u32[]{:S(2)}, u32[]{:S(2)}) %collective-permute-start.6) | collective-permute-done | bytes 426016 | tf_op jit(solution)/shard_map/ppermute | solution.py:219
  70.0 6.8 %all-to-all-start.2 = ((bf16[32,32,256]{2,1,0:T(8,128)(2,1)}), bf16[32,32,256]{2,1,0:T(8,128)(2,1)}, u32[]{:S(2)}, u32[]{:S(2)}) async-start(bf16[32,32,256]{2,1,0:T(8,128)(2,1)} %bitcast.30), calls=%async_computation.2 | async-start | bytes 1048576 | tf_op jit(solution)/shard_map/all_to_all | solution.py:252
  76.8 2.2 %collective-permute-start.7 = (bf16[464,1024]{1,0:T(8,128)(2,1)S(1)}, bf16[464,1024]{1,0:T(8,128)(2,1)S(1)}, u32[]{:S(2)}, u32[]{:S(2)}) collective-permute-start(bf16[464,1024]{1,0:T(8,128)(2,1)S(1)} %collective-permute-done.2.refs_1_), channel_id=1, source_target_pairs={{0,4},{4,0},{8,12},{12,8},{16,20},{20,16},{24,28},{28,24},{1,5},{5... | collective-permute-start | bytes 2850824 | tf_op jit(solution)/shard_map/ppermute | solution.py:222
  79.0 2.1 collective-permute-start.8
  81.1 2.2 %collective-permute-start.9 = (bf16[256,1024]{1,0:T(8,128)(2,1)S(1)}, bf16[256,1024]{1,0:T(8,128)(2,1)}, u32[]{:S(2)}, u32[]{:S(2)}) collective-permute-start(bf16[256,1024]{1,0:T(8,128)(2,1)S(1)} %collective-permute-done.5.refs_3_), channel_id=1, source_target_pairs={{0,4},{4,0},{8,12},{12,8},{16,20},{20,16},{24,28},{28,24},{1,5},{5... | collective-permute-start | bytes 1572872 | tf_op jit(solution)/shard_map/ppermute | solution.py:222
  83.3 2.1 collective-permute-start.10
  85.5 1.5 collective-permute-done.10.refs_9_
  87.8 5.3 %all-to-all-done.2 = bf16[32,32,256]{2,1,0:T(8,128)(2,1)} async-done(((bf16[32,32,256]{2,1,0:T(8,128)(2,1)}), bf16[32,32,256]{2,1,0:T(8,128)(2,1)}, u32[]{:S(2)}, u32[]{:S(2)}) %all-to-all-start.2) | async-done | bytes 524320 | tf_op jit(solution)/shard_map/all_to_all | solution.py:252
  93.1 7.7 %shard_map.66 = bf16[4,464,128]{2,1,0:T(8,128)(2,1)} custom-call(s32[2]{0:T(128)} %copy-done.13, bf16[2,4,4,32,256]{4,3,2,1,0:T(8,128)(2,1)} %bitcast.11.h_hbm, bf16[464,1024]{1,0:T(8,128)(2,1)} %bitcast.26, bf16[464,1024]{1,0:T(8,128)(2,1)} %copy-done.3, bf16[464,1024]{1,0:T(8,128)(2,1)} %collective-permute-done.3.refs_2_, bf16[256,1024]{1,0:T(8,128)(2,1)} %copy-done.5, ...), custom_call_target="tpu_custom_call" | custom-call | flops 973078528 | bytes 8126464 | tf_op jit(solution)/shard_map/pallas_call | solution.py:129
  100.8 12.3 %all-to-all-start.3 = ((bf16[4,464,128]{2,1,0:T(8,128)(2,1)}), bf16[4,464,128]{2,1,0:T(8,128)(2,1)}, u32[]{:S(2)}, u32[]{:S(2)}) async-start(bf16[4,464,128]{2,1,0:T(8,128)(2,1)} %shard_map.66), calls=%async_computation.3 | async-start | bytes 950272 | tf_op jit(solution)/shard_map/all_to_all | solution.py:278
  113.1 1.5 dynamic-slice_bitcast_fusion.1
  114.6 2.1 collective-permute-start.1
  116.7 23.5 %all-to-all-done.3 = bf16[4,464,128]{2,1,0:T(8,128)(2,1)} async-done(((bf16[4,464,128]{2,1,0:T(8,128)(2,1)}), bf16[4,464,128]{2,1,0:T(8,128)(2,1)}, u32[]{:S(2)}, u32[]{:S(2)}) %all-to-all-start.3) | async-done | bytes 475168 | tf_op jit(solution)/shard_map/all_to_all | solution.py:278
  142.3 21.6 %all-gather = bf16[1856,128]{1,0:T(8,128)(2,1)S(1)} all-gather(bf16[464,128]{1,0:T(8,128)(2,1)S(1)} %pad_maximum_fusion), channel_id=2, replica_groups={{0,8,16,24},{4,12,20,28},{1,9,17,25},{5,13,21,29},{2,10,18,26},{6,14,22..., dimensions={0}, use_global_device_ids=true | all-gather | bytes 593920 | tf_op jit(solution)/shard_map/all_gather | solution.py:285
  165.0 4.2 %shard_map.67 = bf16[2,4,4,32,256]{4,3,2,1,0:T(8,128)(2,1)S(1)} custom-call(s32[2]{0:T(128)S(1)} %copy-done.14, bf16[4,464,128]{2,1,0:T(8,128)(2,1)S(1)} %bitcast.29, bf16[464,1024]{1,0:T(8,128)(2,1)S(1)} %bitcast.27, bf16[464,1024]{1,0:T(8,128)(2,1)S(1)} %copy-done.4, bf16[464,1024]{1,0:T(8,128)(2,1)} %collective-permute-done.3.refs_2_, ...), custom_call_target="tpu_custom_call" | custom-call | flops 973078528 | bytes 8077312 | tf_op jit(solution)/shard_map/pallas_call | solution.py:177
  169.2 25.2 %all_to_all.30 = bf16[32,32,256]{2,1,0:T(8,128)(2,1)S(1)} all-to-all(bf16[32,32,256]{2,1,0:T(8,128)(2,1)S(1)} %bitcast.28), channel_id=1, replica_groups={{0,1,2,3,128,129,130,131,256,257,258,259,384,385,386,387,4,5,6,7,132,13..., dimensions={0} | all-to-all | bytes 1048576 | tf_op jit(solution)/shard_map/all_to_all | solution.py:289
  194.5 19.3 %all_to_all.31.dpre_ref = bf16[16,64,256]{2,1,0:T(8,128)(2,1)S(1)} all-to-all(bf16[16,64,256]{2,1,0:T(8,128)(2,1)S(1)} %broadcast_in_dim.8), channel_id=1, replica_groups={{0,128,256,384,32,160,288,416,64,192,320,448,96,224,352,480},{1,129,257..., dimensions={0} | all-to-all | bytes 1048576 | tf_op jit(solution)/shard_map/all_to_all | solution.py:294
  213.8 2.5 %shard_map.68 = bf16[800,256]{1,0:T(8,128)(2,1)} custom-call(s32[2]{0:T(128)S(1)} %copy-done.14, bf16[400,1024]{1,0:T(8,128)(2,1)S(1)} %shard_map.64.mine_ref, bf16[400,1024]{1,0:T(8,128)(2,1)} %collective-permute-done.other_ref, bf16[16,64,256]{2,1,0:T(8,128)(2,1)S(1)} %all_to_all.31.dpre_ref), custom_call_target="tpu_custom_call" | custom-call | flops 419430400 | bytes 2162688 | tf_op jit(solution)/shard_map/pallas_call | solution.py:33
  (66 shorter events, 11.3 us)
Async XLA Ops:
  2.5 5.2 %copy-start.20 = (bf16[1024,231]{0,1:T(8,128)(2,1)S(1)}, bf16[1024,231]{0,1:T(8,128)(2,1)}, u32[]{:S(2)}) copy-start(bf16[1024,231]{0,1:T(8,128)(2,1)} %param.10) | copy-start | bytes 1419268
  2.5 5.2 %copy-start.21 = (bf16[1024,231]{0,1:T(8,128)(2,1)S(1)}, bf16[1024,231]{0,1:T(8,128)(2,1)}, u32[]{:S(2)}) copy-start(bf16[1024,231]{0,1:T(8,128)(2,1)} %param.9) | copy-start | bytes 1419268
  2.5 20.4 %all-to-all-start = ((bf16[4,400,512]{2,1,0:T(8,128)(2,1)}), bf16[4,400,512]{2,1,0:T(8,128)(2,1)}, u32[]{:S(2)}, u32[]{:S(2)}) async-start(bf16[4,400,512]{2,1,0:T(8,128)(2,1)} %broadcast_in_dim.6), calls=%async_computation | async-start | bytes 3276800 | tf_op jit(solution)/shard_map/all_to_all | solution.py:226
  7.6 15.3 %copy-start.15 = (s32[4]{0:T(128)S(1)}, s32[4]{0:T(128)}, u32[]{:S(2)}) copy-start(s32[4]{0:T(128)} %slot_ref.1) | copy-start | bytes 52
  7.7 30.9 %copy-start.1 = (bf16[2,232,1024]{2,1,0:T(8,128)(2,1)}, bf16[2,232,1024]{2,1,0:T(8,128)(2,1)S(1)}, u32[]{:S(2)}) copy-start(bf16[2,232,1024]{2,1,0:T(8,128)(2,1)S(1)} %fusion.2) | copy-start | bytes 2850820
  7.8 31.8 %collective-permute-start.2 = (bf16[464,1024]{1,0:T(8,128)(2,1)S(1)}, bf16[464,1024]{1,0:T(8,128)(2,1)S(1)}, u32[]{:S(2)}, u32[]{:S(2)}) collective-permute-start(bf16[464,1024]{1,0:T(8,128)(2,1)S(1)} %bitcast.23), channel_id=1, source_target_pairs={{0,96},{32,0},{64,32},{96,64},{128,224},{160,128},{192,160},{224,1... | collective-permute-start | bytes 2850824 | tf_op jit(solution)/shard_map/ppermute | solution.py:219
  12.4 27.2 %collective-permute-start.3 = (bf16[464,1024]{1,0:T(8,128)(2,1)S(1)}, bf16[464,1024]{1,0:T(8,128)(2,1)}, u32[]{:S(2)}, u32[]{:S(2)}) collective-permute-start(bf16[464,1024]{1,0:T(8,128)(2,1)S(1)} %bitcast.24), channel_id=1, source_target_pairs={{0,32},{32,64},{64,96},{96,0},{128,160},{160,192},{192,224},{224,1... | collective-permute-start | bytes 2850824 | tf_op jit(solution)/shard_map/ppermute | solution.py:219
  14.3 25.2 %collective-permute-start.4 = (bf16[464,1024]{1,0:T(8,128)(2,1)S(1)}, bf16[464,1024]{1,0:T(8,128)(2,1)}, u32[]{:S(2)}, u32[]{:S(2)}) collective-permute-start(bf16[464,1024]{1,0:T(8,128)(2,1)S(1)} %bitcast.25), channel_id=1, source_target_pairs={{0,4},{4,0},{8,12},{12,8},{16,20},{20,16},{24,28},{28,24},{1,5},{5... | collective-permute-start | bytes 2850824 | tf_op jit(solution)/shard_map/ppermute | solution.py:222
  24.5 11.3 %collective-permute-start = (bf16[400,1024]{1,0:T(8,128)(2,1)S(1)}, bf16[400,1024]{1,0:T(8,128)(2,1)}, u32[]{:S(2)}, u32[]{:S(2)}) collective-permute-start(bf16[400,1024]{1,0:T(8,128)(2,1)S(1)} %shard_map.64.mine_ref), channel_id=1, source_target_pairs={{0,4},{4,0},{8,12},{12,8},{16,20},{20,16},{24,28},{28,24},{1,5},{5... | collective-permute-start | bytes 2457608 | tf_op jit(solution)/shard_map/ppermute | solution.py:222
  33.8 5.8 %copy-start.13 = (s32[2]{0:T(128)}, s32[2]{0:T(128)S(1)}, u32[]{:S(2)}) copy-start(s32[2]{0:T(128)S(1)} %pad_add_fusion.place_ref) | copy-start | bytes 28
  39.5 37.2 %copy-start.3 = (bf16[464,1024]{1,0:T(8,128)(2,1)}, bf16[464,1024]{1,0:T(8,128)(2,1)S(1)}, u32[]{:S(2)}) copy-start(bf16[464,1024]{1,0:T(8,128)(2,1)S(1)} %collective-permute-done.2.refs_1_) | copy-start | bytes 2850820
  39.5 24.1 %all-to-all-start.1 = ((bf16[16,64,256]{2,1,0:T(8,128)(2,1)}), bf16[16,64,256]{2,1,0:T(8,128)(2,1)}, u32[]{:S(2)}, u32[]{:S(2)}) async-start(bf16[16,64,256]{2,1,0:T(8,128)(2,1)} %copy-done.7), calls=%async_computation.1 | async-start | bytes 1048576 | tf_op jit(solution)/shard_map/all_to_all | solution.py:243
  48.7 20.3 %collective-permute-start.5 = (bf16[256,1024]{1,0:T(8,128)(2,1)}, bf16[256,1024]{1,0:T(8,128)(2,1)S(1)}, u32[]{:S(2)}, u32[]{:S(2)}) collective-permute-start(bf16[256,1024]{1,0:T(8,128)(2,1)} %slice.12), channel_id=1, source_target_pairs={{0,96},{32,0},{64,32},{96,64},{128,224},{160,128},{192,160},{224,1... | collective-permute-start | bytes 1572872 | tf_op jit(solution)/shard_map/ppermute | solution.py:219
  54.9 14.1 %collective-permute-start.6 = (bf16[208,1024]{1,0:T(8,128)(2,1)}, bf16[208,1024]{1,0:T(8,128)(2,1)S(1)}, u32[]{:S(2)}, u32[]{:S(2)}) collective-permute-start(bf16[208,1024]{1,0:T(8,128)(2,1)} %slice.13), channel_id=1, source_target_pairs={{0,32},{32,64},{64,96},{96,0},{128,160},{160,192},{192,224},{224,1... | collective-permute-start | bytes 1277960 | tf_op jit(solution)/shard_map/ppermute | solution.py:219
  64.8 4.2 %copy-start.18 = (f32[64,256]{1,0:T(8,128)}, f32[64,256]{1,0:T(8,128)S(1)}, u32[]{:S(2)}) copy-start(f32[64,256]{1,0:T(8,128)S(1)} %convert_reduce_fusion.1) | copy-start | bytes 196612
  69.0 24.1 %copy-start.8 = (bf16[208,1024]{1,0:T(8,128)(2,1)}, bf16[208,1024]{1,0:T(8,128)(2,1)S(1)}, u32[]{:S(2)}) copy-start(bf16[208,1024]{1,0:T(8,128)(2,1)S(1)} %collective-permute-done.6.refs_4_) | copy-start | bytes 1277956
  69.0 24.1 %copy-start.5 = (bf16[256,1024]{1,0:T(8,128)(2,1)}, bf16[256,1024]{1,0:T(8,128)(2,1)S(1)}, u32[]{:S(2)}) copy-start(bf16[256,1024]{1,0:T(8,128)(2,1)S(1)} %collective-permute-done.5.refs_3_) | copy-start | bytes 1572868
  70.0 23.1 %all-to-all-start.2 = ((bf16[32,32,256]{2,1,0:T(8,128)(2,1)}), bf16[32,32,256]{2,1,0:T(8,128)(2,1)}, u32[]{:S(2)}, u32[]{:S(2)}) async-start(bf16[32,32,256]{2,1,0:T(8,128)(2,1)} %bitcast.30), calls=%async_computation.2 | async-start | bytes 1048576 | tf_op jit(solution)/shard_map/all_to_all | solution.py:252
  76.8 8.7 %collective-permute-start.7 = (bf16[464,1024]{1,0:T(8,128)(2,1)S(1)}, bf16[464,1024]{1,0:T(8,128)(2,1)S(1)}, u32[]{:S(2)}, u32[]{:S(2)}) collective-permute-start(bf16[464,1024]{1,0:T(8,128)(2,1)S(1)} %collective-permute-done.2.refs_1_), channel_id=1, source_target_pairs={{0,4},{4,0},{8,12},{12,8},{16,20},{20,16},{24,28},{28,24},{1,5},{5... | collective-permute-start | bytes 2850824 | tf_op jit(solution)/shard_map/ppermute | solution.py:222
  79.0 6.5 %collective-permute-start.8 = (bf16[464,1024]{1,0:T(8,128)(2,1)}, bf16[464,1024]{1,0:T(8,128)(2,1)S(1)}, u32[]{:S(2)}, u32[]{:S(2)}) collective-permute-start(bf16[464,1024]{1,0:T(8,128)(2,1)} %collective-permute-done.3.refs_2_), channel_id=1, source_target_pairs={{0,4},{4,0},{8,12},{12,8},{16,20},{20,16},{24,28},{28,24},{1,5},{5... | collective-permute-start | bytes 2850824 | tf_op jit(solution)/shard_map/ppermute | solution.py:222
  81.1 6.7 %collective-permute-start.9 = (bf16[256,1024]{1,0:T(8,128)(2,1)S(1)}, bf16[256,1024]{1,0:T(8,128)(2,1)}, u32[]{:S(2)}, u32[]{:S(2)}) collective-permute-start(bf16[256,1024]{1,0:T(8,128)(2,1)S(1)} %collective-permute-done.5.refs_3_), channel_id=1, source_target_pairs={{0,4},{4,0},{8,12},{12,8},{16,20},{20,16},{24,28},{28,24},{1,5},{5... | collective-permute-start | bytes 1572872 | tf_op jit(solution)/shard_map/ppermute | solution.py:222
  83.3 3.7 %collective-permute-start.10 = (bf16[208,1024]{1,0:T(8,128)(2,1)S(1)}, bf16[208,1024]{1,0:T(8,128)(2,1)S(1)}, u32[]{:S(2)}, u32[]{:S(2)}) collective-permute-start(bf16[208,1024]{1,0:T(8,128)(2,1)S(1)} %collective-permute-done.6.refs_4_), channel_id=1, source_target_pairs={{0,4},{4,0},{8,12},{12,8},{16,20},{20,16},{24,28},{28,24},{1,5},{5... | collective-permute-start | bytes 1277960 | tf_op jit(solution)/shard_map/ppermute | solution.py:222
  85.5 1.5 copy-start.16
  85.5 1.5 copy-start.17
  100.8 63.1 %copy-start.2 = (bf16[2,232,1024]{2,1,0:T(8,128)(2,1)S(1)}, bf16[2,232,1024]{2,1,0:T(8,128)(2,1)}, u32[]{:S(2)}) copy-start(bf16[2,232,1024]{2,1,0:T(8,128)(2,1)} %copy-done.1) | copy-start | bytes 2850820
  100.8 63.1 %copy-start.4 = (bf16[464,1024]{1,0:T(8,128)(2,1)S(1)}, bf16[464,1024]{1,0:T(8,128)(2,1)}, u32[]{:S(2)}) copy-start(bf16[464,1024]{1,0:T(8,128)(2,1)} %copy-done.3) | copy-start | bytes 2850820
  100.8 63.1 %copy-start.14 = (s32[2]{0:T(128)S(1)}, s32[2]{0:T(128)}, u32[]{:S(2)}) copy-start(s32[2]{0:T(128)} %copy-done.13) | copy-start | bytes 28
  100.8 39.3 %all-to-all-start.3 = ((bf16[4,464,128]{2,1,0:T(8,128)(2,1)}), bf16[4,464,128]{2,1,0:T(8,128)(2,1)}, u32[]{:S(2)}, u32[]{:S(2)}) async-start(bf16[4,464,128]{2,1,0:T(8,128)(2,1)} %shard_map.66), calls=%async_computation.3 | async-start | bytes 950272 | tf_op jit(solution)/shard_map/all_to_all | solution.py:278
  114.6 26.8 %collective-permute-start.1 = (bf16[231,128]{1,0:T(8,128)(2,1)}, bf16[231,128]{1,0:T(8,128)(2,1)}, u32[]{:S(2)}, u32[]{:S(2)}) collective-permute-start(bf16[231,128]{1,0:T(8,128)(2,1)} %dynamic-slice_bitcast_fusion.1), channel_id=1, source_target_pairs={{0,0},{4,4},{40,8},{44,12},{112,16},{116,20},{88,24},{92,28},{32,1... | collective-permute-start | bytes 177416 | tf_op jit(solution)/shard_map/ppermute | solution.py:272
  140.2 23.7 %copy-start.6 = (bf16[256,1024]{1,0:T(8,128)(2,1)S(1)}, bf16[256,1024]{1,0:T(8,128)(2,1)}, u32[]{:S(2)}) copy-start(bf16[256,1024]{1,0:T(8,128)(2,1)} %copy-done.5) | copy-start | bytes 1572868
  140.2 23.8 %copy-start.9 = (bf16[208,1024]{1,0:T(8,128)(2,1)S(1)}, bf16[208,1024]{1,0:T(8,128)(2,1)}, u32[]{:S(2)}) copy-start(bf16[208,1024]{1,0:T(8,128)(2,1)} %copy-done.8) | copy-start | bytes 1277956
  169.2 25.2 %copy-start.19 = (f32[64,256]{1,0:T(8,128)S(1)}, f32[64,256]{1,0:T(8,128)}, u32[]{:S(2)}) copy-start(f32[64,256]{1,0:T(8,128)} %copy-done.18) | copy-start | bytes 196612
  (5 other events, 4.8 us)
